TPU v7x, 256 devices: a whole 4x4x8 slice. The times are simulated.
256 devices in a mesh: fsdp: 32 (over y, x, z_hi), head: 8 (over z_lo, core).
Axes of the slice: x: 4, y: 4, z: 8 (z_hi: 2, z_lo: 4; z = z_hi * 4 + z_lo), core: 2. Of those that a mesh axis runs over, the one named last changes fastest.
Arguments:
- tokens: bfloat16 [16384, 8192], P(('fsdp', 'head')), may hold values from -6 to 6
- w_x: bfloat16 [8192, 8192], P('fsdp', 'head'), may hold values from -0.0625 to 0.0625
- w_b: bfloat16 [8192, 1024], P('fsdp', 'head'), may hold values from -0.0625 to 0.0625
- w_c: bfloat16 [8192, 1024], P('fsdp', 'head'), may hold values from -0.0625 to 0.0625
- w_dt: bfloat16 [8192, 128], P('fsdp', 'head'), may hold values from -0.0625 to 0.0625
- conv_x: float32 [4, 8192], P(None, 'head'), may hold values from -3 to 3
- conv_b: float32 [4, 1024], P(None, 'head'), may hold values from -3 to 3
- conv_c: float32 [4, 1024], P(None, 'head'), may hold values from -3 to 3
- dt_bias: float32 [128], P('head'), may hold values from -3 to 0
- decay_rate: float32 [128], P('head'), may hold values from 0.01 to 0.5
- d_skip: float32 [128], P('head'), may hold values from 0.5 to 1.5
Outputs:
- mixed: bfloat16 [16384, 8192], P(('fsdp', 'head'))
- block_states: float32 [128, 128, 64, 128], P('fsdp', 'head')
All inputs are finite; a program needn't handle non-finite values.
Results may differ from a plain program's by a relative error of at most 0.0065.
Values may be sent and summed in bfloat16 or wider, within the bound.
No kernel may reach another device: no remote copies, remote signals or barrier semaphores. Data moves between devices by JAX's collectives and lax.ppermute only.
A program may use at most 128 MiB of HBM per device.

v0:
```python
import jax
import jax.numpy as jnp
from jax import lax
from jax.sharding import PartitionSpec as P

HEAD_DIM = 64
STATE = 128
SPAN = 128


def causal_conv(values, taps):
    width = taps.shape[0]
    length = values.shape[0]
    padded = jnp.pad(values.astype(jnp.float32), ((width - 1, 0), (0, 0)))
    total = jnp.zeros((length, values.shape[1]), jnp.float32)
    for tap in range(width):
        total = total + taps[tap][None, :] * padded[tap : tap + length]
    return jax.nn.silu(total).astype(jnp.bfloat16)


def mix_sequence(projected, conv_x, conv_b, conv_c, dt_bias, decay_rate, d_skip):
    length = projected.shape[0]
    heads = dt_bias.shape[0]
    x_width = conv_x.shape[1]
    b_width = conv_b.shape[1]
    groups = b_width // STATE
    per_group = heads // groups
    blocks = length // SPAN
    xs = causal_conv(projected[:, :x_width], conv_x)
    bs = causal_conv(projected[:, x_width : x_width + b_width], conv_b)
    cs = causal_conv(projected[:, x_width + b_width : x_width + 2 * b_width], conv_c)
    step = jax.nn.softplus(
        projected[:, x_width + 2 * b_width :].astype(jnp.float32) + dt_bias[None, :]
    )
    step3 = step.reshape(blocks, SPAN, heads)
    cum = jnp.cumsum(-decay_rate[None, None, :] * step3, axis=1)
    x_blocks = xs.reshape(blocks, SPAN, heads, HEAD_DIM)
    b_blocks = bs.reshape(blocks, SPAN, groups, STATE)
    c_blocks = cs.reshape(blocks, SPAN, groups, STATE)
    scores = jnp.einsum("cqgn,ckgn->cgqk", c_blocks, b_blocks, preferred_element_type=jnp.float32)
    scores = jnp.repeat(scores, per_group, axis=1)
    cum_t = jnp.transpose(cum, (0, 2, 1))
    diff = cum_t[:, :, :, None] - cum_t[:, :, None, :]
    lower = jnp.tril(jnp.ones((SPAN, SPAN), dtype=bool))[None, None]
    decay = jnp.where(lower, jnp.exp(jnp.where(lower, diff, 0.0)), 0.0)
    step_t = jnp.transpose(step3, (0, 2, 1))[:, :, None, :]
    weights = (scores * decay * step_t).astype(jnp.bfloat16)
    output = jnp.einsum("chqk,ckhp->cqhp", weights, x_blocks, preferred_element_type=jnp.float32)
    output = output + d_skip[None, None, :, None] * x_blocks.astype(jnp.float32)
    mixed = output.reshape(length, heads * HEAD_DIM).astype(jnp.bfloat16)
    tail = jnp.exp(cum[:, -1:, :] - cum)
    carried = (x_blocks.astype(jnp.float32) * (step3 * tail)[..., None]).astype(jnp.bfloat16)
    b_heads = jnp.repeat(b_blocks, per_group, axis=2)
    states = jnp.einsum("cqhp,cqhn->chpn", carried, b_heads, preferred_element_type=jnp.float32)
    return (mixed, states)


def per_device(tokens, w_x, w_b, w_c, w_dt, conv_x, conv_b, conv_c, dt_bias, decay_rate, d_skip):
    panel = jnp.concatenate([w_x, w_b, w_c, w_dt], axis=1)
    gathered = lax.all_gather(tokens, "head", axis=0, tiled=True)
    projected = jnp.dot(
        gathered,
        lax.all_gather(panel, "fsdp", axis=0, tiled=True),
        preferred_element_type=jnp.float32,
    )
    projected = projected.astype(jnp.bfloat16)
    local_mixed, states = mix_sequence(
        projected, conv_x, conv_b, conv_c, dt_bias, decay_rate, d_skip
    )
    mixed = lax.all_to_all(local_mixed, "head", split_axis=0, concat_axis=1, tiled=True)
    return (mixed, states)


def solution(mesh):
    in_specs = (
        P(("fsdp", "head"), None),
        P("fsdp", "head"),
        P("fsdp", "head"),
        P("fsdp", "head"),
        P("fsdp", "head"),
        P(None, "head"),
        P(None, "head"),
        P(None, "head"),
        P("head"),
        P("head"),
        P("head"),
    )
    out_specs = (P(("fsdp", "head"), None), P("fsdp", "head", None, None))
    return jax.shard_map(
        per_device, mesh=mesh, in_specs=in_specs, out_specs=out_specs, check_vma=False
    )
```

profile of v0, /device:TPU:1, one launch (start us, length us, event | category | flops | bytes accessed | tf_op | source)
XLA Modules:
  0.0 495.5 jit_solution(12741843958430300359)
XLA Ops:
  7.2 0.0 copy-start.7
  7.2 0.0 copy-start.4
  7.2 0.0 copy-start.5
  7.2 0.0 copy-start.3
  7.2 0.0 all-gather.5.cloned.1.call-start
  7.3 0.7 all-gather.5.cloned.1.call-update
  7.9 0.0 all-gather.3.cloned.1.call-start
  8.0 0.8 copy.34
  8.8 2.0 pad_maximum_fusion
  10.8 0.0 all-gather.3.cloned.1.call-update
  10.9 0.0 copy-done.7
  10.9 0.0 copy-done.4
  10.9 0.0 copy-done.5
  11.0 0.0 copy-done.3
  11.0 94.3 %all-gather.5.cloned.1.call-done = bf16[512,8192]{1,0:T(8,128)(2,1)} async-done(((bf16[64,8192]{1,0:T(8,128)(2,1)}), bf16[512,8192]{1,0:T(8,128)(2,1)}) %all-gather.5.cloned.1.call-update) | async-done | bytes 8388624 | tf_op jit(solution)/shard_map/all_gather | solution.py:60
  105.3 319.7 %all-gather.3.cloned.1.call-done = bf16[8192,1296]{1,0:T(8,128)(2,1)} async-done(((bf16[256,1296]{1,0:T(8,128)(2,1)}), bf16[8192,1296]{1,0:T(8,128)(2,1)}) %all-gather.3.cloned.1.call-update) | async-done | bytes 21233680 | tf_op jit(solution)/shard_map/all_gather | solution.py:63
  425.0 18.2 %fusion = bf16[512,1296]{0,1:T(8,128)(2,1)S(1)} fusion(bf16[8192,1296]{1,0:T(8,128)(2,1)} %all-gather.3.cloned.1.call-done, bf16[512,8192]{1,0:T(8,128)(2,1)} %all-gather.5.cloned.1.call-done), kind=kOutput, calls=%fused_computation.5 | convolution fusion | flops 10872299520 | bytes 30949376 | tf_op jit(solution)/shard_map/dot_general | solution.py:61
  443.2 0.0 copy-start.2
  443.2 0.1 slice_convert_fusion.1
  443.3 0.3 slice_convert_fusion
  443.6 0.7 multiply_convert_fusion.5
  444.2 0.0 copy-done.2
  444.3 0.1 copy.49
  444.4 0.1 copy.48
  444.5 0.0 copy-start.6
  444.6 2.6 multiply_convert_fusion.2
  447.1 0.0 copy-start.8
  447.1 0.3 reshape.58
  447.4 0.0 copy-done.6
  447.4 0.8 compare_select_fusion
  448.3 0.1 copy.37
  448.4 0.0 copy-start
  448.4 0.3 reduce_window_sum.11
  448.7 0.1 copy.38
  448.8 0.2 fusion.37
  449.0 0.1 copy-done
  449.1 0.0 copy-done.8
  449.1 3.1 fusion.3
  452.2 2.6 copy.43
  454.8 2.3 convert_element_type.61
  457.1 0.0 copy-start.1
  457.1 4.7 all-to-all-start
  461.8 0.0 copy-done.1
  461.9 0.1 copy.46
  462.0 2.0 fusion.17
  464.0 23.6 %all-to-all-done = bf16[8,64,1024]{2,1,0:T(8,128)(2,1)S(1)} async-done(((bf16[8,64,1024]{2,1,0:T(8,128)(2,1)}), bf16[8,64,1024]{2,1,0:T(8,128)(2,1)S(1)}, u32[]{:S(2)}, u32[]{:S(2)}) %all-to-all-start) | async-done | bytes 1048608 | tf_op jit(solution)/shard_map/all_to_all | solution.py:70
  487.6 1.1 copy.50
  (10 shorter events, 0.1 us)
Async XLA Ops:
  7.2 3.7 copy-start.7
  7.2 3.7 copy-start.4
  7.2 3.8 copy-start.5
  7.2 3.8 copy-start.3
  7.2 98.1 %all-gather.5.cloned.1.call-start = ((), (), s32[]{:S(2)}) async-start(), calls=%async_computation.2 | async-start | bytes 9437184 | tf_op jit(solution)/shard_map/all_gather | solution.py:60
  7.9 417.1 %all-gather.3.cloned.1.call-start = ((), (), s32[]{:S(2)}) async-start(), calls=%async_computation.1 | async-start | bytes 23789568 | tf_op jit(solution)/shard_map/all_gather | solution.py:63
  443.2 1.1 copy-start.2
  444.5 2.9 copy-start.6
  447.1 2.0 copy-start.8
  448.4 0.7 copy-start
  457.1 4.7 copy-start.1
  457.1 30.4 %all-to-all-start = ((bf16[8,64,1024]{2,1,0:T(8,128)(2,1)}), bf16[8,64,1024]{2,1,0:T(8,128)(2,1)S(1)}, u32[]{:S(2)}, u32[]{:S(2)}) async-start(bf16[8,64,1024]{2,1,0:T(8,128)(2,1)} %convert_element_type.61), calls=%async_computation | async-start | bytes 2097152 | tf_op jit(solution)/shard_map/all_to_all | solution.py:70
Sparse Core Ops, SparseCore 0:
  9.8 95.4 all-gather.4
  109.3 315.6 all-gather.2
where the time goes:
time: 496 us; the launch traced here: 495 us
  waiting for transfers between devices  438 us (88%)
  matrix products  23.5 us (5%)
  between operations  14.3 us (3%)
  local copies, waits for them, and re-layouts  7.85 us (2%)
  other arithmetic  6.74 us (1%)
    all_gather x1, waiting for transfers between devices, per_device(): lax.all_gather(panel, 'fsdp', axis=0, tiled=True)  320 us
    all_gather x1, waiting for transfers between devices, per_device(): gathered = lax.all_gather(tokens, 'head', axis=0, tiled=True)  94.3 us
    all_to_all x1, waiting for transfers between devices, per_device(): lax.all_to_all(local_mixed, 'head', split_axis=0, concat_axis=1, tiled=True)  23.6 us
    dot_general x1, matrix products, per_device(): jnp.dot(gathered, lax.all_gather(panel, 'fsdp', axis=0, tiled=True), pref...  18.2 us
  transfers between devices with their start and end apart: 3, of which 3 were waited for; matrix products, arithmetic and copies ran while one was open for 1% of the time, Pallas kernels for 0%

commit v1 on v0

v1 whole, which is shorter than its diff:
```python
import functools

import jax
import jax.numpy as jnp
from jax import lax
from jax.experimental import pallas as pl
from jax.experimental.pallas import tpu as pltpu
from jax.sharding import Mesh, PartitionSpec as P

AXES = ("y", "x", "zh", "zl", "c")


def shifted(value, rows):
    at = lax.broadcasted_iota(jnp.int32, value.shape, 0)
    return jnp.where(at >= rows, pltpu.roll(value, rows, 0), 0.0)


def scan_block(current, before, refs, core, same, other, states):
    taps, bias, rate, skip = refs
    width = taps.shape[1]
    ext = jnp.concatenate([before[:, :width], current[:, :width]], axis=0)
    total = taps[0:1, :] * ext[13:141]
    for k in (1, 2, 3):
        total = total + taps[k : k + 1, :] * ext[13 + k : 141 + k]
    values = (total / (1.0 + jnp.exp(-total))).astype(jnp.bfloat16)
    xs, bs, cs = values[:, :1024], values[:, 1024:1152], values[:, 1152:1280]

    raw = current[:, width:] + bias[...]
    step = jnp.maximum(raw, 0.0) + jnp.log1p(jnp.exp(-jnp.abs(raw)))
    cum = -rate[...] * step
    for rows in (1, 2, 4, 8, 16, 32, 64):
        cum = cum + shifted(cum, rows)
    cum_t, step_t = cum.T, step.T
    factor = step * jnp.exp(cum[127:128, :] - cum)
    scores = lax.dot_general(cs, bs, (((1,), (1,)), ((), ())), preferred_element_type=jnp.float32)
    lower = lax.broadcasted_iota(jnp.int32, (128, 128), 0) >= lax.broadcasted_iota(
        jnp.int32, (128, 128), 1
    )
    left = lax.broadcasted_iota(jnp.int32, (128, 128), 1) < 64
    for pair in range(8):
        lanes = slice(128 * pair, 128 * pair + 128)
        x_pair = xs[:, lanes]
        wide = x_pair.astype(jnp.float32)
        outs = []
        for h in (2 * pair, 2 * pair + 1):
            diff = cum[:, h : h + 1] - cum_t[h : h + 1, :]
            decay = jnp.exp(jnp.where(lower, diff, -1e30))
            weights = (scores * decay * step_t[h : h + 1, :]).astype(jnp.bfloat16)
            outs.append(jnp.dot(weights, x_pair, preferred_element_type=jnp.float32))
        out = jnp.where(left, outs[0], outs[1]) + skip[:, lanes] * wide
        out = out.astype(jnp.bfloat16)
        top, bottom = out[:64], out[64:]
        same[:, lanes] = jnp.where(core == 0, top, bottom)
        other[:, lanes] = jnp.where(core == 0, bottom, top)
        column = jnp.where(
            left, factor[:, 2 * pair : 2 * pair + 1], factor[:, 2 * pair + 1 : 2 * pair + 2]
        )
        carried = (wide * column).astype(jnp.bfloat16)
        state = lax.dot_general(
            carried, bs, (((0,), (0,)), ((), ())), preferred_element_type=jnp.float32
        )
        states[2 * pair] = state[:64]
        states[2 * pair + 1] = state[64:]


def scan_kernel(late, place, *refs):
    core, zl = place[0], place[1]
    if late:
        near, edge, swapped, came, *refs = refs
        refs = refs[:4] + refs[5:]
    else:
        own, near, edge, swapped, *refs = refs
    params, outs = refs[:4], refs[4:]
    pieces, states, scratch, sems = outs[:4], outs[4], outs[5], outs[6]

    def whole(ref):
        return ref[...].astype(jnp.float32)

    def tail(value):
        return value[112:128]

    ahead = jnp.where(zl == 3, whole(swapped), whole(near))
    behind = jnp.where(zl == 0, whole(swapped), whole(edge))
    if late:
        beyond = jnp.sum(came[...].astype(jnp.float32), axis=0)
        beyond = beyond.astype(jnp.bfloat16).astype(jnp.float32)
        work = [
            (behind, jnp.where(zl == 1, 0.0, tail(beyond)), lax.rem(zl + 3, 4)),
            (beyond, jnp.where(zl == 2, 0.0, tail(ahead)), lax.rem(zl + 2, 4)),
        ]
    else:
        mine = whole(own)
        work = [
            (mine, jnp.where(zl == 0, 0.0, tail(behind)), zl),
            (ahead, jnp.where(zl == 3, 0.0, tail(mine)), lax.rem(zl + 1, 4)),
        ]
    copies = []
    for k, (current, before, block) in enumerate(work):
        scan_block(current, before, params, core, pieces[2 * k], pieces[2 * k + 1], scratch.at[k])
        copies.append(pltpu.make_async_copy(scratch.at[k], states.at[block], sems.at[k]))
        copies[-1].start()
    for copy in copies:
        copy.wait()


def scan(place, sums, params, states=None):
    whole = pl.BlockSpec(memory_space=pltpu.VMEM)
    late = states is not None
    operands = [place, *sums, *params] + ([states] if late else [])
    in_specs = [pl.BlockSpec(memory_space=pltpu.SMEM)] + [whole] * (len(sums) + len(params))
    in_specs += [pl.BlockSpec(memory_space=pl.ANY)] if late else []
    return pl.pallas_call(
        functools.partial(scan_kernel, late),
        out_shape=[jax.ShapeDtypeStruct((64, 1024), jnp.bfloat16)] * 4
        + [jax.ShapeDtypeStruct((4, 16, 64, 128), jnp.float32)],
        in_specs=in_specs,
        out_specs=[whole] * 4 + [pl.BlockSpec(memory_space=pl.ANY)],
        scratch_shapes=[
            pltpu.VMEM((2, 16, 64, 128), jnp.float32),
            pltpu.SemaphoreType.DMA((2,)),
        ],
        input_output_aliases={len(operands) - 1: 4} if late else {},
        compiler_params=pltpu.CompilerParams(vmem_limit_bytes=48 << 20),
        cost_estimate=pl.CostEstimate(flops=1 << 20, bytes_accessed=1 << 16, transcendentals=0),
    )(*operands)


def assemble_kernel(place, *refs):
    pieces, out = refs[:-1], refs[-1]
    for k, piece in enumerate(pieces):
        out[:, pl.ds(pl.multiple_of(place[k] * 1024, 1024), 1024)] = piece[...]


def assemble(place, pieces):
    whole = pl.BlockSpec(memory_space=pltpu.VMEM)
    return pl.pallas_call(
        assemble_kernel,
        out_shape=jax.ShapeDtypeStruct((64, 8192), jnp.bfloat16),
        in_specs=[pl.BlockSpec(memory_space=pltpu.SMEM)] + [whole] * 8,
        out_specs=whole,
        compiler_params=pltpu.CompilerParams(vmem_limit_bytes=16 << 20),
    )(place, *pieces)


def reorder_kernel(place, tokens, out):
    width = 256
    for part in range(4):
        for piece in range(8):
            start = pl.multiple_of(place[part * 8 + piece] * width, width)
            out[part, :, piece * width : (piece + 1) * width] = tokens[:, pl.ds(start, width)]


def reorder_tokens(tokens, place):
    rows = tokens.shape[0]
    whole = pl.BlockSpec(memory_space=pltpu.VMEM)
    return pl.pallas_call(
        reorder_kernel,
        out_shape=jax.ShapeDtypeStruct((4, rows, 2048), tokens.dtype),
        in_specs=[pl.BlockSpec(memory_space=pltpu.SMEM), whole],
        out_specs=whole,
        compiler_params=pltpu.CompilerParams(vmem_limit_bytes=16 << 20),
    )(place, tokens)


TILE = 256


def project_kernel(pairs, start, place, *refs):
    chunks, refs = refs[: 2 * pairs], refs[2 * pairs :]
    panels, out = refs[:-1], refs[-1]
    tile = pl.program_id(0)
    core, zh = place[0], place[2]

    def work(group, paired):
        values = [ref[...] for ref in group]
        ordered = [jnp.where(zh == 0, a, b) for a, b in zip(values[:2], values[2:])]
        ordered += [jnp.where(zh == 0, b, a) for a, b in zip(values[:2], values[2:])]
        values = ordered
        if not paired:
            values = [v[h : h + 256] for f in (0, 2) for h in (0, 256) for v in values[f : f + 2]]
        rhs = jnp.concatenate(values, axis=0)
        for p in range(pairs):
            lhs = jnp.concatenate([chunks[2 * p][...], chunks[2 * p + 1][...]], axis=0)
            partial = jnp.dot(lhs, rhs, preferred_element_type=jnp.float32).astype(out.dtype)
            for half, at in ((0, core), (256, 1 - core)):
                rows = pl.ds(pl.multiple_of(p * 128 + at * 64, 64), 64)
                for d in range(4):
                    low = half + 64 * d
                    out[d, rows, :] = partial[low : low + 64]

    pl.when(tile < start)(lambda: work(panels[:4], True))
    pl.when(tile >= start)(lambda: work(panels[4:], False))


def project(place, chunks, panels):
    pairs = len(chunks) // 2
    widths = [panel.shape[1] for panel in panels[::4]]
    counts = [pl.cdiv(width, TILE) for width in widths]
    whole = pl.BlockSpec((256, 2048), lambda j: (0, 0))
    first = pl.BlockSpec((512, TILE), lambda j: (0, jnp.minimum(j, counts[0] - 1)))
    last = pl.BlockSpec((512, TILE), lambda j: (0, jnp.maximum(j - counts[0], 0)))
    return pl.pallas_call(
        functools.partial(project_kernel, pairs, counts[0]),
        grid=(sum(counts),),
        out_shape=jax.ShapeDtypeStruct((4, 128 * pairs, sum(widths)), jnp.bfloat16),
        in_specs=[pl.BlockSpec(memory_space=pltpu.SMEM)]
        + [whole] * len(chunks) + [first] * 4 + [last] * 4,
        out_specs=pl.BlockSpec((4, 128 * pairs, TILE), lambda j: (0, 0, j)),
        compiler_params=pltpu.CompilerParams(vmem_limit_bytes=60 << 20),
        cost_estimate=pl.CostEstimate(flops=1 << 20, bytes_accessed=1 << 16, transcendentals=0),
    )(place, *chunks, *panels)


def from_ahead(value, axis, distance):
    size = lax.axis_size(axis)
    return lax.ppermute(value, axis, [(i, (i - distance) % size) for i in range(size)])


def after(values, *others):
    flat, tree = jax.tree.flatten(values)
    held = lax.optimization_barrier(tuple(flat) + tuple(jax.tree.leaves(others)))
    return jax.tree.unflatten(tree, held[: len(flat)])


NEXT = [(i, i ^ 1) for i in range(4)]
MIRROR = [(i, 3 - i) for i in range(4)]


def gather_x(panel, pairings):
    both = jnp.concatenate([panel, lax.ppermute(panel, "x", pairings[0])], axis=0)
    return [both, lax.ppermute(both, "x", pairings[1])]


def exchange(partial):
    return lax.all_to_all(partial, "y", split_axis=0, concat_axis=0, tiled=True)


def add_up(came):
    return jnp.sum(came.astype(jnp.float32), axis=0).astype(jnp.bfloat16)


def per_device(tokens, w_x, w_b, w_c, w_dt, conv_x, conv_b, conv_c, dt_bias, decay_rate, d_skip):
    y, x, zh, zl, core = (lax.axis_index(a) for a in AXES)
    split = 768
    panel = jnp.concatenate([w_x, w_b, w_c, jnp.pad(w_dt, ((0, 0), (0, 112)))], axis=1)
    twin = from_ahead(panel, "zh", 1)
    near_a = gather_x(panel[:, :split], (NEXT, MIRROR))
    near_b = gather_x(panel[:, split:], (MIRROR, NEXT))

    sources = jnp.stack([x, x ^ 1, 3 - x, 3 - (x ^ 1)])
    order = (
        jnp.arange(4)[:, None, None] * 8
        + jnp.arange(2)[None, :, None]
        + sources[None, None, :] * 2
    ).astype(jnp.int32).reshape(32)
    parts = reorder_tokens(after(tokens, panel), order)
    own = lax.all_to_all(parts, "y", split_axis=0, concat_axis=0, tiled=True).reshape(256, 2048)
    own_other = from_ahead(own, "c", 1)

    line = ("zh", "zl")
    own_sent, twin = after((own, twin), near_a, near_b)
    right1 = lax.ppermute(own_sent, line, [(i, (i + 1) % 8) for i in range(8)])
    left1 = lax.ppermute(own_sent, line, [(i, (i - 1) % 8) for i in range(8)])
    panels = near_a + gather_x(twin[:, :split], (NEXT, MIRROR))
    panels += near_b + gather_x(twin[:, split:], (MIRROR, NEXT))

    place = jnp.stack([core, zl, zh]).astype(jnp.int32)
    partial = project(place, [own, own_other], panels)
    came_own = exchange(partial)

    right2 = lax.ppermute(right1, line, [(1, 2), (2, 3), (5, 6), (6, 7)])
    left2 = lax.ppermute(left1, line, [(1, 0), (2, 1), (5, 4), (6, 5)])
    sides = [left1, from_ahead(left1, "c", 1), right1, from_ahead(right1, "c", 1)]
    partial = project(place, after(sides, partial), panels)
    came_sides = exchange(partial)

    second = jnp.where(zl < 2, left2, right2)
    pair = after([second, from_ahead(second, "c", 1)], partial)
    partial = project(place, pair, panels)
    came_own, came_sides = after((came_own, came_sides), partial)
    came_second = exchange(partial)

    params = [
        jnp.concatenate([conv_x, conv_b, conv_c], axis=1),
        jnp.pad(dt_bias, (0, 112))[None],
        jnp.pad(decay_rate, (0, 112))[None],
        jnp.repeat(d_skip, 64)[None],
    ]
    own_sum, both = add_up(came_own), add_up(came_sides)
    left, right = both[:128], both[128:]
    swapped = lax.ppermute(
        jnp.where(zl == 3, left, right), line, [(i, (i + 4) % 8) for i in (0, 3, 4, 7)]
    )
    *early, states = scan(place, [own_sum, left, right, swapped], params)
    *last, states = scan(place, [left, right, swapped, came_second], params, states)
    heads = ("zl", "c")

    def to(piece, distance, flip):
        pairs = [
            (2 * z + c, 2 * ((z + distance) % 4) + (c ^ flip)) for z in range(4) for c in range(2)
        ]
        return lax.ppermute(piece, heads, pairs)

    pieces = [
        early[0], to(early[1], 0, 1), to(early[2], 1, 0), to(early[3], 1, 1),
        to(last[0], 3, 0), to(last[1], 3, 1), to(last[2], 2, 0), to(last[3], 2, 1),
    ]
    origin = zl + jnp.asarray([0, 0, 3, 3, 1, 1, 2, 2])
    columns = (origin % 4) * 2 + (core + jnp.asarray([0, 1] * 4)) % 2
    return (assemble(columns.astype(jnp.int32), pieces), states)


def solution(mesh):
    fine = Mesh(mesh.devices.reshape(4, 4, 2, 4, 2), AXES)
    fsdp, head = ("y", "x", "zh"), ("zl", "c")
    in_specs = (
        P(AXES, None),
        P(fsdp, head),
        P(fsdp, head),
        P(fsdp, head),
        P(fsdp, head),
        P(None, head),
        P(None, head),
        P(None, head),
        P(head),
        P(head),
        P(head),
    )
    out_specs = (P(AXES, None), P(fsdp, head, None, None))
    return jax.shard_map(
        per_device, mesh=fine, in_specs=in_specs, out_specs=out_specs, check_vma=False
    )
```

time: 496 us -> 218 us (0.44)
  waiting for transfers between devices: 438 us -> 84.6 us
  starting transfers between devices: 4.77 us -> 71.6 us
  Pallas kernels: 0 us -> 41 us
  matrix products: 23.5 us -> 0 us
  between operations: 14.3 us -> 1.07 us
    all_gather x2 -> x0, waiting for transfers between devices: 414 us -> none  [the longest x1 320 us: per_device(): lax.all_gather(panel, 'fsdp', axis=0, tiled=True)]
    ppermute x0 -> x25, waiting for transfers between devices: none -> 69.5 us  [the longest x5 20.3 us: from_ahead(): lax.ppermute(value, axis, [(i, (i - distance) % size) for i in range(size)])]
    ppermute x0 -> x25, starting transfers between devices: none -> 55.1 us  [the longest x5 23.8 us: from_ahead(): lax.ppermute(value, axis, [(i, (i - distance) % size) for i in range(size)])]
    pallas_call x0 -> x7, Pallas kernels: none -> 41 us  [the longest x3 29.1 us: project(): pl.pallas_call(functools.partial(project_kernel, pairs, counts[0]), grid=...]
    dot_general x4 -> x0, matrix products: 23.5 us -> none  [the longest x1 18.2 us: per_device(): jnp.dot(gathered, lax.all_gather(panel, 'fsdp', axis=0, tiled=True), pref...]
    all_to_all x1 -> x4, starting transfers between devices: 4.7 us -> 16.5 us  [the longest x3 12.2 us: exchange(): return lax.all_to_all(partial, 'y', split_axis=0, concat_axis=0, tiled=True)]
    all_to_all x1 -> x4, waiting for transfers between devices: 23.6 us -> 15.2 us  [the longest x3 15.2 us: exchange(): return lax.all_to_all(partial, 'y', split_axis=0, concat_axis=0, tiled=True)]
  transfers between devices with their start and end apart: 3 -> 29, of which waited for: 3 -> 11; matrix products, arithmetic and copies ran while one was open for 1% -> 4% of each run, Pallas kernels for 0% -> 16%
where the time goes in v1:
time: 218 us; the launch traced here: 217 us
  waiting for transfers between devices  84.6 us (39%)
  starting transfers between devices  71.6 us (33%)
  Pallas kernels  41 us (19%)
  other arithmetic  9.82 us (5%)
  local copies, waits for them, and re-layouts  9.28 us (4%)
    pallas_call x3, Pallas kernels, project(): pl.pallas_call(functools.partial(project_kernel, pairs, counts[0]), grid=...  29.1 us
    ppermute x5, starting transfers between devices, from_ahead(): lax.ppermute(value, axis, [(i, (i - distance) % size) for i in range(size)])  23.8 us
    ppermute x5, waiting for transfers between devices, from_ahead(): lax.ppermute(value, axis, [(i, (i - distance) % size) for i in range(size)])  20.3 us
    ppermute x4, waiting for transfers between devices, gather_x(): return [both, lax.ppermute(both, 'x', pairings[1])]  18.2 us
    ppermute x7, waiting for transfers between devices, to(): return lax.ppermute(piece, heads, pairs)  17.1 us
    all_to_all x3, waiting for transfers between devices, exchange(): return lax.all_to_all(partial, 'y', split_axis=0, concat_axis=0, tiled=True)  15.2 us
    all_to_all x3, starting transfers between devices, exchange(): return lax.all_to_all(partial, 'y', split_axis=0, concat_axis=0, tiled=True)  12.2 us
    ppermute x7, starting transfers between devices, to(): return lax.ppermute(piece, heads, pairs)  11 us
  transfers between devices with their start and end apart: 29, of which 11 were waited for; matrix products, arithmetic and copies ran while one was open for 4% of the time, Pallas kernels for 16%

profile of v1, /device:TPU:1, one launch (start us, length us, event | category | flops | bytes accessed | tf_op | source)
XLA Modules:
  0.0 217.4 jit_solution(4269555391759552841)
XLA Ops:
  0.6 0.9 copy.16
  1.5 2.1 fusion.1
  3.6 1.0 slice.24
  4.6 3.4 %collective-permute-start.4 = (bf16[256,640]{1,0:T(8,128)(2,1)S(1)}, bf16[256,640]{1,0:T(8,128)(2,1)}, u32[]{:S(2)}, u32[]{:S(2)}) collective-permute-start(bf16[256,640]{1,0:T(8,128)(2,1)S(1)} %slice.24), channel_id=1, source_target_pairs={{0,48},{16,32},{32,16},{48,0},{1,49},{17,33},{33,17},{49,1},{2,50}... | collective-permute-start | bytes 983048 | tf_op jit(solution)/shard_map/ppermute | solution.py:230
  8.1 0.1 collective-permute-start.1
  8.2 0.1 add_multiply_fusion
  8.4 0.1 add.79.place
  8.5 1.7 shard_map.140
  10.2 4.2 %all-to-all-start = ((bf16[4,64,2048]{2,1,0:T(8,128)(2,1)}), bf16[4,64,2048]{2,1,0:T(8,128)(2,1)}, u32[]{:S(2)}, u32[]{:S(2)}) async-start(bf16[4,64,2048]{2,1,0:T(8,128)(2,1)} %shard_map.140), calls=%async_computation | async-start | bytes 2097152 | tf_op jit(solution)/shard_map/all_to_all | solution.py:257
  14.4 3.4 %collective-permute-done.1 = bf16[256,768]{1,0:T(8,128)(2,1)S(1)} collective-permute-done((bf16[256,768]{1,0:T(8,128)(2,1)S(1)}, bf16[256,768]{1,0:T(8,128)(2,1)S(1)}, u32[]{:S(2)}, u32[]{:S(2)}) %collective-permute-start.1) | collective-permute-done | bytes 393248 | tf_op jit(solution)/shard_map/ppermute | solution.py:230
  17.9 0.1 collective-permute-start.2
  18.0 7.2 %collective-permute-start.3 = (bf16[256,1408]{1,0:T(8,128)(2,1)}, bf16[256,1408]{1,0:T(8,128)(2,1)}, u32[]{:S(2)}, u32[]{:S(2)}) collective-permute-start(bf16[256,1408]{1,0:T(8,128)(2,1)} %fusion.1), channel_id=1, source_target_pairs={{0,8},{8,0},{1,9},{9,1},{2,10},{10,2},{3,11},{11,3},{4,12},{12,4},... | collective-permute-start | bytes 2162696 | tf_op jit(solution)/shard_map/ppermute | solution.py:216
  25.2 1.0 pad_maximum_fusion.2.refs_6_.refs_8_
  26.2 0.1 collective-permute-start.5
  26.3 16.9 %collective-permute-done.3 = bf16[256,1408]{1,0:T(8,128)(2,1)} collective-permute-done((bf16[256,1408]{1,0:T(8,128)(2,1)}, bf16[256,1408]{1,0:T(8,128)(2,1)}, u32[]{:S(2)}, u32[]{:S(2)}) %collective-permute-start.3) | collective-permute-done | bytes 720928 | tf_op jit(solution)/shard_map/ppermute | solution.py:216
  43.3 1.3 slice.20
  44.6 0.1 collective-permute-start.6
  44.7 1.0 slice.21
  45.7 2.4 %collective-permute-start.8 = (bf16[256,640]{1,0:T(8,128)(2,1)S(1)}, bf16[256,640]{1,0:T(8,128)(2,1)S(1)}, u32[]{:S(2)}, u32[]{:S(2)}) collective-permute-start(bf16[256,640]{1,0:T(8,128)(2,1)S(1)} %slice.21), channel_id=1, source_target_pairs={{0,48},{16,32},{32,16},{48,0},{1,49},{17,33},{33,17},{49,1},{2,50}... | collective-permute-start | bytes 983048 | tf_op jit(solution)/shard_map/ppermute | solution.py:230
  48.1 13.9 %collective-permute-start = (bf16[256,2048]{1,0:T(8,128)(2,1)}, bf16[256,2048]{1,0:T(8,128)(2,1)}, u32[]{:S(2)}, u32[]{:S(2)}) collective-permute-start(bf16[256,2048]{1,0:T(8,128)(2,1)} %bitcast.7.refs_0_), channel_id=1, source_target_pairs={{0,1},{1,0},{2,3},{3,2},{4,5},{5,4},{6,7},{7,6},{8,9},{9,8},{10,11... | collective-permute-start | bytes 3145736 | tf_op jit(solution)/shard_map/ppermute | solution.py:216
  61.9 4.4 %collective-permute-start.10 = (bf16[256,2048]{1,0:T(8,128)(2,1)}, bf16[256,2048]{1,0:T(8,128)(2,1)}, u32[]{:S(2)}, u32[]{:S(2)}) collective-permute-start(bf16[256,2048]{1,0:T(8,128)(2,1)} %bitcast.7.refs_0_), channel_id=1, source_target_pairs={{0,14},{2,0},{4,2},{6,4},{8,6},{10,8},{12,10},{14,12},{1,15},{3,1}... | collective-permute-start | bytes 3145736 | tf_op jit(solution)/shard_map/ppermute | solution.py:263
  66.5 0.6 collective-permute-start.7
  67.1 0.8 collective-permute-start.9
  67.9 0.7 pad_add_fusion.place
  68.6 13.2 %collective-permute-done.9.refs_9_.refs_11_ = bf16[512,640]{1,0:T(8,128)(2,1)S(1)} collective-permute-done((bf16[512,640]{1,0:T(8,128)(2,1)S(1)}, bf16[512,640]{1,0:T(8,128)(2,1)S(1)}, u32[]{:S(2)}, u32[]{:S(2)}) %collective-permute-start.9) | collective-permute-done | bytes 655392 | tf_op jit(solution)/shard_map/ppermute | solution.py:231
  81.8 5.0 %collective-permute-done.7.refs_5_.refs_7_ = bf16[512,768]{1,0:T(8,128)(2,1)} collective-permute-done((bf16[512,768]{1,0:T(8,128)(2,1)S(1)}, bf16[512,768]{1,0:T(8,128)(2,1)}, u32[]{:S(2)}, u32[]{:S(2)}) %collective-permute-start.7) | collective-permute-done | bytes 786464 | tf_op jit(solution)/shard_map/ppermute | solution.py:231
  86.8 8.6 %shard_map.141 = bf16[4,128,1408]{2,1,0:T(8,128)(2,1)} custom-call(s32[3]{0:T(128)} %pad_add_fusion.place, bf16[256,2048]{1,0:T(8,128)(2,1)} %bitcast.7.refs_0_, bf16[256,2048]{1,0:T(8,128)(2,1)} %collective-permute-done.refs_1_, bf16[512,768]{1,0:T(8,128)(2,1)} %copy-done.2, bf16[512,768]{1,0:T(8,128)(2,1)} %copy-done.7, bf16[512,768]{1,0:T(8,128)(2,1)} %copy-done.3, ...), custom_call_target="tpu_custom_call" | custom-call | flops 1048576 | bytes 65536 | tf_op jit(solution)/shard_map/pallas_call | solution.py:202
  95.3 4.2 %all-to-all-start.1 = ((bf16[4,128,1408]{2,1,0:T(8,128)(2,1)}), bf16[4,128,1408]{2,1,0:T(8,128)(2,1)S(1)}, u32[]{:S(2)}, u32[]{:S(2)}) async-start(bf16[4,128,1408]{2,1,0:T(8,128)(2,1)} %shard_map.141), calls=%async_computation.1 | async-start | bytes 2883584 | tf_op jit(solution)/shard_map/all_to_all | solution.py:235
  99.5 1.4 collective-permute-start.11
  100.9 0.1 collective-permute-start.13
  101.0 1.3 collective-permute-start.14
  102.3 1.6 collective-permute-start.15
  103.9 1.0 collective-permute-done.13.refs_3_
  104.9 1.1 copy-done.14
  106.0 11.9 %shard_map.142 = bf16[4,256,1408]{2,1,0:T(8,128)(2,1)} custom-call(s32[3]{0:T(128)} %pad_add_fusion.place, bf16[256,2048]{1,0:T(8,128)(2,1)} %collective-permute-done.10.refs_0_, bf16[256,2048]{1,0:T(8,128)(2,1)} %copy-done.13, bf16[256,2048]{1,0:T(8,128)(2,1)} %collective-permute-done.12.refs_2_, bf16[256,2048]{1,0:T(8,128)(2,1)} %copy-done.14, ...), custom_call_target="tpu_custom_call" | custom-call | flops 1048576 | bytes 65536 | tf_op jit(solution)/shard_map/pallas_call | solution.py:202
  117.9 1.1 copy-done.10
  119.0 4.5 %all-to-all-start.2 = ((bf16[4,256,1408]{2,1,0:T(8,128)(2,1)}), bf16[4,256,1408]{2,1,0:T(8,128)(2,1)S(1)}, u32[]{:S(2)}, u32[]{:S(2)}) async-start(bf16[4,256,1408]{2,1,0:T(8,128)(2,1)} %shard_map.142), calls=%async_computation.2 | async-start | bytes 5767168 | tf_op jit(solution)/shard_map/all_to_all | solution.py:235
  123.5 4.0 %collective-permute-done.14 = bf16[256,2048]{1,0:T(8,128)(2,1)} collective-permute-done((bf16[256,2048]{1,0:T(8,128)(2,1)}, bf16[256,2048]{1,0:T(8,128)(2,1)}, u32[]{:S(2)}, u32[]{:S(2)}) %collective-permute-start.14) | collective-permute-done | bytes 1048608 | tf_op jit(solution)/shard_map/ppermute | solution.py:272
  127.5 1.3 broadcast_select_fusion.refs_0_
  128.9 1.0 copy-done.11
  129.9 1.2 collective-permute-start.16
  131.1 2.4 %collective-permute-done.16.refs_1_ = bf16[256,2048]{1,0:T(8,128)(2,1)} collective-permute-done((bf16[256,2048]{1,0:T(8,128)(2,1)S(1)}, bf16[256,2048]{1,0:T(8,128)(2,1)}, u32[]{:S(2)}, u32[]{:S(2)}) %collective-permute-start.16) | collective-permute-done | bytes 1048608 | tf_op jit(solution)/shard_map/ppermute | solution.py:216
  133.5 8.6 %shard_map.143 = bf16[4,128,1408]{2,1,0:T(8,128)(2,1)} custom-call(s32[3]{0:T(128)} %pad_add_fusion.place, bf16[256,2048]{1,0:T(8,128)(2,1)} %copy-done.11, bf16[256,2048]{1,0:T(8,128)(2,1)} %collective-permute-done.16.refs_1_, bf16[512,768]{1,0:T(8,128)(2,1)} %copy-done.2, bf16[512,768]{1,0:T(8,128)(2,1)} %copy-done.7, bf16[512,768]{1,0:T(8,128)(2,1)} %copy-done.3, ...), custom_call_target="tpu_custom_call" | custom-call | flops 1048576 | bytes 65536 | tf_op jit(solution)/shard_map/pallas_call | solution.py:202
  142.1 15.1 %all-to-all-done.2 = bf16[4,256,1408]{2,1,0:T(8,128)(2,1)S(1)} async-done(((bf16[4,256,1408]{2,1,0:T(8,128)(2,1)}), bf16[4,256,1408]{2,1,0:T(8,128)(2,1)S(1)}, u32[]{:S(2)}, u32[]{:S(2)}) %all-to-all-start.2) | async-done | bytes 2883616 | tf_op jit(solution)/shard_map/all_to_all | solution.py:235
  157.2 1.6 copy-done.4
  158.8 3.5 %all-to-all-start.3 = ((bf16[4,128,1408]{2,1,0:T(8,128)(2,1)}), bf16[4,128,1408]{2,1,0:T(8,128)(2,1)S(1)}, u32[]{:S(2)}, u32[]{:S(2)}) async-start(bf16[4,128,1408]{2,1,0:T(8,128)(2,1)} %shard_map.143), calls=%async_computation.3 | async-start | bytes 2883584 | tf_op jit(solution)/shard_map/all_to_all | solution.py:235
  162.4 2.6 %reduce_sum.25 = bf16[256,1408]{1,0:T(8,128)(2,1)S(1)} reduce(bf16[4,256,1408]{2,1,0:T(8,128)(2,1)} %copy-done.4, bf16[]{:T(256)} %constant.57.clone.1), dimensions={0}, to_apply=%region_1.2 | reduce | flops 1081344 | bytes 3604482 | tf_op jit(solution)/shard_map/reduce_sum | solution.py:239
  165.0 0.1 broadcast_select_fusion.1
  165.1 5.4 %collective-permute-start.17 = (bf16[128,1408]{1,0:T(8,128)(2,1)S(1)}, bf16[128,1408]{1,0:T(8,128)(2,1)S(1)}, u32[]{:S(2)}, u32[]{:S(2)}) collective-permute-start(bf16[128,1408]{1,0:T(8,128)(2,1)S(1)} %get-tuple-element.44), channel_id=1, source_target_pairs={{0,8},{6,14},{8,0},{14,6},{1,9},{7,15},{9,1},{15,7},{16,24},{22,30... | collective-permute-start | bytes 1081352 | tf_op jit(solution)/shard_map/ppermute | solution.py:291
  170.7 0.1 broadcast_in_dim_reshape.3.refs_7_
  170.8 1.6 reduce_sum.24.refs_0_
  172.4 6.5 %collective-permute-done.17.refs_3_.refs_2_ = bf16[128,1408]{1,0:T(8,128)(2,1)S(1)} collective-permute-done((bf16[128,1408]{1,0:T(8,128)(2,1)S(1)}, bf16[128,1408]{1,0:T(8,128)(2,1)S(1)}, u32[]{:S(2)}, u32[]{:S(2)}) %collective-permute-start.17) | collective-permute-done | bytes 360480 | tf_op jit(solution)/shard_map/ppermute | solution.py:291
  178.9 4.3 %shard_map.144 = (bf16[64,1024]{1,0:T(8,128)(2,1)S(1)}, bf16[64,1024]{1,0:T(8,128)(2,1)S(1)}, bf16[64,1024]{1,0:T(8,128)(2,1)S(1)}, bf16[64,1024]{1,0:T(8,128)(2,1)S(1)}, f32[4,16,64,128]{3,2,1,0:T(8,128)}) custom-call(s32[3]{0:T(128)S(1)} %copy-done.1, bf16[128,1408]{1,0:T(8,128)(2,1)S(1)} %reduce_sum.24.refs_0_, ...), custom_call_target="tpu_custom_call" | custom-call | flops 1048576 | bytes 65536 | tf_op jit(solution)/shard_map/pallas_call | solution.py:112
  183.2 4.5 %shard_map.145 = (bf16[64,1024]{1,0:T(8,128)(2,1)S(1)}, bf16[64,1024]{1,0:T(8,128)(2,1)S(1)}, bf16[64,1024]{1,0:T(8,128)(2,1)S(1)}, bf16[64,1024]{1,0:T(8,128)(2,1)S(1)}, f32[4,16,64,128]{3,2,1,0:T(8,128)}) custom-call(s32[3]{0:T(128)S(1)} %copy-done.1, bf16[128,1408]{1,0:T(8,128)(2,1)S(1)} %get-tuple-element.46.refs_1_.refs_0_, ...), custom_call_target="tpu_custom_call", output_to_operand_aliasing={{4}: (9, {})} | custom-call | flops 1048576 | bytes 65536 | tf_op jit(solution)/shard_map/pallas_call | solution.py:112
  187.7 2.7 %collective-permute-start.21 = (bf16[64,1024]{1,0:T(8,128)(2,1)S(1)}, bf16[64,1024]{1,0:T(8,128)(2,1)S(1)}, u32[]{:S(2)}, u32[]{:S(2)}) collective-permute-start(bf16[64,1024]{1,0:T(8,128)(2,1)S(1)} %get-tuple-element.39), channel_id=1, source_target_pairs={{0,6},{1,7},{2,0},{3,1},{4,2},{5,3},{6,4},{7,5},{8,14},{9,15},{10,... | collective-permute-start | bytes 393224 | tf_op jit(solution)/shard_map/ppermute | solution.py:302
  190.4 2.8 %collective-permute-start.22 = (bf16[64,1024]{1,0:T(8,128)(2,1)S(1)}, bf16[64,1024]{1,0:T(8,128)(2,1)S(1)}, u32[]{:S(2)}, u32[]{:S(2)}) collective-permute-start(bf16[64,1024]{1,0:T(8,128)(2,1)S(1)} %get-tuple-element.40), channel_id=1, source_target_pairs={{0,7},{1,6},{2,1},{3,0},{4,3},{5,2},{6,5},{7,4},{8,15},{9,14},{10,... | collective-permute-start | bytes 393224 | tf_op jit(solution)/shard_map/ppermute | solution.py:302
  193.2 0.6 collective-permute-start.23
  193.8 2.0 collective-permute-start.24
  195.9 0.2 collective-permute-start.18
  196.0 1.4 collective-permute-start.19
  197.5 1.3 collective-permute-start.20
  198.7 12.6 %collective-permute-done.23.refs_6_ = bf16[64,1024]{1,0:T(8,128)(2,1)S(1)} collective-permute-done((bf16[64,1024]{1,0:T(8,128)(2,1)S(1)}, bf16[64,1024]{1,0:T(8,128)(2,1)S(1)}, u32[]{:S(2)}, u32[]{:S(2)}) %collective-permute-start.23) | collective-permute-done | bytes 131104 | tf_op jit(solution)/shard_map/ppermute | solution.py:302
  211.3 4.5 %collective-permute-done.24.refs_7_ = bf16[64,1024]{1,0:T(8,128)(2,1)S(1)} collective-permute-done((bf16[64,1024]{1,0:T(8,128)(2,1)S(1)}, bf16[64,1024]{1,0:T(8,128)(2,1)S(1)}, u32[]{:S(2)}, u32[]{:S(2)}) %collective-permute-start.24) | collective-permute-done | bytes 131104 | tf_op jit(solution)/shard_map/ppermute | solution.py:302
  215.8 1.6 shard_map.146
  (74 shorter events, 0.6 us)
Async XLA Ops:
  0.6 7.4 %copy-start.12 = (bf16[256,1024]{1,0:T(8,128)(2,1)S(1)}, bf16[256,1024]{1,0:T(8,128)(2,1)}, u32[]{:S(2)}) copy-start(bf16[256,1024]{1,0:T(8,128)(2,1)} %param.14) | copy-start | bytes 1572868
  1.5 7.0 %copy-start = (bf16[64,8192]{1,0:T(8,128)(2,1)S(1)}, bf16[64,8192]{1,0:T(8,128)(2,1)}, u32[]{:S(2)}) copy-start(bf16[64,8192]{1,0:T(8,128)(2,1)} %tokens) | copy-start | bytes 3145732
  4.6 20.6 %collective-permute-start.4 = (bf16[256,640]{1,0:T(8,128)(2,1)S(1)}, bf16[256,640]{1,0:T(8,128)(2,1)}, u32[]{:S(2)}, u32[]{:S(2)}) collective-permute-start(bf16[256,640]{1,0:T(8,128)(2,1)S(1)} %slice.24), channel_id=1, source_target_pairs={{0,48},{16,32},{32,16},{48,0},{1,49},{17,33},{33,17},{49,1},{2,50}... | collective-permute-start | bytes 983048 | tf_op jit(solution)/shard_map/ppermute | solution.py:230
  8.1 9.8 %collective-permute-start.1 = (bf16[256,768]{1,0:T(8,128)(2,1)S(1)}, bf16[256,768]{1,0:T(8,128)(2,1)S(1)}, u32[]{:S(2)}, u32[]{:S(2)}) collective-permute-start(bf16[256,768]{1,0:T(8,128)(2,1)S(1)} %slice.18), channel_id=1, source_target_pairs={{0,16},{16,0},{32,48},{48,32},{1,17},{17,1},{33,49},{49,33},{2,18}... | collective-permute-start | bytes 1179656 | tf_op jit(solution)/shard_map/ppermute | solution.py:230
  10.2 33.1 %all-to-all-start = ((bf16[4,64,2048]{2,1,0:T(8,128)(2,1)}), bf16[4,64,2048]{2,1,0:T(8,128)(2,1)}, u32[]{:S(2)}, u32[]{:S(2)}) async-start(bf16[4,64,2048]{2,1,0:T(8,128)(2,1)} %shard_map.140), calls=%async_computation | async-start | bytes 2097152 | tf_op jit(solution)/shard_map/all_to_all | solution.py:257
  17.9 48.6 %copy-start.2 = (bf16[512,768]{1,0:T(8,128)(2,1)}, bf16[512,768]{1,0:T(8,128)(2,1)S(1)}, u32[]{:S(2)}) copy-start(bf16[512,768]{1,0:T(8,128)(2,1)S(1)} %pad_maximum_fusion.refs_2_.refs_4_) | copy-start | bytes 2359300
  17.9 25.4 %collective-permute-start.2 = (bf16[512,768]{1,0:T(8,128)(2,1)S(1)}, bf16[512,768]{1,0:T(8,128)(2,1)S(1)}, u32[]{:S(2)}, u32[]{:S(2)}) collective-permute-start(bf16[512,768]{1,0:T(8,128)(2,1)S(1)} %pad_maximum_fusion.refs_2_.refs_4_), channel_id=1, source_target_pairs={{0,48},{16,32},{32,16},{48,0},{1,49},{17,33},{33,17},{49,1},{2,50}... | collective-permute-start | bytes 2359304 | tf_op jit(solution)/shard_map/ppermute | solution.py:231
  18.0 25.2 %collective-permute-start.3 = (bf16[256,1408]{1,0:T(8,128)(2,1)}, bf16[256,1408]{1,0:T(8,128)(2,1)}, u32[]{:S(2)}, u32[]{:S(2)}) collective-permute-start(bf16[256,1408]{1,0:T(8,128)(2,1)} %fusion.1), channel_id=1, source_target_pairs={{0,8},{8,0},{1,9},{9,1},{2,10},{10,2},{3,11},{11,3},{4,12},{12,4},... | collective-permute-start | bytes 2162696 | tf_op jit(solution)/shard_map/ppermute | solution.py:216
  26.2 40.2 %copy-start.5 = (bf16[512,640]{1,0:T(8,128)(2,1)}, bf16[512,640]{1,0:T(8,128)(2,1)S(1)}, u32[]{:S(2)}) copy-start(bf16[512,640]{1,0:T(8,128)(2,1)S(1)} %pad_maximum_fusion.2.refs_6_.refs_8_) | copy-start | bytes 1966084
  26.2 17.0 %collective-permute-start.5 = (bf16[512,640]{1,0:T(8,128)(2,1)S(1)}, bf16[512,640]{1,0:T(8,128)(2,1)S(1)}, u32[]{:S(2)}, u32[]{:S(2)}) collective-permute-start(bf16[512,640]{1,0:T(8,128)(2,1)S(1)} %pad_maximum_fusion.2.refs_6_.refs_8_), channel_id=1, source_target_pairs={{0,16},{16,0},{32,48},{48,32},{1,17},{17,1},{33,49},{49,33},{2,18}... | collective-permute-start | bytes 1966088 | tf_op jit(solution)/shard_map/ppermute | solution.py:231
  43.2 23.1 %copy-start.8 = (bf16[512,640]{1,0:T(8,128)(2,1)}, bf16[512,640]{1,0:T(8,128)(2,1)S(1)}, u32[]{:S(2)}) copy-start(bf16[512,640]{1,0:T(8,128)(2,1)S(1)} %collective-permute-done.5.refs_7_.refs_9_) | copy-start | bytes 1966084
  43.3 23.2 %copy-start.7 = (bf16[512,768]{1,0:T(8,128)(2,1)}, bf16[512,768]{1,0:T(8,128)(2,1)S(1)}, u32[]{:S(2)}) copy-start(bf16[512,768]{1,0:T(8,128)(2,1)S(1)} %collective-permute-done.2.refs_3_.refs_5_) | copy-start | bytes 2359300
  44.6 21.8 %collective-permute-start.6 = (bf16[256,768]{1,0:T(8,128)(2,1)S(1)}, bf16[256,768]{1,0:T(8,128)(2,1)S(1)}, u32[]{:S(2)}, u32[]{:S(2)}) collective-permute-start(bf16[256,768]{1,0:T(8,128)(2,1)S(1)} %slice.20), channel_id=1, source_target_pairs={{0,16},{16,0},{32,48},{48,32},{1,17},{17,1},{33,49},{49,33},{2,18}... | collective-permute-start | bytes 1179656 | tf_op jit(solution)/shard_map/ppermute | solution.py:230
  45.7 21.3 %collective-permute-start.8 = (bf16[256,640]{1,0:T(8,128)(2,1)S(1)}, bf16[256,640]{1,0:T(8,128)(2,1)S(1)}, u32[]{:S(2)}, u32[]{:S(2)}) collective-permute-start(bf16[256,640]{1,0:T(8,128)(2,1)S(1)} %slice.21), channel_id=1, source_target_pairs={{0,48},{16,32},{32,16},{48,0},{1,49},{17,33},{33,17},{49,1},{2,50}... | collective-permute-start | bytes 983048 | tf_op jit(solution)/shard_map/ppermute | solution.py:230
  48.1 20.5 %collective-permute-start = (bf16[256,2048]{1,0:T(8,128)(2,1)}, bf16[256,2048]{1,0:T(8,128)(2,1)}, u32[]{:S(2)}, u32[]{:S(2)}) collective-permute-start(bf16[256,2048]{1,0:T(8,128)(2,1)} %bitcast.7.refs_0_), channel_id=1, source_target_pairs={{0,1},{1,0},{2,3},{3,2},{4,5},{5,4},{6,7},{7,6},{8,9},{9,8},{10,11... | collective-permute-start | bytes 3145736 | tf_op jit(solution)/shard_map/ppermute | solution.py:216
  61.9 37.6 %collective-permute-start.10 = (bf16[256,2048]{1,0:T(8,128)(2,1)}, bf16[256,2048]{1,0:T(8,128)(2,1)}, u32[]{:S(2)}, u32[]{:S(2)}) collective-permute-start(bf16[256,2048]{1,0:T(8,128)(2,1)} %bitcast.7.refs_0_), channel_id=1, source_target_pairs={{0,14},{2,0},{4,2},{6,4},{8,6},{10,8},{12,10},{14,12},{1,15},{3,1}... | collective-permute-start | bytes 3145736 | tf_op jit(solution)/shard_map/ppermute | solution.py:263
  66.4 34.5 %collective-permute-start.12 = (bf16[256,2048]{1,0:T(8,128)(2,1)}, bf16[256,2048]{1,0:T(8,128)(2,1)}, u32[]{:S(2)}, u32[]{:S(2)}) collective-permute-start(bf16[256,2048]{1,0:T(8,128)(2,1)} %bitcast.7.refs_0_), channel_id=1, source_target_pairs={{0,2},{2,4},{4,6},{6,8},{8,10},{10,12},{12,14},{14,0},{1,3},{3,5},... | collective-permute-start | bytes 3145736 | tf_op jit(solution)/shard_map/ppermute | solution.py:262
  66.5 20.3 %copy-start.3 = (bf16[512,768]{1,0:T(8,128)(2,1)}, bf16[512,768]{1,0:T(8,128)(2,1)S(1)}, u32[]{:S(2)}) copy-start(bf16[512,768]{1,0:T(8,128)(2,1)S(1)} %pad_maximum_fusion.1.refs_4_.refs_6_) | copy-start | bytes 2359300
  66.5 20.3 %collective-permute-start.7 = (bf16[512,768]{1,0:T(8,128)(2,1)S(1)}, bf16[512,768]{1,0:T(8,128)(2,1)}, u32[]{:S(2)}, u32[]{:S(2)}) collective-permute-start(bf16[512,768]{1,0:T(8,128)(2,1)S(1)} %pad_maximum_fusion.1.refs_4_.refs_6_), channel_id=1, source_target_pairs={{0,48},{16,32},{32,16},{48,0},{1,49},{17,33},{33,17},{49,1},{2,50}... | collective-permute-start | bytes 2359304 | tf_op jit(solution)/shard_map/ppermute | solution.py:231
  67.1 19.6 %copy-start.6 = (bf16[512,640]{1,0:T(8,128)(2,1)}, bf16[512,640]{1,0:T(8,128)(2,1)S(1)}, u32[]{:S(2)}) copy-start(bf16[512,640]{1,0:T(8,128)(2,1)S(1)} %pad_maximum_fusion.3.refs_8_.refs_10_) | copy-start | bytes 1966084
  67.1 14.7 %collective-permute-start.9 = (bf16[512,640]{1,0:T(8,128)(2,1)S(1)}, bf16[512,640]{1,0:T(8,128)(2,1)S(1)}, u32[]{:S(2)}, u32[]{:S(2)}) collective-permute-start(bf16[512,640]{1,0:T(8,128)(2,1)S(1)} %pad_maximum_fusion.3.refs_8_.refs_10_), channel_id=1, source_target_pairs={{0,16},{16,0},{32,48},{48,32},{1,17},{17,1},{33,49},{49,33},{2,18}... | collective-permute-start | bytes 1966088 | tf_op jit(solution)/shard_map/ppermute | solution.py:231
  81.8 5.0 %copy-start.9 = (bf16[512,640]{1,0:T(8,128)(2,1)}, bf16[512,640]{1,0:T(8,128)(2,1)S(1)}, u32[]{:S(2)}) copy-start(bf16[512,640]{1,0:T(8,128)(2,1)S(1)} %collective-permute-done.9.refs_9_.refs_11_) | copy-start | bytes 1966084
  95.3 22.6 %all-to-all-start.1 = ((bf16[4,128,1408]{2,1,0:T(8,128)(2,1)}), bf16[4,128,1408]{2,1,0:T(8,128)(2,1)S(1)}, u32[]{:S(2)}, u32[]{:S(2)}) async-start(bf16[4,128,1408]{2,1,0:T(8,128)(2,1)} %shard_map.141), calls=%async_computation.1 | async-start | bytes 2883584 | tf_op jit(solution)/shard_map/all_to_all | solution.py:235
  99.5 4.4 %collective-permute-start.11 = (bf16[256,2048]{1,0:T(8,128)(2,1)}, bf16[256,2048]{1,0:T(8,128)(2,1)S(1)}, u32[]{:S(2)}, u32[]{:S(2)}) collective-permute-start(bf16[256,2048]{1,0:T(8,128)(2,1)} %collective-permute-done.10.refs_0_), channel_id=1, source_target_pairs={{0,1},{1,0},{2,3},{3,2},{4,5},{5,4},{6,7},{7,6},{8,9},{9,8},{10,11... | collective-permute-start | bytes 3145736 | tf_op jit(solution)/shard_map/ppermute | solution.py:216
  100.9 4.0 %collective-permute-start.13 = (bf16[256,2048]{1,0:T(8,128)(2,1)}, bf16[256,2048]{1,0:T(8,128)(2,1)S(1)}, u32[]{:S(2)}, u32[]{:S(2)}) collective-permute-start(bf16[256,2048]{1,0:T(8,128)(2,1)} %collective-permute-done.12.refs_2_), channel_id=1, source_target_pairs={{0,1},{1,0},{2,3},{3,2},{4,5},{5,4},{6,7},{7,6},{8,9},{9,8},{10,11... | collective-permute-start | bytes 3145736 | tf_op jit(solution)/shard_map/ppermute | solution.py:216
  101.0 26.5 %collective-permute-start.14 = (bf16[256,2048]{1,0:T(8,128)(2,1)}, bf16[256,2048]{1,0:T(8,128)(2,1)}, u32[]{:S(2)}, u32[]{:S(2)}) collective-permute-start(bf16[256,2048]{1,0:T(8,128)(2,1)} %collective-permute-done.10.refs_0_), channel_id=1, source_target_pairs={{2,0},{4,2},{10,8},{12,10},{3,1},{5,3},{11,9},{13,11},{18,16},{20,... | collective-permute-start | bytes 3145736 | tf_op jit(solution)/shard_map/ppermute | solution.py:272
  102.3 25.2 %collective-permute-start.15 = (bf16[256,2048]{1,0:T(8,128)(2,1)}, bf16[256,2048]{1,0:T(8,128)(2,1)}, u32[]{:S(2)}, u32[]{:S(2)}) collective-permute-start(bf16[256,2048]{1,0:T(8,128)(2,1)} %collective-permute-done.12.refs_2_), channel_id=1, source_target_pairs={{2,4},{4,6},{10,12},{12,14},{3,5},{5,7},{11,13},{13,15},{18,20},{2... | collective-permute-start | bytes 3145736 | tf_op jit(solution)/shard_map/ppermute | solution.py:271
  103.9 1.0 copy-start.13
  104.9 1.1 copy-start.14
  117.9 1.1 copy-start.10
  119.0 38.2 %all-to-all-start.2 = ((bf16[4,256,1408]{2,1,0:T(8,128)(2,1)}), bf16[4,256,1408]{2,1,0:T(8,128)(2,1)S(1)}, u32[]{:S(2)}, u32[]{:S(2)}) async-start(bf16[4,256,1408]{2,1,0:T(8,128)(2,1)} %shard_map.142), calls=%async_computation.2 | async-start | bytes 5767168 | tf_op jit(solution)/shard_map/all_to_all | solution.py:235
  128.9 1.0 copy-start.11
  129.9 3.7 %collective-permute-start.16 = (bf16[256,2048]{1,0:T(8,128)(2,1)S(1)}, bf16[256,2048]{1,0:T(8,128)(2,1)}, u32[]{:S(2)}, u32[]{:S(2)}) collective-permute-start(bf16[256,2048]{1,0:T(8,128)(2,1)S(1)} %broadcast_select_fusion.refs_0_), channel_id=1, source_target_pairs={{0,1},{1,0},{2,3},{3,2},{4,5},{5,4},{6,7},{7,6},{8,9},{9,8},{10,11... | collective-permute-start | bytes 3145736 | tf_op jit(solution)/shard_map/ppermute | solution.py:216
  157.2 1.6 copy-start.4
  158.8 24.4 %all-to-all-start.3 = ((bf16[4,128,1408]{2,1,0:T(8,128)(2,1)}), bf16[4,128,1408]{2,1,0:T(8,128)(2,1)S(1)}, u32[]{:S(2)}, u32[]{:S(2)}) async-start(bf16[4,128,1408]{2,1,0:T(8,128)(2,1)} %shard_map.143), calls=%async_computation.3 | async-start | bytes 2883584 | tf_op jit(solution)/shard_map/all_to_all | solution.py:235
  165.0 5.6 %copy-start.21 = (f32[16]{0:T(128)S(1)}, f32[16]{0:T(128)}, u32[]{:S(2)}) copy-start(f32[16]{0:T(128)} %param.22) | copy-start | bytes 196
  165.0 5.6 %copy-start.22 = (f32[16]{0:T(128)S(1)}, f32[16]{0:T(128)}, u32[]{:S(2)}) copy-start(f32[16]{0:T(128)} %param.21) | copy-start | bytes 196
  165.0 5.6 %copy-start.18 = (f32[16]{0:T(128)S(1)}, f32[16]{0:T(128)}, u32[]{:S(2)}) copy-start(f32[16]{0:T(128)} %param.23) | copy-start | bytes 196
  165.0 5.8 %copy-start.15 = (f32[4,1024]{1,0:T(4,128)S(1)}, f32[4,1024]{1,0:T(4,128)}, u32[]{:S(2)}) copy-start(f32[4,1024]{1,0:T(4,128)} %param.18) | copy-start | bytes 49156
  165.0 5.8 %copy-start.16 = (f32[4,128]{1,0:T(4,128)S(1)}, f32[4,128]{1,0:T(4,128)}, u32[]{:S(2)}) copy-start(f32[4,128]{1,0:T(4,128)} %param.19) | copy-start | bytes 6148
  165.0 5.8 %copy-start.17 = (f32[4,128]{1,0:T(4,128)S(1)}, f32[4,128]{1,0:T(4,128)}, u32[]{:S(2)}) copy-start(f32[4,128]{1,0:T(4,128)} %param.20) | copy-start | bytes 6148
  165.0 13.8 %copy-start.1 = (s32[3]{0:T(128)S(1)}, s32[3]{0:T(128)}, u32[]{:S(2)}) copy-start(s32[3]{0:T(128)} %pad_add_fusion.place) | copy-start | bytes 40
  165.1 13.7 %collective-permute-start.17 = (bf16[128,1408]{1,0:T(8,128)(2,1)S(1)}, bf16[128,1408]{1,0:T(8,128)(2,1)S(1)}, u32[]{:S(2)}, u32[]{:S(2)}) collective-permute-start(bf16[128,1408]{1,0:T(8,128)(2,1)S(1)} %get-tuple-element.44), channel_id=1, source_target_pairs={{0,8},{6,14},{8,0},{14,6},{1,9},{7,15},{9,1},{15,7},{16,24},{22,30... | collective-permute-start | bytes 1081352 | tf_op jit(solution)/shard_map/ppermute | solution.py:291
  183.2 15.6 %copy-start.19 = (s32[8]{0:T(128)S(1)}, s32[8]{0:T(128)}, u32[]{:S(2)}) copy-start(s32[8]{0:T(128)} %constant.59.clone) | copy-start | bytes 100
  183.2 15.6 %copy-start.20 = (s32[8]{0:T(128)S(1)}, s32[8]{0:T(128)}, u32[]{:S(2)}) copy-start(s32[8]{0:T(128)} %constant.60.clone) | copy-start | bytes 100
  187.7 8.4 %collective-permute-start.21 = (bf16[64,1024]{1,0:T(8,128)(2,1)S(1)}, bf16[64,1024]{1,0:T(8,128)(2,1)S(1)}, u32[]{:S(2)}, u32[]{:S(2)}) collective-permute-start(bf16[64,1024]{1,0:T(8,128)(2,1)S(1)} %get-tuple-element.39), channel_id=1, source_target_pairs={{0,6},{1,7},{2,0},{3,1},{4,2},{5,3},{6,4},{7,5},{8,14},{9,15},{10,... | collective-permute-start | bytes 393224 | tf_op jit(solution)/shard_map/ppermute | solution.py:302
  190.4 7.1 %collective-permute-start.22 = (bf16[64,1024]{1,0:T(8,128)(2,1)S(1)}, bf16[64,1024]{1,0:T(8,128)(2,1)S(1)}, u32[]{:S(2)}, u32[]{:S(2)}) collective-permute-start(bf16[64,1024]{1,0:T(8,128)(2,1)S(1)} %get-tuple-element.40), channel_id=1, source_target_pairs={{0,7},{1,6},{2,1},{3,0},{4,3},{5,2},{6,5},{7,4},{8,15},{9,14},{10,... | collective-permute-start | bytes 393224 | tf_op jit(solution)/shard_map/ppermute | solution.py:302
  193.2 18.1 %collective-permute-start.23 = (bf16[64,1024]{1,0:T(8,128)(2,1)S(1)}, bf16[64,1024]{1,0:T(8,128)(2,1)S(1)}, u32[]{:S(2)}, u32[]{:S(2)}) collective-permute-start(bf16[64,1024]{1,0:T(8,128)(2,1)S(1)} %get-tuple-element.41), channel_id=1, source_target_pairs={{0,4},{1,5},{2,6},{3,7},{4,0},{5,1},{6,2},{7,3},{8,12},{9,13},{10,... | collective-permute-start | bytes 393224 | tf_op jit(solution)/shard_map/ppermute | solution.py:302
  193.8 22.0 %collective-permute-start.24 = (bf16[64,1024]{1,0:T(8,128)(2,1)S(1)}, bf16[64,1024]{1,0:T(8,128)(2,1)S(1)}, u32[]{:S(2)}, u32[]{:S(2)}) collective-permute-start(bf16[64,1024]{1,0:T(8,128)(2,1)S(1)} %get-tuple-element.42), channel_id=1, source_target_pairs={{0,5},{1,4},{2,7},{3,6},{4,1},{5,0},{6,3},{7,2},{8,13},{9,12},{10,... | collective-permute-start | bytes 393224 | tf_op jit(solution)/shard_map/ppermute | solution.py:302
  195.9 20.0 %collective-permute-start.18 = (bf16[64,1024]{1,0:T(8,128)(2,1)S(1)}, bf16[64,1024]{1,0:T(8,128)(2,1)S(1)}, u32[]{:S(2)}, u32[]{:S(2)}) collective-permute-start(bf16[64,1024]{1,0:T(8,128)(2,1)S(1)} %get-tuple-element.35), channel_id=1, source_target_pairs={{0,1},{1,0},{2,3},{3,2},{4,5},{5,4},{6,7},{7,6},{8,9},{9,8},{10,11... | collective-permute-start | bytes 393224 | tf_op jit(solution)/shard_map/ppermute | solution.py:302
  196.0 19.8 %collective-permute-start.19 = (bf16[64,1024]{1,0:T(8,128)(2,1)S(1)}, bf16[64,1024]{1,0:T(8,128)(2,1)S(1)}, u32[]{:S(2)}, u32[]{:S(2)}) collective-permute-start(bf16[64,1024]{1,0:T(8,128)(2,1)S(1)} %get-tuple-element.36), channel_id=1, source_target_pairs={{0,2},{1,3},{2,4},{3,5},{4,6},{5,7},{6,0},{7,1},{8,10},{9,11},{10,... | collective-permute-start | bytes 393224 | tf_op jit(solution)/shard_map/ppermute | solution.py:302
  197.5 18.4 %collective-permute-start.20 = (bf16[64,1024]{1,0:T(8,128)(2,1)S(1)}, bf16[64,1024]{1,0:T(8,128)(2,1)S(1)}, u32[]{:S(2)}, u32[]{:S(2)}) collective-permute-start(bf16[64,1024]{1,0:T(8,128)(2,1)S(1)} %get-tuple-element.37), channel_id=1, source_target_pairs={{0,3},{1,2},{2,5},{3,4},{4,7},{5,6},{6,1},{7,0},{8,11},{9,10},{10,... | collective-permute-start | bytes 393224 | tf_op jit(solution)/shard_map/ppermute | solution.py:302

commit v2 on v1

v2 whole, which is shorter than its diff:
```python
import functools

import jax
import jax.numpy as jnp
from jax import lax
from jax.experimental import pallas as pl
from jax.experimental.pallas import tpu as pltpu
from jax.sharding import Mesh, PartitionSpec as P

AXES = ("y", "x", "zh", "zl", "c")


def shifted(value, rows):
    at = lax.broadcasted_iota(jnp.int32, value.shape, 0)
    return jnp.where(at >= rows, pltpu.roll(value, rows, 0), 0.0)


def scan_block(current, before, refs, core, mixed, states):
    taps, bias, rate, skip = refs
    width = taps.shape[1]
    ext = jnp.concatenate([before[:, :width], current[:, :width]], axis=0)
    total = taps[0:1, :] * ext[13:141]
    for k in (1, 2, 3):
        total = total + taps[k : k + 1, :] * ext[13 + k : 141 + k]
    values = (total / (1.0 + jnp.exp(-total))).astype(jnp.bfloat16)
    xs, bs, cs = values[:, :1024], values[:, 1024:1152], values[:, 1152:1280]

    raw = current[:, width:] + bias[...]
    step = jnp.maximum(raw, 0.0) + jnp.log1p(jnp.exp(-jnp.abs(raw)))
    cum = -rate[...] * step
    for rows in (1, 2, 4, 8, 16, 32, 64):
        cum = cum + shifted(cum, rows)
    cum_t, step_t = cum.T, step.T
    factor = step * jnp.exp(cum[127:128, :] - cum)
    scores = lax.dot_general(cs, bs, (((1,), (1,)), ((), ())), preferred_element_type=jnp.float32)
    lower = lax.broadcasted_iota(jnp.int32, (128, 128), 0) >= lax.broadcasted_iota(
        jnp.int32, (128, 128), 1
    )
    left = lax.broadcasted_iota(jnp.int32, (128, 128), 1) < 64
    for pair in range(8):
        lanes = slice(128 * pair, 128 * pair + 128)
        x_pair = xs[:, lanes]
        wide = x_pair.astype(jnp.float32)
        outs = []
        for h in (2 * pair, 2 * pair + 1):
            diff = cum[:, h : h + 1] - cum_t[h : h + 1, :]
            decay = jnp.exp(jnp.where(lower, diff, -1e30))
            weights = (scores * decay * step_t[h : h + 1, :]).astype(jnp.bfloat16)
            outs.append(jnp.dot(weights, x_pair, preferred_element_type=jnp.float32))
        out = jnp.where(left, outs[0], outs[1]) + skip[:, lanes] * wide
        out = out.astype(jnp.bfloat16)
        top, bottom = out[:64], out[64:]
        mixed[:64, lanes] = jnp.where(core == 0, top, bottom)
        mixed[64:, lanes] = jnp.where(core == 0, bottom, top)
        column = jnp.where(
            left, factor[:, 2 * pair : 2 * pair + 1], factor[:, 2 * pair + 1 : 2 * pair + 2]
        )
        carried = (wide * column).astype(jnp.bfloat16)
        state = lax.dot_general(
            carried, bs, (((0,), (0,)), ((), ())), preferred_element_type=jnp.float32
        )
        states[2 * pair] = state[:64]
        states[2 * pair + 1] = state[64:]


def scan_kernel(late, place, *refs):
    core, zl = place[0], place[1]
    sums, swapped, came, *refs = refs
    if late:
        refs = refs[:4] + refs[5:]
    params, outs = refs[:4], refs[4:]
    mixed, states, scratch, sems = outs[:2], outs[2], outs[3], outs[4]

    def whole(ref):
        return ref[...].astype(jnp.float32)

    def tail(value):
        return value[112:128]

    ahead = jnp.where(zl == 3, whole(swapped), sums[:128].astype(jnp.float32))
    behind = jnp.where(zl == 0, whole(swapped), sums[128:].astype(jnp.float32))
    total = jnp.sum(whole(came), axis=0).astype(jnp.bfloat16).astype(jnp.float32)
    if late:
        beyond = total
        work = [
            (behind, jnp.where(zl == 1, 0.0, tail(beyond)), lax.rem(zl + 3, 4)),
            (beyond, jnp.where(zl == 2, 0.0, tail(ahead)), lax.rem(zl + 2, 4)),
        ]
    else:
        mine = total
        work = [
            (mine, jnp.where(zl == 0, 0.0, tail(behind)), zl),
            (ahead, jnp.where(zl == 3, 0.0, tail(mine)), lax.rem(zl + 1, 4)),
        ]
    copies = []
    for k, (current, before, block) in enumerate(work):
        scan_block(current, before, params, core, mixed[k], scratch.at[k])
        copies.append(pltpu.make_async_copy(scratch.at[k], states.at[block], sems.at[k]))
        copies[-1].start()
    for copy in copies:
        copy.wait()


def scan(place, sums, params, states=None):
    whole = pl.BlockSpec(memory_space=pltpu.VMEM)
    late = states is not None
    operands = [place, *sums, *params] + ([states] if late else [])
    in_specs = [pl.BlockSpec(memory_space=pltpu.SMEM)] + [whole] * (len(sums) + len(params))
    in_specs += [pl.BlockSpec(memory_space=pl.ANY)] if late else []
    return pl.pallas_call(
        functools.partial(scan_kernel, late),
        out_shape=[jax.ShapeDtypeStruct((128, 1024), jnp.bfloat16)] * 2
        + [jax.ShapeDtypeStruct((4, 16, 64, 128), jnp.float32)],
        in_specs=in_specs,
        out_specs=[whole] * 2 + [pl.BlockSpec(memory_space=pl.ANY)],
        scratch_shapes=[
            pltpu.VMEM((2, 16, 64, 128), jnp.float32),
            pltpu.SemaphoreType.DMA((2,)),
        ],
        input_output_aliases={len(operands) - 1: 2} if late else {},
        compiler_params=pltpu.CompilerParams(vmem_limit_bytes=48 << 20),
        cost_estimate=pl.CostEstimate(flops=1 << 20, bytes_accessed=1 << 16, transcendentals=0),
    )(*operands)


def assemble_kernel(place, *refs):
    blocks, other, out = refs[:4], refs[4], refs[5]
    pieces = [block[:64] for block in blocks] + [other[64 * k : 64 * k + 64] for k in range(4)]
    for k, piece in enumerate(pieces):
        out[:, pl.ds(pl.multiple_of(place[k] * 1024, 1024), 1024)] = piece


def assemble(place, pieces):
    whole = pl.BlockSpec(memory_space=pltpu.VMEM)
    return pl.pallas_call(
        assemble_kernel,
        out_shape=jax.ShapeDtypeStruct((64, 8192), jnp.bfloat16),
        in_specs=[pl.BlockSpec(memory_space=pltpu.SMEM)] + [whole] * 5,
        out_specs=whole,
        compiler_params=pltpu.CompilerParams(vmem_limit_bytes=16 << 20),
    )(place, *pieces)


def reorder_kernel(place, tokens, *outs):
    width = 256
    for part in range(4):
        for piece in range(8):
            start = pl.multiple_of(place[part * 8 + piece] * width, width)
            outs[part][:, piece * width : (piece + 1) * width] = tokens[:, pl.ds(start, width)]


def reorder_tokens(tokens, place):
    rows = tokens.shape[0]
    whole = pl.BlockSpec(memory_space=pltpu.VMEM)
    return pl.pallas_call(
        reorder_kernel,
        out_shape=[jax.ShapeDtypeStruct((rows, 2048), tokens.dtype)] * 4,
        in_specs=[pl.BlockSpec(memory_space=pltpu.SMEM), whole],
        out_specs=[whole] * 4,
        compiler_params=pltpu.CompilerParams(vmem_limit_bytes=16 << 20),
    )(place, tokens)


TILE = 768


def project_kernel(pairs, start, place, *refs):
    chunks, refs = refs[: 2 * pairs], refs[2 * pairs :]
    near, far, out = refs[:4], refs[4:8], refs[8]
    tile = pl.program_id(0)
    core, zh, y = place[0], place[2], place[3]

    def work(group, paired):
        mine = jnp.concatenate([ref[...] for ref in near], axis=0)
        values = [ref[...] for ref in group]
        if not paired:
            values = [value[h : h + 256] for h in (0, 256) for value in values]
        twin = jnp.concatenate(values, axis=0)
        rhs = jnp.concatenate(
            [jnp.where(zh == 0, mine, twin), jnp.where(zh == 0, twin, mine)], axis=0
        )
        for p in range(pairs):
            lhs = jnp.concatenate([chunks[2 * p][...], chunks[2 * p + 1][...]], axis=0)
            partial = jnp.dot(lhs, rhs, preferred_element_type=jnp.float32)
            for half, at in ((0, core), (256, 1 - core)):
                rows = pl.ds(pl.multiple_of(p * 128 + at * 64, 64), 64)
                for d in range(4):
                    low = half + 64 * d
                    out[y ^ d, rows, :] = partial[low : low + 64].astype(jnp.bfloat16)

    pl.when(tile < start)(lambda: work(far[:2], True))
    pl.when(tile >= start)(lambda: work(far[2:], False))


def project(place, chunks, panels):
    pairs = len(chunks) // 2
    widths = [panels[4].shape[1], panels[6].shape[1]]
    counts = [pl.cdiv(width, TILE) for width in widths]
    whole = pl.BlockSpec((256, 2048), lambda j: (0, 0))
    near = pl.BlockSpec((256, TILE), lambda j: (0, j))
    first = pl.BlockSpec((512, TILE), lambda j: (0, jnp.minimum(j, counts[0] - 1)))
    last = pl.BlockSpec((512, TILE), lambda j: (0, jnp.maximum(j - counts[0], 0)))
    return pl.pallas_call(
        functools.partial(project_kernel, pairs, counts[0]),
        grid=(sum(counts),),
        out_shape=jax.ShapeDtypeStruct((4, 128 * pairs, sum(widths)), jnp.bfloat16),
        in_specs=[pl.BlockSpec(memory_space=pltpu.SMEM)]
        + [whole] * len(chunks) + [near] * 4 + [first] * 2 + [last] * 2,
        out_specs=pl.BlockSpec((4, 128 * pairs, TILE), lambda j: (0, 0, j)),
        compiler_params=pltpu.CompilerParams(vmem_limit_bytes=60 << 20),
        cost_estimate=pl.CostEstimate(flops=1 << 20, bytes_accessed=1 << 16, transcendentals=0),
    )(place, *chunks, *panels)


def after(values, *others):
    flat, tree = jax.tree.flatten(values)
    held = lax.optimization_barrier(tuple(flat) + tuple(jax.tree.leaves(others)))
    return jax.tree.unflatten(tree, held[: len(flat)])


def swap(value, axis, distance):
    size = lax.axis_size(axis)
    return lax.ppermute(value, axis, [(i, i ^ distance) for i in range(size)])


def gather_x(panel, first, second, *others):
    both = jnp.concatenate([panel, swap(panel, "x", first)], axis=0)
    return [both, swap(after(both, *others), "x", second)]


def exchange(parts):
    return lax.all_to_all(parts, "y", split_axis=0, concat_axis=0, tiled=True)


def add_up(came):
    return jnp.sum(came.astype(jnp.float32), axis=0).astype(jnp.bfloat16)


def per_device(tokens, w_x, w_b, w_c, w_dt, conv_x, conv_b, conv_c, dt_bias, decay_rate, d_skip):
    y, x, zh, zl, core = (lax.axis_index(a) for a in AXES)
    split = TILE
    panel = jnp.concatenate([w_x, w_b, w_c, jnp.pad(w_dt, ((0, 0), (0, 112)))], axis=1)
    twin = swap(panel, "zh", 1)
    near = [panel] + [swap(panel, "x", d) for d in (1, 3, 2)]

    sources = x ^ jnp.asarray([0, 1, 3, 2])
    order = (
        (jnp.arange(4) ^ y)[:, None, None] * 8
        + jnp.arange(2)[None, :, None]
        + sources[None, None, :] * 2
    ).astype(jnp.int32).reshape(32)
    parts = reorder_tokens(after(tokens, panel), order)
    rows = [parts[0]] + [swap(parts[d], "y", d) for d in (1, 2, 3)]
    own = jnp.concatenate(rows, axis=0)
    own_other = swap(own, "c", 1)

    line = ("zh", "zl")
    own_sent, twin = after((own, twin), near)
    right1 = lax.ppermute(own_sent, line, [(i, (i + 1) % 8) for i in range(8)])
    left1 = lax.ppermute(own_sent, line, [(i, (i - 1) % 8) for i in range(8)])
    panels = near + gather_x(twin[:, :split], 1, 3)
    panels += gather_x(twin[:, split:], 3, 1)

    place = jnp.stack([core, zl, zh, y]).astype(jnp.int32)
    left1, right1 = after((left1, right1), panels)
    sides = [left1, swap(left1, "c", 1), right1, swap(right1, "c", 1)]
    parts = project(place, [own, own_other], panels)
    came_own = exchange(parts)
    parts = project(place, after(sides, parts), panels)
    came_sides = exchange(parts)

    left1, right1 = after((left1, right1), parts)
    right2 = lax.ppermute(right1, line, [(1, 2), (2, 3), (5, 6), (6, 7)])
    left2 = lax.ppermute(left1, line, [(1, 0), (2, 1), (5, 4), (6, 5)])
    second = jnp.where(zl < 2, left2, right2)
    pair = after([second, swap(second, "c", 1)], parts)
    parts = project(place, pair, panels)
    came_own, came_sides = after((came_own, came_sides), parts)
    came_second = exchange(parts)

    params = [
        jnp.concatenate([conv_x, conv_b, conv_c], axis=1),
        jnp.pad(dt_bias, (0, 112))[None],
        jnp.pad(decay_rate, (0, 112))[None],
        jnp.repeat(d_skip, 64)[None],
    ]
    sums = add_up(came_sides)
    swapped = lax.ppermute(
        jnp.where(zl == 3, sums[:128], sums[128:]), line, [(i, (i + 4) % 8) for i in (0, 3, 4, 7)]
    )
    *early, states = scan(place, [sums, swapped, came_own], params)
    def to(block, distance):
        return lax.ppermute(block, "zl", [(z, (z + distance) % 4) for z in range(4)])

    ahead = to(early[1], 1)
    came_second, ahead = after((came_second, ahead))
    *last, states = scan(place, [sums, swapped, came_second], params, states)
    blocks = [early[0], ahead, to(last[0], 3), to(last[1], 2)]
    other = swap(jnp.concatenate([block[64:] for block in blocks], axis=0), "c", 1)
    origin = (zl + jnp.asarray([0, 3, 1, 2])) % 4
    columns = jnp.concatenate([origin * 2 + core, origin * 2 + 1 - core])
    return (assemble(columns.astype(jnp.int32), blocks + [other]), states)


def solution(mesh):
    fine = Mesh(mesh.devices.reshape(4, 4, 2, 4, 2), AXES)
    fsdp, head = ("y", "x", "zh"), ("zl", "c")
    in_specs = (
        P(AXES, None),
        P(fsdp, head),
        P(fsdp, head),
        P(fsdp, head),
        P(fsdp, head),
        P(None, head),
        P(None, head),
        P(None, head),
        P(head),
        P(head),
        P(head),
    )
    out_specs = (P(AXES, None), P(fsdp, head, None, None))
    return jax.shard_map(
        per_device, mesh=fine, in_specs=in_specs, out_specs=out_specs, check_vma=False
    )
```

time: 218 us -> 211 us (0.968)
  waiting for transfers between devices: 84.6 us -> 93 us
  other arithmetic: 9.82 us -> 4.94 us
  starting transfers between devices: 71.6 us -> 67 us
  local copies, waits for them, and re-layouts: 9.28 us -> 6.04 us
  Pallas kernels: 41 us -> 38.7 us
    ppermute x1, waiting for transfers between devices: 4.05 us -> 14.6 us  [per_device(): left2 = lax.ppermute(left1, line, [(1, 0), (2, 1), (5, 4), (6, 5)])]
    ppermute x21 -> x20, waiting for transfers between devices: 65.4 us -> 55 us  [the longest x16 23.8 us: swap(): return lax.ppermute(value, axis, [(i, i ^ distance) for i in range(size)])]
    ppermute x1, waiting for transfers between devices: 0.01 us -> 8.14 us  [per_device(): left1 = lax.ppermute(own_sent, line, [(i, (i - 1) % 8) for i in range(8)])]
    ppermute x21 -> x20, starting transfers between devices: 47.8 us -> 42.5 us  [the longest x16 39.9 us: swap(): return lax.ppermute(value, axis, [(i, i ^ distance) for i in range(size)])]
    ppermute x1, waiting for transfers between devices: 0.01 us -> 4.55 us  [per_device(): right1 = lax.ppermute(own_sent, line, [(i, (i + 1) % 8) for i in range(8)])]
    all_to_all x4 -> x3, waiting for transfers between devices: 15.2 us -> 10.7 us  [exchange(): return lax.all_to_all(parts, 'y', split_axis=0, concat_axis=0, tiled=True)]
    slice x4 -> x6, local copies, waits for them, and re-layouts: 3.36 us -> 0.1 us  [the longest x4 0.04 us: per_device(): block[64:]]
    all_to_all x4 -> x3, starting transfers between devices: 16.5 us -> 13.3 us  [exchange(): return lax.all_to_all(parts, 'y', split_axis=0, concat_axis=0, tiled=True)]
  transfers between devices with their start and end apart: 29 -> 27, of which waited for: 11 -> 14; matrix products, arithmetic and copies ran while one was open for 4% -> 3% of each run, Pallas kernels for 16% -> 15%
where the time goes in v2:
time: 211 us
  waiting for transfers between devices  93 us (44%)
  starting transfers between devices  67 us (32%)
  Pallas kernels  38.7 us (18%)
  local copies, waits for them, and re-layouts  6.04 us (3%)
  other arithmetic  4.94 us (2%)
    ppermute x16, starting transfers between devices, swap(): return lax.ppermute(value, axis, [(i, i ^ distance) for i in range(size)])  39.9 us
    pallas_call x3, Pallas kernels, project(): pl.pallas_call(functools.partial(project_kernel, pairs, counts[0]), grid=...  26.7 us
    ppermute x16, waiting for transfers between devices, swap(): return lax.ppermute(value, axis, [(i, i ^ distance) for i in range(size)])  23.8 us
    ppermute x3, waiting for transfers between devices, to(): lax.ppermute(block, 'zl', [(z, (z + distance) % 4) for z in range(4)])  20.3 us
    ppermute x1, waiting for transfers between devices, per_device(): left2 = lax.ppermute(left1, line, [(1, 0), (2, 1), (5, 4), (6, 5)])  14.6 us
    all_to_all x3, starting transfers between devices, exchange(): return lax.all_to_all(parts, 'y', split_axis=0, concat_axis=0, tiled=True)  13.3 us
    ppermute x1, waiting for transfers between devices, per_device(): lax.ppermute(jnp.where(zl == 3, sums[:128], sums[128:]), line, [(i, (i +...  10.8 us
    all_to_all x3, waiting for transfers between devices, exchange(): return lax.all_to_all(parts, 'y', split_axis=0, concat_axis=0, tiled=True)  10.7 us
  transfers between devices with their start and end apart: 27, of which 14 were waited for; matrix products, arithmetic and copies ran while one was open for 3% of the time, Pallas kernels for 15%

profile of v2, /device:TPU:1, one launch (start us, length us, event | category | flops | bytes accessed | tf_op | source)
XLA Modules:
  0.0 210.8 jit_solution(2018158587758442606)
XLA Ops:
  0.7 0.9 copy.16
  1.6 1.2 fusion.1.refs_2_.refs_4_
  2.8 0.1 iota_add_fusion
  2.9 0.1 broadcast_add_fusion
  2.9 0.1 add.74.place
  3.0 0.7 shard_map.140
  3.7 2.2 %collective-permute-start = (bf16[64,2048]{1,0:T(8,128)(2,1)S(1)}, bf16[64,2048]{1,0:T(8,128)(2,1)S(1)}, u32[]{:S(2)}, u32[]{:S(2)}) collective-permute-start(bf16[64,2048]{1,0:T(8,128)(2,1)S(1)} %get-tuple-element.31), channel_id=1, source_target_pairs={{0,64},{64,0},{128,192},{192,128},{1,65},{65,1},{129,193},{193,129... | collective-permute-start | bytes 786440 | tf_op jit(solution)/shard_map/ppermute | solution.py:223
  5.9 2.6 %collective-permute-start.1 = (bf16[64,2048]{1,0:T(8,128)(2,1)S(1)}, bf16[64,2048]{1,0:T(8,128)(2,1)S(1)}, u32[]{:S(2)}, u32[]{:S(2)}) collective-permute-start(bf16[64,2048]{1,0:T(8,128)(2,1)S(1)} %get-tuple-element.32), channel_id=1, source_target_pairs={{0,128},{64,192},{128,0},{192,64},{1,129},{65,193},{129,1},{193,65... | collective-permute-start | bytes 786440 | tf_op jit(solution)/shard_map/ppermute | solution.py:223
  8.5 1.2 collective-permute-start.4
  9.8 1.8 collective-permute-start.5
  11.6 0.6 collective-permute-start.6
  12.2 6.9 %collective-permute-start.7 = (bf16[256,1408]{1,0:T(8,128)(2,1)S(1)}, bf16[256,1408]{1,0:T(8,128)(2,1)S(1)}, u32[]{:S(2)}, u32[]{:S(2)}) collective-permute-start(bf16[256,1408]{1,0:T(8,128)(2,1)S(1)} %fusion.1.refs_2_.refs_4_), channel_id=1, source_target_pairs={{0,8},{8,0},{1,9},{9,1},{2,10},{10,2},{3,11},{11,3},{4,12},{12,4},... | collective-permute-start | bytes 2162696 | tf_op jit(solution)/shard_map/ppermute | solution.py:223
  19.1 0.7 constant_dynamic-update-slice_fusion.3
  19.9 2.3 %collective-permute-start.2 = (bf16[64,2048]{1,0:T(8,128)(2,1)S(1)}, bf16[64,2048]{1,0:T(8,128)(2,1)S(1)}, u32[]{:S(2)}, u32[]{:S(2)}) collective-permute-start(bf16[64,2048]{1,0:T(8,128)(2,1)S(1)} %get-tuple-element.33), channel_id=1, source_target_pairs={{0,192},{64,128},{128,64},{192,0},{1,193},{65,129},{129,65},{193,1... | collective-permute-start | bytes 786440 | tf_op jit(solution)/shard_map/ppermute | solution.py:223
  22.2 0.7 constant_dynamic-update-slice_fusion.2
  22.9 0.7 constant_dynamic-update-slice_fusion.1
  23.6 3.0 %collective-permute-done.2 = bf16[64,2048]{1,0:T(8,128)(2,1)S(1)} collective-permute-done((bf16[64,2048]{1,0:T(8,128)(2,1)S(1)}, bf16[64,2048]{1,0:T(8,128)(2,1)S(1)}, u32[]{:S(2)}, u32[]{:S(2)}) %collective-permute-start.2) | collective-permute-done | bytes 262176 | tf_op jit(solution)/shard_map/ppermute | solution.py:223
  26.6 0.7 constant_dynamic-update-slice_fusion.refs_0_
  27.3 15.3 %collective-permute-done.6.refs_5_.refs_7_ = bf16[256,1408]{1,0:T(8,128)(2,1)S(1)} collective-permute-done((bf16[256,1408]{1,0:T(8,128)(2,1)S(1)}, bf16[256,1408]{1,0:T(8,128)(2,1)S(1)}, u32[]{:S(2)}, u32[]{:S(2)}) %collective-permute-start.6) | collective-permute-done | bytes 720928 | tf_op jit(solution)/shard_map/ppermute | solution.py:223
  42.6 0.8 copy-done.8
  43.5 0.1 collective-permute-start.8
  43.6 0.9 collective-permute-start.10
  44.5 5.6 %collective-permute-start.12 = (bf16[256,2048]{1,0:T(8,128)(2,1)}, bf16[256,2048]{1,0:T(8,128)(2,1)}, u32[]{:S(2)}, u32[]{:S(2)}) collective-permute-start(bf16[256,2048]{1,0:T(8,128)(2,1)} %constant_dynamic-update-slice_fusion.refs_0_), channel_id=1, source_target_pairs={{0,14},{2,0},{4,2},{6,4},{8,6},{10,8},{12,10},{14,12},{1,15},{3,1}... | collective-permute-start | bytes 3145736 | tf_op jit(solution)/shard_map/ppermute | solution.py:260
  50.1 2.5 %collective-permute-start.13 = (bf16[256,2048]{1,0:T(8,128)(2,1)}, bf16[256,2048]{1,0:T(8,128)(2,1)}, u32[]{:S(2)}, u32[]{:S(2)}) collective-permute-start(bf16[256,2048]{1,0:T(8,128)(2,1)} %constant_dynamic-update-slice_fusion.refs_0_), channel_id=1, source_target_pairs={{0,2},{2,4},{4,6},{6,8},{8,10},{10,12},{12,14},{14,0},{1,3},{3,5},... | collective-permute-start | bytes 3145736 | tf_op jit(solution)/shard_map/ppermute | solution.py:259
  52.7 0.9 collective-permute-start.9
  53.7 0.1 collective-permute-start.11
  53.8 9.4 %collective-permute-start.3 = (bf16[256,2048]{1,0:T(8,128)(2,1)}, bf16[256,2048]{1,0:T(8,128)(2,1)}, u32[]{:S(2)}, u32[]{:S(2)}) collective-permute-start(bf16[256,2048]{1,0:T(8,128)(2,1)} %constant_dynamic-update-slice_fusion.refs_0_), channel_id=1, source_target_pairs={{0,1},{1,0},{2,3},{3,2},{4,5},{5,4},{6,7},{7,6},{8,9},{9,8},{10,11... | collective-permute-start | bytes 3145736 | tf_op jit(solution)/shard_map/ppermute | solution.py:223
  63.2 1.8 collective-permute-done.11.refs_9_.refs_11_
  65.0 8.1 %collective-permute-done.12.refs_0_ = bf16[256,2048]{1,0:T(8,128)(2,1)} collective-permute-done((bf16[256,2048]{1,0:T(8,128)(2,1)}, bf16[256,2048]{1,0:T(8,128)(2,1)}, u32[]{:S(2)}, u32[]{:S(2)}) %collective-permute-start.12) | collective-permute-done | bytes 1048608 | tf_op jit(solution)/shard_map/ppermute | solution.py:260
  73.1 4.5 %collective-permute-done.13.refs_2_ = bf16[256,2048]{1,0:T(8,128)(2,1)} collective-permute-done((bf16[256,2048]{1,0:T(8,128)(2,1)}, bf16[256,2048]{1,0:T(8,128)(2,1)}, u32[]{:S(2)}, u32[]{:S(2)}) %collective-permute-start.13) | collective-permute-done | bytes 1048608 | tf_op jit(solution)/shard_map/ppermute | solution.py:259
  77.7 4.4 %collective-permute-start.14 = (bf16[256,2048]{1,0:T(8,128)(2,1)}, bf16[256,2048]{1,0:T(8,128)(2,1)}, u32[]{:S(2)}, u32[]{:S(2)}) collective-permute-start(bf16[256,2048]{1,0:T(8,128)(2,1)} %collective-permute-done.12.refs_0_), channel_id=1, source_target_pairs={{0,1},{1,0},{2,3},{3,2},{4,5},{5,4},{6,7},{7,6},{8,9},{9,8},{10,11... | collective-permute-start | bytes 3145736 | tf_op jit(solution)/shard_map/ppermute | solution.py:223
  82.1 0.3 collective-permute-start.15
  82.4 0.6 pad_add_fusion.1.place
  83.0 7.5 %shard_map.141 = bf16[4,128,1408]{2,1,0:T(8,128)(2,1)} custom-call(s32[4]{0:T(128)} %pad_add_fusion.1.place, bf16[256,2048]{1,0:T(8,128)(2,1)} %constant_dynamic-update-slice_fusion.refs_0_, bf16[256,2048]{1,0:T(8,128)(2,1)} %collective-permute-done.3.refs_1_, bf16[256,1408]{1,0:T(8,128)(2,1)} %copy-done.3, bf16[256,1408]{1,0:T(8,128)(2,1)} %copy-done.6, ...), custom_call_target="tpu_custom_call" | custom-call | flops 1048576 | bytes 65536 | tf_op jit(solution)/shard_map/pallas_call | solution.py:203
  90.5 4.2 %all-to-all-start = ((bf16[4,128,1408]{2,1,0:T(8,128)(2,1)}), bf16[4,128,1408]{2,1,0:T(8,128)(2,1)S(1)}, u32[]{:S(2)}, u32[]{:S(2)}) async-start(bf16[4,128,1408]{2,1,0:T(8,128)(2,1)} %shard_map.141), calls=%async_computation | async-start | bytes 2883584 | tf_op jit(solution)/shard_map/all_to_all | solution.py:232
  94.7 11.7 %shard_map.142 = bf16[4,256,1408]{2,1,0:T(8,128)(2,1)} custom-call(s32[4]{0:T(128)} %pad_add_fusion.1.place, bf16[256,2048]{1,0:T(8,128)(2,1)} %collective-permute-done.12.refs_0_, bf16[256,2048]{1,0:T(8,128)(2,1)} %collective-permute-done.14.refs_1_, bf16[256,2048]{1,0:T(8,128)(2,1)} %collective-permute-done.13.refs_2_, ...), custom_call_target="tpu_custom_call" | custom-call | flops 1048576 | bytes 65536 | tf_op jit(solution)/shard_map/pallas_call | solution.py:203
  106.4 1.3 collective-permute-start.16
  107.7 1.7 collective-permute-start.17
  109.4 4.2 %all-to-all-done.refs_2_ = bf16[4,128,1408]{2,1,0:T(8,128)(2,1)S(1)} async-done(((bf16[4,128,1408]{2,1,0:T(8,128)(2,1)}), bf16[4,128,1408]{2,1,0:T(8,128)(2,1)S(1)}, u32[]{:S(2)}, u32[]{:S(2)}) %all-to-all-start) | async-done | bytes 1441824 | tf_op jit(solution)/shard_map/all_to_all | solution.py:232
  113.5 4.6 %all-to-all-start.1 = ((bf16[4,256,1408]{2,1,0:T(8,128)(2,1)}), bf16[4,256,1408]{2,1,0:T(8,128)(2,1)}, u32[]{:S(2)}, u32[]{:S(2)}) async-start(bf16[4,256,1408]{2,1,0:T(8,128)(2,1)} %shard_map.142), calls=%async_computation.1 | async-start | bytes 5767168 | tf_op jit(solution)/shard_map/all_to_all | solution.py:232
  118.2 14.6 %collective-permute-done.16 = bf16[256,2048]{1,0:T(8,128)(2,1)S(1)} collective-permute-done((bf16[256,2048]{1,0:T(8,128)(2,1)}, bf16[256,2048]{1,0:T(8,128)(2,1)S(1)}, u32[]{:S(2)}, u32[]{:S(2)}) %collective-permute-start.16) | collective-permute-done | bytes 1048608 | tf_op jit(solution)/shard_map/ppermute | solution.py:274
  132.8 0.1 broadcast_select_fusion.refs_0_
  132.9 1.3 collective-permute-start.18
  134.3 2.3 %collective-permute-done.18.refs_1_ = bf16[256,2048]{1,0:T(8,128)(2,1)S(1)} collective-permute-done((bf16[256,2048]{1,0:T(8,128)(2,1)S(1)}, bf16[256,2048]{1,0:T(8,128)(2,1)S(1)}, u32[]{:S(2)}, u32[]{:S(2)}) %collective-permute-start.18) | collective-permute-done | bytes 1048608 | tf_op jit(solution)/shard_map/ppermute | solution.py:223
  136.5 1.0 copy-done.11
  137.5 7.5 %shard_map.143 = bf16[4,128,1408]{2,1,0:T(8,128)(2,1)} custom-call(s32[4]{0:T(128)} %pad_add_fusion.1.place, bf16[256,2048]{1,0:T(8,128)(2,1)} %copy-done.10, bf16[256,2048]{1,0:T(8,128)(2,1)} %copy-done.11, bf16[256,1408]{1,0:T(8,128)(2,1)} %copy-done.3, bf16[256,1408]{1,0:T(8,128)(2,1)} %copy-done.6, bf16[256,1408]{1,0:T(8,128)(2,1)} %copy-done.7, ...), custom_call_target="tpu_custom_call" | custom-call | flops 1048576 | bytes 65536 | tf_op jit(solution)/shard_map/pallas_call | solution.py:203
  145.1 6.6 %all-to-all-done.1 = bf16[4,256,1408]{2,1,0:T(8,128)(2,1)} async-done(((bf16[4,256,1408]{2,1,0:T(8,128)(2,1)}), bf16[4,256,1408]{2,1,0:T(8,128)(2,1)}, u32[]{:S(2)}, u32[]{:S(2)}) %all-to-all-start.1) | async-done | bytes 2883616 | tf_op jit(solution)/shard_map/all_to_all | solution.py:232
  151.6 4.5 %all-to-all-start.2 = ((bf16[4,128,1408]{2,1,0:T(8,128)(2,1)}), bf16[4,128,1408]{2,1,0:T(8,128)(2,1)}, u32[]{:S(2)}, u32[]{:S(2)}) async-start(bf16[4,128,1408]{2,1,0:T(8,128)(2,1)} %shard_map.143), calls=%async_computation.2 | async-start | bytes 2883584 | tf_op jit(solution)/shard_map/all_to_all | solution.py:232
  156.3 2.6 %reduce_sum.12.refs_0_ = bf16[256,1408]{1,0:T(8,128)(2,1)S(1)} reduce(bf16[4,256,1408]{2,1,0:T(8,128)(2,1)} %all-to-all-done.1, bf16[]{:T(256)} %constant.52.clone.1), dimensions={0}, to_apply=%region_0.1 | reduce | flops 1081344 | bytes 3604482 | tf_op jit(solution)/shard_map/reduce_sum | solution.py:236
  158.9 2.4 %collective-permute-start.19 = (bf16[128,1408]{1,0:T(8,128)(2,1)S(1)}, bf16[128,1408]{1,0:T(8,128)(2,1)S(1)}, u32[]{:S(2)}, u32[]{:S(2)}) collective-permute-start(bf16[128,1408]{1,0:T(8,128)(2,1)S(1)} %slice_select_fusion), channel_id=1, source_target_pairs={{0,8},{6,14},{8,0},{14,6},{1,9},{7,15},{9,1},{15,7},{16,24},{22,30... | collective-permute-start | bytes 1081352 | tf_op jit(solution)/shard_map/ppermute | solution.py:288
  161.4 0.1 broadcast_in_dim_reshape.3.refs_6_
  161.5 10.8 %collective-permute-done.19.refs_1_ = bf16[128,1408]{1,0:T(8,128)(2,1)S(1)} collective-permute-done((bf16[128,1408]{1,0:T(8,128)(2,1)S(1)}, bf16[128,1408]{1,0:T(8,128)(2,1)S(1)}, u32[]{:S(2)}, u32[]{:S(2)}) %collective-permute-start.19) | collective-permute-done | bytes 360480 | tf_op jit(solution)/shard_map/ppermute | solution.py:288
  172.4 4.4 %shard_map.144 = (bf16[128,1024]{1,0:T(8,128)(2,1)S(1)}, bf16[128,1024]{1,0:T(8,128)(2,1)S(1)}, f32[4,16,64,128]{3,2,1,0:T(8,128)}) custom-call(s32[4]{0:T(128)S(1)} %copy-done.1, bf16[256,1408]{1,0:T(8,128)(2,1)S(1)} %reduce_sum.12.refs_0_, bf16[128,1408]{1,0:T(8,128)(2,1)S(1)} %collective-permute-done.19.refs_1_, ...), custom_call_target="tpu_custom_call" | custom-call | flops 1048576 | bytes 65536 | tf_op jit(solution)/shard_map/pallas_call | solution.py:110
  176.8 0.1 collective-permute-start.20
  176.9 7.0 %collective-permute-done.20.refs_1_ = bf16[128,1024]{1,0:T(8,128)(2,1)S(1)} collective-permute-done((bf16[128,1024]{1,0:T(8,128)(2,1)S(1)}, bf16[128,1024]{1,0:T(8,128)(2,1)S(1)}, u32[]{:S(2)}, u32[]{:S(2)}) %collective-permute-start.20) | collective-permute-done | bytes 262176 | tf_op jit(solution)/shard_map/ppermute | solution.py:293
  183.9 5.3 %shard_map.145 = (bf16[128,1024]{1,0:T(8,128)(2,1)S(1)}, bf16[128,1024]{1,0:T(8,128)(2,1)S(1)}, f32[4,16,64,128]{3,2,1,0:T(8,128)}) custom-call(s32[4]{0:T(128)S(1)} %copy-done.1, bf16[256,1408]{1,0:T(8,128)(2,1)S(1)} %reduce_sum.12.refs_0_, bf16[128,1408]{1,0:T(8,128)(2,1)S(1)} %collective-permute-done.19.refs_1_, ...), custom_call_target="tpu_custom_call", output_to_operand_aliasing={{2}: (8, {})} | custom-call | flops 1048576 | bytes 65536 | tf_op jit(solution)/shard_map/pallas_call | solution.py:110
  189.2 0.1 collective-permute-start.21
  189.3 0.1 collective-permute-start.22
  189.5 6.7 %collective-permute-done.21.refs_2_ = bf16[128,1024]{1,0:T(8,128)(2,1)S(1)} collective-permute-done((bf16[128,1024]{1,0:T(8,128)(2,1)S(1)}, bf16[128,1024]{1,0:T(8,128)(2,1)S(1)}, u32[]{:S(2)}, u32[]{:S(2)}) %collective-permute-start.21) | collective-permute-done | bytes 262176 | tf_op jit(solution)/shard_map/ppermute | solution.py:293
  196.2 6.6 %collective-permute-done.22.refs_3_ = bf16[128,1024]{1,0:T(8,128)(2,1)S(1)} collective-permute-done((bf16[128,1024]{1,0:T(8,128)(2,1)S(1)}, bf16[128,1024]{1,0:T(8,128)(2,1)S(1)}, u32[]{:S(2)}, u32[]{:S(2)}) %collective-permute-start.22) | collective-permute-done | bytes 262176 | tf_op jit(solution)/shard_map/ppermute | solution.py:293
  202.9 4.8 %collective-permute-start.23 = (bf16[256,1024]{1,0:T(8,128)(2,1)S(1)}, bf16[256,1024]{1,0:T(8,128)(2,1)S(1)}, u32[]{:S(2)}, u32[]{:S(2)}) collective-permute-start(bf16[256,1024]{1,0:T(8,128)(2,1)S(1)} %pad_maximum_fusion.2), channel_id=1, source_target_pairs={{0,1},{1,0},{2,3},{3,2},{4,5},{5,4},{6,7},{7,6},{8,9},{9,8},{10,11... | collective-permute-start | bytes 1572872 | tf_op jit(solution)/shard_map/ppermute | solution.py:223
  207.7 0.1 pad_add_fusion.place
  207.8 1.4 collective-permute-done.23.refs_4_
  209.2 1.6 shard_map.146
  (70 shorter events, 0.6 us)
Async XLA Ops:
  0.6 2.2 %copy-start.19 = (s32[4]{0:T(128)S(1)}, s32[4]{0:T(128)}, u32[]{:S(2)}) copy-start(s32[4]{0:T(128)} %constant.54.clone) | copy-start | bytes 52
  0.6 2.4 %copy-start = (bf16[64,8192]{1,0:T(8,128)(2,1)S(1)}, bf16[64,8192]{1,0:T(8,128)(2,1)}, u32[]{:S(2)}) copy-start(bf16[64,8192]{1,0:T(8,128)(2,1)} %tokens) | copy-start | bytes 3145732
  2.7 24.6 %copy-start.3 = (bf16[256,1408]{1,0:T(8,128)(2,1)}, bf16[256,1408]{1,0:T(8,128)(2,1)S(1)}, u32[]{:S(2)}) copy-start(bf16[256,1408]{1,0:T(8,128)(2,1)S(1)} %fusion.1.refs_2_.refs_4_) | copy-start | bytes 2162692
  3.7 8.5 %collective-permute-start = (bf16[64,2048]{1,0:T(8,128)(2,1)S(1)}, bf16[64,2048]{1,0:T(8,128)(2,1)S(1)}, u32[]{:S(2)}, u32[]{:S(2)}) collective-permute-start(bf16[64,2048]{1,0:T(8,128)(2,1)S(1)} %get-tuple-element.31), channel_id=1, source_target_pairs={{0,64},{64,0},{128,192},{192,128},{1,65},{65,1},{129,193},{193,129... | collective-permute-start | bytes 786440 | tf_op jit(solution)/shard_map/ppermute | solution.py:223
  5.9 13.9 %collective-permute-start.1 = (bf16[64,2048]{1,0:T(8,128)(2,1)S(1)}, bf16[64,2048]{1,0:T(8,128)(2,1)S(1)}, u32[]{:S(2)}, u32[]{:S(2)}) collective-permute-start(bf16[64,2048]{1,0:T(8,128)(2,1)S(1)} %get-tuple-element.32), channel_id=1, source_target_pairs={{0,128},{64,192},{128,0},{192,64},{1,129},{65,193},{129,1},{193,65... | collective-permute-start | bytes 786440 | tf_op jit(solution)/shard_map/ppermute | solution.py:223
  8.5 18.8 %collective-permute-start.4 = (bf16[256,1408]{1,0:T(8,128)(2,1)S(1)}, bf16[256,1408]{1,0:T(8,128)(2,1)S(1)}, u32[]{:S(2)}, u32[]{:S(2)}) collective-permute-start(bf16[256,1408]{1,0:T(8,128)(2,1)S(1)} %fusion.1.refs_2_.refs_4_), channel_id=1, source_target_pairs={{0,16},{16,0},{32,48},{48,32},{1,17},{17,1},{33,49},{49,33},{2,18}... | collective-permute-start | bytes 2162696 | tf_op jit(solution)/shard_map/ppermute | solution.py:223
  9.8 17.6 %collective-permute-start.5 = (bf16[256,1408]{1,0:T(8,128)(2,1)S(1)}, bf16[256,1408]{1,0:T(8,128)(2,1)S(1)}, u32[]{:S(2)}, u32[]{:S(2)}) collective-permute-start(bf16[256,1408]{1,0:T(8,128)(2,1)S(1)} %fusion.1.refs_2_.refs_4_), channel_id=1, source_target_pairs={{0,48},{16,32},{32,16},{48,0},{1,49},{17,33},{33,17},{49,1},{2,50}... | collective-permute-start | bytes 2162696 | tf_op jit(solution)/shard_map/ppermute | solution.py:223
  11.6 31.1 %collective-permute-start.6 = (bf16[256,1408]{1,0:T(8,128)(2,1)S(1)}, bf16[256,1408]{1,0:T(8,128)(2,1)S(1)}, u32[]{:S(2)}, u32[]{:S(2)}) collective-permute-start(bf16[256,1408]{1,0:T(8,128)(2,1)S(1)} %fusion.1.refs_2_.refs_4_), channel_id=1, source_target_pairs={{0,32},{16,48},{32,0},{48,16},{1,33},{17,49},{33,1},{49,17},{2,34}... | collective-permute-start | bytes 2162696 | tf_op jit(solution)/shard_map/ppermute | solution.py:223
  12.2 31.3 %collective-permute-start.7 = (bf16[256,1408]{1,0:T(8,128)(2,1)S(1)}, bf16[256,1408]{1,0:T(8,128)(2,1)S(1)}, u32[]{:S(2)}, u32[]{:S(2)}) collective-permute-start(bf16[256,1408]{1,0:T(8,128)(2,1)S(1)} %fusion.1.refs_2_.refs_4_), channel_id=1, source_target_pairs={{0,8},{8,0},{1,9},{9,1},{2,10},{10,2},{3,11},{11,3},{4,12},{12,4},... | collective-permute-start | bytes 2162696 | tf_op jit(solution)/shard_map/ppermute | solution.py:223
  19.9 6.7 %collective-permute-start.2 = (bf16[64,2048]{1,0:T(8,128)(2,1)S(1)}, bf16[64,2048]{1,0:T(8,128)(2,1)S(1)}, u32[]{:S(2)}, u32[]{:S(2)}) collective-permute-start(bf16[64,2048]{1,0:T(8,128)(2,1)S(1)} %get-tuple-element.33), channel_id=1, source_target_pairs={{0,192},{64,128},{128,64},{192,0},{1,193},{65,129},{129,65},{193,1... | collective-permute-start | bytes 786440 | tf_op jit(solution)/shard_map/ppermute | solution.py:223
  27.3 15.3 %copy-start.6 = (bf16[256,1408]{1,0:T(8,128)(2,1)}, bf16[256,1408]{1,0:T(8,128)(2,1)S(1)}, u32[]{:S(2)}) copy-start(bf16[256,1408]{1,0:T(8,128)(2,1)S(1)} %collective-permute-done.4.refs_3_.refs_5_) | copy-start | bytes 2162692
  27.3 15.3 %copy-start.7 = (bf16[256,1408]{1,0:T(8,128)(2,1)}, bf16[256,1408]{1,0:T(8,128)(2,1)S(1)}, u32[]{:S(2)}) copy-start(bf16[256,1408]{1,0:T(8,128)(2,1)S(1)} %collective-permute-done.5.refs_4_.refs_6_) | copy-start | bytes 2162692
  42.6 0.8 copy-start.8
  43.5 9.1 %collective-permute-start.8 = (bf16[256,768]{1,0:T(8,128)(2,1)S(1)}, bf16[256,768]{1,0:T(8,128)(2,1)S(1)}, u32[]{:S(2)}, u32[]{:S(2)}) collective-permute-start(bf16[256,768]{1,0:T(8,128)(2,1)S(1)} %slice.24), channel_id=1, source_target_pairs={{0,16},{16,0},{32,48},{48,32},{1,17},{17,1},{33,49},{49,33},{2,18}... | collective-permute-start | bytes 1179656 | tf_op jit(solution)/shard_map/ppermute | solution.py:223
  43.6 10.0 %collective-permute-start.10 = (bf16[256,640]{1,0:T(8,128)(2,1)S(1)}, bf16[256,640]{1,0:T(8,128)(2,1)S(1)}, u32[]{:S(2)}, u32[]{:S(2)}) collective-permute-start(bf16[256,640]{1,0:T(8,128)(2,1)S(1)} %slice.25), channel_id=1, source_target_pairs={{0,48},{16,32},{32,16},{48,0},{1,49},{17,33},{33,17},{49,1},{2,50}... | collective-permute-start | bytes 983048 | tf_op jit(solution)/shard_map/ppermute | solution.py:223
  44.5 28.6 %collective-permute-start.12 = (bf16[256,2048]{1,0:T(8,128)(2,1)}, bf16[256,2048]{1,0:T(8,128)(2,1)}, u32[]{:S(2)}, u32[]{:S(2)}) collective-permute-start(bf16[256,2048]{1,0:T(8,128)(2,1)} %constant_dynamic-update-slice_fusion.refs_0_), channel_id=1, source_target_pairs={{0,14},{2,0},{4,2},{6,4},{8,6},{10,8},{12,10},{14,12},{1,15},{3,1}... | collective-permute-start | bytes 3145736 | tf_op jit(solution)/shard_map/ppermute | solution.py:260
  50.1 27.6 %collective-permute-start.13 = (bf16[256,2048]{1,0:T(8,128)(2,1)}, bf16[256,2048]{1,0:T(8,128)(2,1)}, u32[]{:S(2)}, u32[]{:S(2)}) collective-permute-start(bf16[256,2048]{1,0:T(8,128)(2,1)} %constant_dynamic-update-slice_fusion.refs_0_), channel_id=1, source_target_pairs={{0,2},{2,4},{4,6},{6,8},{8,10},{10,12},{12,14},{14,0},{1,3},{3,5},... | collective-permute-start | bytes 3145736 | tf_op jit(solution)/shard_map/ppermute | solution.py:259
  52.7 30.3 %copy-start.2 = (bf16[512,768]{1,0:T(8,128)(2,1)}, bf16[512,768]{1,0:T(8,128)(2,1)S(1)}, u32[]{:S(2)}) copy-start(bf16[512,768]{1,0:T(8,128)(2,1)S(1)} %pad_maximum_fusion.refs_6_.refs_8_) | copy-start | bytes 2359300
  52.7 25.0 %collective-permute-start.9 = (bf16[512,768]{1,0:T(8,128)(2,1)S(1)}, bf16[512,768]{1,0:T(8,128)(2,1)S(1)}, u32[]{:S(2)}, u32[]{:S(2)}) collective-permute-start(bf16[512,768]{1,0:T(8,128)(2,1)S(1)} %pad_maximum_fusion.refs_6_.refs_8_), channel_id=1, source_target_pairs={{0,48},{16,32},{32,16},{48,0},{1,49},{17,33},{33,17},{49,1},{2,50}... | collective-permute-start | bytes 2359304 | tf_op jit(solution)/shard_map/ppermute | solution.py:223
  53.7 29.3 %copy-start.4 = (bf16[512,640]{1,0:T(8,128)(2,1)}, bf16[512,640]{1,0:T(8,128)(2,1)S(1)}, u32[]{:S(2)}) copy-start(bf16[512,640]{1,0:T(8,128)(2,1)S(1)} %pad_maximum_fusion.1.refs_8_.refs_10_) | copy-start | bytes 1966084
  53.7 11.3 %collective-permute-start.11 = (bf16[512,640]{1,0:T(8,128)(2,1)S(1)}, bf16[512,640]{1,0:T(8,128)(2,1)S(1)}, u32[]{:S(2)}, u32[]{:S(2)}) collective-permute-start(bf16[512,640]{1,0:T(8,128)(2,1)S(1)} %pad_maximum_fusion.1.refs_8_.refs_10_), channel_id=1, source_target_pairs={{0,16},{16,0},{32,48},{48,32},{1,17},{17,1},{33,49},{49,33},{2,18}... | collective-permute-start | bytes 1966088 | tf_op jit(solution)/shard_map/ppermute | solution.py:223
  53.8 29.1 %collective-permute-start.3 = (bf16[256,2048]{1,0:T(8,128)(2,1)}, bf16[256,2048]{1,0:T(8,128)(2,1)}, u32[]{:S(2)}, u32[]{:S(2)}) collective-permute-start(bf16[256,2048]{1,0:T(8,128)(2,1)} %constant_dynamic-update-slice_fusion.refs_0_), channel_id=1, source_target_pairs={{0,1},{1,0},{2,3},{3,2},{4,5},{5,4},{6,7},{7,6},{8,9},{9,8},{10,11... | collective-permute-start | bytes 3145736 | tf_op jit(solution)/shard_map/ppermute | solution.py:223
  65.0 18.0 %copy-start.9 = (bf16[512,640]{1,0:T(8,128)(2,1)}, bf16[512,640]{1,0:T(8,128)(2,1)S(1)}, u32[]{:S(2)}) copy-start(bf16[512,640]{1,0:T(8,128)(2,1)S(1)} %collective-permute-done.11.refs_9_.refs_11_) | copy-start | bytes 1966084
  77.7 5.3 %copy-start.5 = (bf16[512,768]{1,0:T(8,128)(2,1)}, bf16[512,768]{1,0:T(8,128)(2,1)S(1)}, u32[]{:S(2)}) copy-start(bf16[512,768]{1,0:T(8,128)(2,1)S(1)} %collective-permute-done.9.refs_7_.refs_9_) | copy-start | bytes 2359300
  77.7 17.0 %collective-permute-start.14 = (bf16[256,2048]{1,0:T(8,128)(2,1)}, bf16[256,2048]{1,0:T(8,128)(2,1)}, u32[]{:S(2)}, u32[]{:S(2)}) collective-permute-start(bf16[256,2048]{1,0:T(8,128)(2,1)} %collective-permute-done.12.refs_0_), channel_id=1, source_target_pairs={{0,1},{1,0},{2,3},{3,2},{4,5},{5,4},{6,7},{7,6},{8,9},{9,8},{10,11... | collective-permute-start | bytes 3145736 | tf_op jit(solution)/shard_map/ppermute | solution.py:223
  82.1 12.6 %collective-permute-start.15 = (bf16[256,2048]{1,0:T(8,128)(2,1)}, bf16[256,2048]{1,0:T(8,128)(2,1)}, u32[]{:S(2)}, u32[]{:S(2)}) collective-permute-start(bf16[256,2048]{1,0:T(8,128)(2,1)} %collective-permute-done.13.refs_2_), channel_id=1, source_target_pairs={{0,1},{1,0},{2,3},{3,2},{4,5},{5,4},{6,7},{7,6},{8,9},{9,8},{10,11... | collective-permute-start | bytes 3145736 | tf_op jit(solution)/shard_map/ppermute | solution.py:223
  90.5 23.1 %all-to-all-start = ((bf16[4,128,1408]{2,1,0:T(8,128)(2,1)}), bf16[4,128,1408]{2,1,0:T(8,128)(2,1)S(1)}, u32[]{:S(2)}, u32[]{:S(2)}) async-start(bf16[4,128,1408]{2,1,0:T(8,128)(2,1)} %shard_map.141), calls=%async_computation | async-start | bytes 2883584 | tf_op jit(solution)/shard_map/all_to_all | solution.py:232
  106.4 26.4 %collective-permute-start.16 = (bf16[256,2048]{1,0:T(8,128)(2,1)}, bf16[256,2048]{1,0:T(8,128)(2,1)S(1)}, u32[]{:S(2)}, u32[]{:S(2)}) collective-permute-start(bf16[256,2048]{1,0:T(8,128)(2,1)} %collective-permute-done.12.refs_0_), channel_id=1, source_target_pairs={{2,0},{4,2},{10,8},{12,10},{3,1},{5,3},{11,9},{13,11},{18,16},{20,... | collective-permute-start | bytes 3145736 | tf_op jit(solution)/shard_map/ppermute | solution.py:274
  107.7 25.1 %collective-permute-start.17 = (bf16[256,2048]{1,0:T(8,128)(2,1)}, bf16[256,2048]{1,0:T(8,128)(2,1)}, u32[]{:S(2)}, u32[]{:S(2)}) collective-permute-start(bf16[256,2048]{1,0:T(8,128)(2,1)} %collective-permute-done.13.refs_2_), channel_id=1, source_target_pairs={{2,4},{4,6},{10,12},{12,14},{3,5},{5,7},{11,13},{13,15},{18,20},{2... | collective-permute-start | bytes 3145736 | tf_op jit(solution)/shard_map/ppermute | solution.py:273
  113.5 38.1 %all-to-all-start.1 = ((bf16[4,256,1408]{2,1,0:T(8,128)(2,1)}), bf16[4,256,1408]{2,1,0:T(8,128)(2,1)}, u32[]{:S(2)}, u32[]{:S(2)}) async-start(bf16[4,256,1408]{2,1,0:T(8,128)(2,1)} %shard_map.142), calls=%async_computation.1 | async-start | bytes 5767168 | tf_op jit(solution)/shard_map/all_to_all | solution.py:232
  132.9 3.6 %copy-start.10 = (bf16[256,2048]{1,0:T(8,128)(2,1)}, bf16[256,2048]{1,0:T(8,128)(2,1)S(1)}, u32[]{:S(2)}) copy-start(bf16[256,2048]{1,0:T(8,128)(2,1)S(1)} %broadcast_select_fusion.refs_0_) | copy-start | bytes 3145732
  132.9 3.6 %collective-permute-start.18 = (bf16[256,2048]{1,0:T(8,128)(2,1)S(1)}, bf16[256,2048]{1,0:T(8,128)(2,1)S(1)}, u32[]{:S(2)}, u32[]{:S(2)}) collective-permute-start(bf16[256,2048]{1,0:T(8,128)(2,1)S(1)} %broadcast_select_fusion.refs_0_), channel_id=1, source_target_pairs={{0,1},{1,0},{2,3},{3,2},{4,5},{5,4},{6,7},{7,6},{8,9},{9,8},{10,11... | collective-permute-start | bytes 3145736 | tf_op jit(solution)/shard_map/ppermute | solution.py:223
  136.5 1.0 copy-start.11
  151.6 32.3 %all-to-all-start.2 = ((bf16[4,128,1408]{2,1,0:T(8,128)(2,1)}), bf16[4,128,1408]{2,1,0:T(8,128)(2,1)}, u32[]{:S(2)}, u32[]{:S(2)}) async-start(bf16[4,128,1408]{2,1,0:T(8,128)(2,1)} %shard_map.143), calls=%async_computation.2 | async-start | bytes 2883584 | tf_op jit(solution)/shard_map/all_to_all | solution.py:232
  156.2 5.1 %copy-start.17 = (f32[16]{0:T(128)S(1)}, f32[16]{0:T(128)}, u32[]{:S(2)}) copy-start(f32[16]{0:T(128)} %param.22) | copy-start | bytes 196
  156.2 5.1 %copy-start.18 = (f32[16]{0:T(128)S(1)}, f32[16]{0:T(128)}, u32[]{:S(2)}) copy-start(f32[16]{0:T(128)} %param.21) | copy-start | bytes 196
  156.2 5.1 %copy-start.15 = (f32[16]{0:T(128)S(1)}, f32[16]{0:T(128)}, u32[]{:S(2)}) copy-start(f32[16]{0:T(128)} %param.23) | copy-start | bytes 196
  156.2 5.3 %copy-start.12 = (f32[4,1024]{1,0:T(4,128)S(1)}, f32[4,1024]{1,0:T(4,128)}, u32[]{:S(2)}) copy-start(f32[4,1024]{1,0:T(4,128)} %param.18) | copy-start | bytes 49156
  156.2 5.3 %copy-start.13 = (f32[4,128]{1,0:T(4,128)S(1)}, f32[4,128]{1,0:T(4,128)}, u32[]{:S(2)}) copy-start(f32[4,128]{1,0:T(4,128)} %param.19) | copy-start | bytes 6148
  156.2 5.3 %copy-start.14 = (f32[4,128]{1,0:T(4,128)S(1)}, f32[4,128]{1,0:T(4,128)}, u32[]{:S(2)}) copy-start(f32[4,128]{1,0:T(4,128)} %param.20) | copy-start | bytes 6148
  156.2 16.1 %copy-start.1 = (s32[4]{0:T(128)S(1)}, s32[4]{0:T(128)}, u32[]{:S(2)}) copy-start(s32[4]{0:T(128)} %pad_add_fusion.1.place) | copy-start | bytes 52
  158.9 13.5 %collective-permute-start.19 = (bf16[128,1408]{1,0:T(8,128)(2,1)S(1)}, bf16[128,1408]{1,0:T(8,128)(2,1)S(1)}, u32[]{:S(2)}, u32[]{:S(2)}) collective-permute-start(bf16[128,1408]{1,0:T(8,128)(2,1)S(1)} %slice_select_fusion), channel_id=1, source_target_pairs={{0,8},{6,14},{8,0},{14,6},{1,9},{7,15},{9,1},{15,7},{16,24},{22,30... | collective-permute-start | bytes 1081352 | tf_op jit(solution)/shard_map/ppermute | solution.py:288
  176.8 7.1 %collective-permute-start.20 = (bf16[128,1024]{1,0:T(8,128)(2,1)S(1)}, bf16[128,1024]{1,0:T(8,128)(2,1)S(1)}, u32[]{:S(2)}, u32[]{:S(2)}) collective-permute-start(bf16[128,1024]{1,0:T(8,128)(2,1)S(1)} %get-tuple-element.49), channel_id=1, source_target_pairs={{0,2},{2,4},{4,6},{6,0},{1,3},{3,5},{5,7},{7,1},{8,10},{10,12},{12... | collective-permute-start | bytes 786440 | tf_op jit(solution)/shard_map/ppermute | solution.py:293
  189.2 18.4 %copy-start.16 = (s32[4]{0:T(128)S(1)}, s32[4]{0:T(128)}, u32[]{:S(2)}) copy-start(s32[4]{0:T(128)} %constant.55.clone) | copy-start | bytes 52
  189.2 6.9 %collective-permute-start.21 = (bf16[128,1024]{1,0:T(8,128)(2,1)S(1)}, bf16[128,1024]{1,0:T(8,128)(2,1)S(1)}, u32[]{:S(2)}, u32[]{:S(2)}) collective-permute-start(bf16[128,1024]{1,0:T(8,128)(2,1)S(1)} %get-tuple-element.53), channel_id=1, source_target_pairs={{0,6},{2,0},{4,2},{6,4},{1,7},{3,1},{5,3},{7,5},{8,14},{10,8},{12,... | collective-permute-start | bytes 786440 | tf_op jit(solution)/shard_map/ppermute | solution.py:293
  189.3 13.5 %collective-permute-start.22 = (bf16[128,1024]{1,0:T(8,128)(2,1)S(1)}, bf16[128,1024]{1,0:T(8,128)(2,1)S(1)}, u32[]{:S(2)}, u32[]{:S(2)}) collective-permute-start(bf16[128,1024]{1,0:T(8,128)(2,1)S(1)} %get-tuple-element.54), channel_id=1, source_target_pairs={{0,4},{2,6},{4,0},{6,2},{1,5},{3,7},{5,1},{7,3},{8,12},{10,14},{12... | collective-permute-start | bytes 786440 | tf_op jit(solution)/shard_map/ppermute | solution.py:293
  202.9 6.3 %collective-permute-start.23 = (bf16[256,1024]{1,0:T(8,128)(2,1)S(1)}, bf16[256,1024]{1,0:T(8,128)(2,1)S(1)}, u32[]{:S(2)}, u32[]{:S(2)}) collective-permute-start(bf16[256,1024]{1,0:T(8,128)(2,1)S(1)} %pad_maximum_fusion.2), channel_id=1, source_target_pairs={{0,1},{1,0},{2,3},{3,2},{4,5},{5,4},{6,7},{7,6},{8,9},{9,8},{10,11... | collective-permute-start | bytes 1572872 | tf_op jit(solution)/shard_map/ppermute | solution.py:223

commit v3 on v2

v3 whole, which is shorter than its diff:
```python
import functools

import jax
import jax.numpy as jnp
from jax import lax
from jax.experimental import pallas as pl
from jax.experimental.pallas import tpu as pltpu
from jax.sharding import Mesh, PartitionSpec as P

AXES = ("y", "x", "zh", "zl", "c")


def shifted(value, rows):
    at = lax.broadcasted_iota(jnp.int32, value.shape, 0)
    return jnp.where(at >= rows, pltpu.roll(value, rows, 0), 0.0)


def scan_block(current, before, refs, core, same, other, states):
    taps, bias, rate, skip = refs
    width = taps.shape[1]
    ext = jnp.concatenate([before[:, :width], current[:, :width]], axis=0)
    total = taps[0:1, :] * ext[13:141]
    for k in (1, 2, 3):
        total = total + taps[k : k + 1, :] * ext[13 + k : 141 + k]
    values = (total / (1.0 + jnp.exp(-total))).astype(jnp.bfloat16)
    xs, bs, cs = values[:, :1024], values[:, 1024:1152], values[:, 1152:1280]

    raw = current[:, width:] + bias[...]
    step = jnp.maximum(raw, 0.0) + jnp.log1p(jnp.exp(-jnp.abs(raw)))
    cum = -rate[...] * step
    for rows in (1, 2, 4, 8, 16, 32, 64):
        cum = cum + shifted(cum, rows)
    cum_t, step_t = cum.T, step.T
    factor = step * jnp.exp(cum[127:128, :] - cum)
    scores = lax.dot_general(cs, bs, (((1,), (1,)), ((), ())), preferred_element_type=jnp.float32)
    lower = lax.broadcasted_iota(jnp.int32, (128, 128), 0) >= lax.broadcasted_iota(
        jnp.int32, (128, 128), 1
    )
    left = lax.broadcasted_iota(jnp.int32, (128, 128), 1) < 64
    for pair in range(8):
        lanes = slice(128 * pair, 128 * pair + 128)
        x_pair = xs[:, lanes]
        wide = x_pair.astype(jnp.float32)
        outs = []
        for h in (2 * pair, 2 * pair + 1):
            diff = cum[:, h : h + 1] - cum_t[h : h + 1, :]
            decay = jnp.exp(jnp.where(lower, diff, -1e30))
            weights = (scores * decay * step_t[h : h + 1, :]).astype(jnp.bfloat16)
            outs.append(jnp.dot(weights, x_pair, preferred_element_type=jnp.float32))
        out = jnp.where(left, outs[0], outs[1]) + skip[:, lanes] * wide
        out = out.astype(jnp.bfloat16)
        top, bottom = out[:64], out[64:]
        same[:, lanes] = jnp.where(core == 0, top, bottom)
        other[:, lanes] = jnp.where(core == 0, bottom, top)
        column = jnp.where(
            left, factor[:, 2 * pair : 2 * pair + 1], factor[:, 2 * pair + 1 : 2 * pair + 2]
        )
        carried = (wide * column).astype(jnp.bfloat16)
        state = lax.dot_general(
            carried, bs, (((0,), (0,)), ((), ())), preferred_element_type=jnp.float32
        )
        states[2 * pair] = state[:64]
        states[2 * pair + 1] = state[64:]


def scan_kernel(late, place, *refs):
    core, zl = place[0], place[1]
    sums, came, *refs = refs
    if late:
        swapped, *refs = refs
        refs = refs[:4] + refs[5:]
    params, (*pieces, states, scratch, sems) = refs[:4], refs[4:]

    def whole(ref):
        return ref[...].astype(jnp.float32)

    def tail(value):
        return value[112:128]

    ahead, behind = (sums[k : k + 128].astype(jnp.float32) for k in (0, 128))
    total = jnp.sum(whole(came), axis=0).astype(jnp.bfloat16).astype(jnp.float32)
    always = zl >= 0
    if late:
        first = whole(swapped)
        ahead = jnp.where(zl == 3, first, ahead)
        behind = jnp.where(zl == 0, first, behind)
        work = [
            (zl == 3, first, jnp.zeros_like(tail(first)), 0),
            (always, total, jnp.where(zl == 2, 0.0, tail(ahead)), lax.rem(zl + 2, 4)),
            (always, behind, jnp.where(zl == 1, 0.0, tail(total)), lax.rem(zl + 3, 4)),
        ]
    else:
        work = [
            (always, total, jnp.where(zl == 0, 0.0, tail(behind)), zl),
            (zl < 3, ahead, tail(total), lax.rem(zl + 1, 4)),
        ]

    def copy(k, block):
        return pltpu.make_async_copy(scratch.at[k], states.at[block], sems.at[k])

    for k, (needed, current, before, block) in enumerate(work):
        @pl.when(needed)
        def _(k=k, current=current, before=before, block=block):
            same, other = pieces[2 * k], pieces[2 * k + 1]
            scan_block(current, before, params, core, same, other, scratch.at[k])
            copy(k, block).start()

    for k, (needed, _, _, block) in enumerate(work):
        pl.when(needed)(lambda k=k, block=block: copy(k, block).wait())


def scan(place, sums, params, states=None):
    whole = pl.BlockSpec(memory_space=pltpu.VMEM)
    late = states is not None
    blocks = 3 if late else 2
    operands = [place, *sums, *params] + ([states] if late else [])
    in_specs = [pl.BlockSpec(memory_space=pltpu.SMEM)] + [whole] * (len(sums) + len(params))
    in_specs += [pl.BlockSpec(memory_space=pl.ANY)] if late else []
    return pl.pallas_call(
        functools.partial(scan_kernel, late),
        out_shape=[jax.ShapeDtypeStruct((64, 1024), jnp.bfloat16)] * (2 * blocks)
        + [jax.ShapeDtypeStruct((4, 16, 64, 128), jnp.float32)],
        in_specs=in_specs,
        out_specs=[whole] * (2 * blocks) + [pl.BlockSpec(memory_space=pl.ANY)],
        scratch_shapes=[
            pltpu.VMEM((blocks, 16, 64, 128), jnp.float32),
            pltpu.SemaphoreType.DMA((blocks,)),
        ],
        input_output_aliases={len(operands) - 1: 2 * blocks} if late else {},
        compiler_params=pltpu.CompilerParams(vmem_limit_bytes=48 << 20),
        cost_estimate=pl.CostEstimate(flops=1 << 20, bytes_accessed=1 << 16, transcendentals=0),
    )(*operands)


def assemble_kernel(place, *refs):
    pieces, out = refs[:-1], refs[-1]
    values = [piece[...] for piece in pieces[2:]]
    values[:2] = [
        jnp.where(place[8] == 0, late[...], early) for late, early in zip(pieces[:2], values[:2])
    ]
    for k, value in enumerate(values):
        out[:, pl.ds(pl.multiple_of(place[k] * 1024, 1024), 1024)] = value


def assemble(place, pieces):
    whole = pl.BlockSpec(memory_space=pltpu.VMEM)
    return pl.pallas_call(
        assemble_kernel,
        out_shape=jax.ShapeDtypeStruct((64, 8192), jnp.bfloat16),
        in_specs=[pl.BlockSpec(memory_space=pltpu.SMEM)] + [whole] * 10,
        out_specs=whole,
        compiler_params=pltpu.CompilerParams(vmem_limit_bytes=16 << 20),
    )(place, *pieces)


def reorder_kernel(place, tokens, *outs):
    width = 256
    for part in range(4):
        for piece in range(8):
            start = pl.multiple_of(place[part * 8 + piece] * width, width)
            outs[part][:, piece * width : (piece + 1) * width] = tokens[:, pl.ds(start, width)]


def reorder_tokens(tokens, place):
    rows = tokens.shape[0]
    whole = pl.BlockSpec(memory_space=pltpu.VMEM)
    return pl.pallas_call(
        reorder_kernel,
        out_shape=[jax.ShapeDtypeStruct((rows, 2048), tokens.dtype)] * 4,
        in_specs=[pl.BlockSpec(memory_space=pltpu.SMEM), whole],
        out_specs=[whole] * 4,
        compiler_params=pltpu.CompilerParams(vmem_limit_bytes=16 << 20),
    )(place, tokens)


TILE = 768


def project_kernel(pairs, place, *refs):
    chunks, refs = refs[: 2 * pairs], refs[2 * pairs :]
    near, far, out = refs[:4], refs[4:9], refs[9]
    core, zh, y = place[0], place[2], place[3]
    mine = jnp.concatenate([ref[...] for ref in near], axis=0)
    across = jnp.where(pl.program_id(0) == 0, far[3][...], far[4][...])
    twin = jnp.concatenate([ref[...] for ref in far[:3]] + [across], axis=0)
    rhs = jnp.concatenate(
        [jnp.where(zh == 0, mine, twin), jnp.where(zh == 0, twin, mine)], axis=0
    )
    for p in range(pairs):
        lhs = jnp.concatenate([chunks[2 * p][...], chunks[2 * p + 1][...]], axis=0)
        partial = jnp.dot(lhs, rhs, preferred_element_type=jnp.float32)
        for half, at in ((0, core), (256, 1 - core)):
            rows = pl.ds(pl.multiple_of(p * 128 + at * 64, 64), 64)
            for d in range(4):
                low = half + 64 * d
                out[y ^ d, rows, :] = partial[low : low + 64].astype(jnp.bfloat16)


def project(place, chunks, panels):
    pairs = len(chunks) // 2
    width = panels[0].shape[1]
    whole = pl.BlockSpec((256, 2048), lambda j: (0, 0))
    column = pl.BlockSpec((256, TILE), lambda j: (0, j))
    single = pl.BlockSpec((256, TILE), lambda j: (0, 0))
    return pl.pallas_call(
        functools.partial(project_kernel, pairs),
        grid=(2,),
        out_shape=jax.ShapeDtypeStruct((4, 128 * pairs, width), jnp.bfloat16),
        in_specs=[pl.BlockSpec(memory_space=pltpu.SMEM)]
        + [whole] * len(chunks) + [column] * 7 + [single] * 2,
        out_specs=pl.BlockSpec((4, 128 * pairs, TILE), lambda j: (0, 0, j)),
        compiler_params=pltpu.CompilerParams(vmem_limit_bytes=60 << 20),
        cost_estimate=pl.CostEstimate(flops=1 << 20, bytes_accessed=1 << 16, transcendentals=0),
    )(place, *chunks, *panels)


def marker(value):
    anywhere = pl.BlockSpec(memory_space=pl.ANY)
    return pl.pallas_call(
        lambda given, same: None,
        out_shape=jax.ShapeDtypeStruct(value.shape, value.dtype),
        in_specs=[anywhere],
        out_specs=anywhere,
        input_output_aliases={0: 0},
        cost_estimate=pl.CostEstimate(flops=1 << 36, bytes_accessed=1 << 16, transcendentals=0),
    )(value)


def after(values, *others):
    flat, tree = jax.tree.flatten(values)
    held = lax.optimization_barrier(tuple(flat) + tuple(jax.tree.leaves(others)))
    return jax.tree.unflatten(tree, held[: len(flat)])


def swap(value, axis, distance):
    size = lax.axis_size(axis)
    return lax.ppermute(value, axis, [(i, i ^ distance) for i in range(size)])


def exchange(parts):
    return lax.all_to_all(parts, "y", split_axis=0, concat_axis=0, tiled=True)


def add_up(came):
    return jnp.sum(came.astype(jnp.float32), axis=0).astype(jnp.bfloat16)


def per_device(tokens, w_x, w_b, w_c, w_dt, conv_x, conv_b, conv_c, dt_bias, decay_rate, d_skip):
    y, x, zh, zl, core = (lax.axis_index(a) for a in AXES)
    panel = jnp.concatenate([w_x, w_b, w_c, jnp.pad(w_dt, ((0, 0), (0, 112)))], axis=1)
    twin = marker(swap(panel, "zh", 1))
    near = [panel] + [swap(panel, "x", d) for d in (1, 3, 2)]

    sources = x ^ jnp.asarray([0, 1, 3, 2])
    order = (
        (jnp.arange(4) ^ y)[:, None, None] * 8
        + jnp.arange(2)[None, :, None]
        + sources[None, None, :] * 2
    ).astype(jnp.int32).reshape(32)
    parts = reorder_tokens(after(tokens, panel), order)
    rows = [parts[0]] + [swap(parts[d], "y", d) for d in (1, 2, 3)]
    own = jnp.concatenate(rows, axis=0)
    own_other = swap(own, "c", 1)

    line = ("zh", "zl")
    own_sent, twin = after((own, twin), near)
    right1 = lax.ppermute(own_sent, line, [(i, (i + 1) % 8) for i in range(8)])
    left1 = lax.ppermute(own_sent, line, [(i, (i - 1) % 8) for i in range(8)])
    next_x, mirror_x = swap(twin, "x", 1), swap(twin, "x", 3)
    across = [swap(next_x[:, :TILE], "x", 3), swap(mirror_x[:, TILE:], "x", 1)]
    panels = near + [twin, next_x, mirror_x, *across]

    place = jnp.stack([core, zl, zh, y]).astype(jnp.int32)
    left1, right1 = after((left1, right1), panels)
    sides = [left1, swap(left1, "c", 1), right1, swap(right1, "c", 1)]
    parts = project(place, [own, own_other], panels)
    came_own = exchange(parts)
    parts = project(place, after(sides, parts), panels)
    came_sides = exchange(parts)

    left1, right1 = after((left1, right1), parts)
    right2 = lax.ppermute(right1, line, [(1, 2), (2, 3), (5, 6), (6, 7)])
    left2 = lax.ppermute(left1, line, [(1, 0), (2, 1), (5, 4), (6, 5)])
    second = jnp.where(zl < 2, left2, right2)
    pair = after([second, swap(second, "c", 1)], parts)
    parts = project(place, pair, panels)
    came_own, came_sides = after((came_own, came_sides), parts)
    came_second = exchange(parts)

    params = [
        jnp.concatenate([conv_x, conv_b, conv_c], axis=1),
        jnp.pad(dt_bias, (0, 112))[None],
        jnp.pad(decay_rate, (0, 112))[None],
        jnp.repeat(d_skip, 64)[None],
    ]
    sums = add_up(came_sides)
    swapped = lax.ppermute(
        jnp.where(zl == 3, sums[:128], sums[128:]), line, [(i, (i + 4) % 8) for i in (0, 3, 4, 7)]
    )
    *early, states = scan(place, [sums, came_own], params)

    def to(piece, distance, flip, origins=range(4)):
        pairs = [
            (2 * z + c, 2 * ((z + distance) % 4) + (c ^ flip)) for z in origins for c in range(2)
        ]
        return lax.ppermute(piece, ("zl", "c"), pairs)

    pieces = [to(early[2], 1, 0, range(3)), to(early[3], 1, 1, range(3))]
    pieces += [early[0], to(early[1], 0, 1)]
    came_second, pieces = after((came_second, pieces))
    *last, states = scan(place, [sums, came_second, swapped], params, states)
    pieces += [to(last[2], 2, 0), to(last[3], 2, 1), to(last[4], 3, 0), to(last[5], 3, 1)]
    pieces = [to(last[0], 1, 0, [3]), to(last[1], 1, 1, [3])] + pieces
    origin = zl + jnp.asarray([3, 3, 0, 0, 2, 2, 1, 1])
    columns = (origin % 4) * 2 + (core + jnp.asarray([0, 1] * 4)) % 2
    columns = jnp.concatenate([columns, zl[None]]).astype(jnp.int32)
    return (assemble(columns, pieces), states)


def solution(mesh):
    fine = Mesh(mesh.devices.reshape(4, 4, 2, 4, 2), AXES)
    fsdp, head = ("y", "x", "zh"), ("zl", "c")
    in_specs = (
        P(AXES, None),
        P(fsdp, head),
        P(fsdp, head),
        P(fsdp, head),
        P(fsdp, head),
        P(None, head),
        P(None, head),
        P(None, head),
        P(head),
        P(head),
        P(head),
    )
    out_specs = (P(AXES, None), P(fsdp, head, None, None))
    return jax.shard_map(
        per_device, mesh=fine, in_specs=in_specs, out_specs=out_specs, check_vma=False
    )
```

time: 211 us -> 205 us (0.972); the launches traced: 211 us -> 201 us
  waiting for transfers between devices: 93 us -> 75.7 us
  starting transfers between devices: 67 us -> 73.9 us
    ppermute x3 -> x9, starting transfers between devices: 0.26 us -> 17.1 us  [to(): return lax.ppermute(piece, ('zl', 'c'), pairs)]
    ppermute x1, waiting for transfers between devices: 10.8 us -> 0.01 us  [per_device(): lax.ppermute(jnp.where(zl == 3, sums[:128], sums[128:]), line, [(i, (i +...]
    ppermute x16 -> x15, starting transfers between devices: 39.9 us -> 30.7 us  [swap(): return lax.ppermute(value, axis, [(i, i ^ distance) for i in range(size)])]
    ppermute x3 -> x9, waiting for transfers between devices: 20.3 us -> 14.7 us  [to(): return lax.ppermute(piece, ('zl', 'c'), pairs)]
    ppermute x16 -> x15, waiting for transfers between devices: 23.8 us -> 26.3 us  [swap(): return lax.ppermute(value, axis, [(i, i ^ distance) for i in range(size)])]
    pallas_call x3 -> x4, Pallas kernels: 26.7 us -> 25.5 us  [the longest x3 25.5 us: project(): pl.pallas_call(functools.partial(project_kernel, pairs), grid=(2,), out_s...]
    unnamed x46 -> x48, local copies, waits for them, and re-layouts: 4.98 us -> 5.03 us
  transfers between devices with their start and end apart: 27 -> 32, of which waited for: 14 -> 14; matrix products, arithmetic and copies ran while one was open for 3% -> 4% of each run, Pallas kernels for 15% -> 15%
where the time goes in v3:
time: 205 us; the launch traced here: 201 us
  waiting for transfers between devices  75.7 us (37%)
  starting transfers between devices  73.9 us (36%)
  Pallas kernels  38.3 us (19%)
  local copies, waits for them, and re-layouts  6.06 us (3%)
  other arithmetic  5.99 us (3%)
    ppermute x15, starting transfers between devices, swap(): return lax.ppermute(value, axis, [(i, i ^ distance) for i in range(size)])  30.7 us
    ppermute x15, waiting for transfers between devices, swap(): return lax.ppermute(value, axis, [(i, i ^ distance) for i in range(size)])  26.3 us
    pallas_call x3, Pallas kernels, project(): pl.pallas_call(functools.partial(project_kernel, pairs), grid=(2,), out_s...  25.5 us
    ppermute x9, starting transfers between devices, to(): return lax.ppermute(piece, ('zl', 'c'), pairs)  17.1 us
    ppermute x9, waiting for transfers between devices, to(): return lax.ppermute(piece, ('zl', 'c'), pairs)  14.7 us
    ppermute x1, waiting for transfers between devices, per_device(): left2 = lax.ppermute(left1, line, [(1, 0), (2, 1), (5, 4), (6, 5)])  14.3 us
    all_to_all x3, starting transfers between devices, exchange(): return lax.all_to_all(parts, 'y', split_axis=0, concat_axis=0, tiled=True)  12.8 us
    pallas_call x2, Pallas kernels, scan(): pl.pallas_call(functools.partial(scan_kernel, late), out_shape=[jax.Shape...  10.5 us
  transfers between devices with their start and end apart: 32, of which 14 were waited for; matrix products, arithmetic and copies ran while one was open for 4% of the time, Pallas kernels for 15%

profile of v3, /device:TPU:1, one launch (start us, length us, event | category | flops | bytes accessed | tf_op | source)
XLA Modules:
  0.0 201.0 jit_solution(17341788741488602434)
XLA Ops:
  0.7 0.9 copy.18
  1.6 1.2 fusion.1.refs_2_.refs_4_
  2.9 0.1 add.79.place
  3.0 0.7 shard_map.149
  3.7 2.2 %collective-permute-start = (bf16[64,2048]{1,0:T(8,128)(2,1)S(1)}, bf16[64,2048]{1,0:T(8,128)(2,1)S(1)}, u32[]{:S(2)}, u32[]{:S(2)}) collective-permute-start(bf16[64,2048]{1,0:T(8,128)(2,1)S(1)} %get-tuple-element.40), channel_id=1, source_target_pairs={{0,64},{64,0},{128,192},{192,128},{1,65},{65,1},{129,193},{193,129... | collective-permute-start | bytes 786440 | tf_op jit(solution)/shard_map/ppermute | solution.py:237
  5.9 1.2 collective-permute-start.4
  7.1 1.8 collective-permute-start.5
  8.9 6.9 %collective-permute-start.7 = (bf16[256,1408]{1,0:T(8,128)(2,1)S(1)}, bf16[256,1408]{1,0:T(8,128)(2,1)}, u32[]{:S(2)}, u32[]{:S(2)}) collective-permute-start(bf16[256,1408]{1,0:T(8,128)(2,1)S(1)} %fusion.1.refs_2_.refs_4_), channel_id=1, source_target_pairs={{0,8},{8,0},{1,9},{9,1},{2,10},{10,2},{3,11},{11,3},{4,12},{12,4},... | collective-permute-start | bytes 2162696 | tf_op jit(solution)/shard_map/ppermute | solution.py:237
  15.9 2.6 %collective-permute-start.1 = (bf16[64,2048]{1,0:T(8,128)(2,1)S(1)}, bf16[64,2048]{1,0:T(8,128)(2,1)S(1)}, u32[]{:S(2)}, u32[]{:S(2)}) collective-permute-start(bf16[64,2048]{1,0:T(8,128)(2,1)S(1)} %get-tuple-element.41), channel_id=1, source_target_pairs={{0,128},{64,192},{128,0},{192,64},{1,129},{65,193},{129,1},{193,65... | collective-permute-start | bytes 786440 | tf_op jit(solution)/shard_map/ppermute | solution.py:237
  18.5 0.7 constant_dynamic-update-slice_fusion.3
  19.2 0.7 constant_dynamic-update-slice_fusion.2
  19.9 3.5 %collective-permute-done.1 = bf16[64,2048]{1,0:T(8,128)(2,1)S(1)} collective-permute-done((bf16[64,2048]{1,0:T(8,128)(2,1)S(1)}, bf16[64,2048]{1,0:T(8,128)(2,1)S(1)}, u32[]{:S(2)}, u32[]{:S(2)}) %collective-permute-start.1) | collective-permute-done | bytes 262176 | tf_op jit(solution)/shard_map/ppermute | solution.py:237
  23.5 0.9 collective-permute-start.6
  24.4 0.7 constant_dynamic-update-slice_fusion.1
  25.1 6.2 %collective-permute-done.2 = bf16[64,2048]{1,0:T(8,128)(2,1)S(1)} collective-permute-done((bf16[64,2048]{1,0:T(8,128)(2,1)S(1)}, bf16[64,2048]{1,0:T(8,128)(2,1)S(1)}, u32[]{:S(2)}, u32[]{:S(2)}) %collective-permute-start.2) | collective-permute-done | bytes 262176 | tf_op jit(solution)/shard_map/ppermute | solution.py:237
  31.3 0.7 constant_dynamic-update-slice_fusion.refs_0_
  32.0 2.2 %collective-permute-done.7.given = bf16[256,1408]{1,0:T(8,128)(2,1)} collective-permute-done((bf16[256,1408]{1,0:T(8,128)(2,1)S(1)}, bf16[256,1408]{1,0:T(8,128)(2,1)}, u32[]{:S(2)}, u32[]{:S(2)}) %collective-permute-start.7) | collective-permute-done | bytes 720928 | tf_op jit(solution)/shard_map/ppermute | solution.py:237
  34.2 5.6 %collective-permute-done.6.refs_5_.refs_7_ = bf16[256,1408]{1,0:T(8,128)(2,1)S(1)} collective-permute-done((bf16[256,1408]{1,0:T(8,128)(2,1)S(1)}, bf16[256,1408]{1,0:T(8,128)(2,1)S(1)}, u32[]{:S(2)}, u32[]{:S(2)}) %collective-permute-start.6) | collective-permute-done | bytes 720928 | tf_op jit(solution)/shard_map/ppermute | solution.py:237
  39.9 0.9 copy-done.7
  40.8 0.3 collective-permute-start.8
  41.1 1.2 collective-permute-start.9
  42.3 5.2 %collective-permute-start.12 = (bf16[256,2048]{1,0:T(8,128)(2,1)}, bf16[256,2048]{1,0:T(8,128)(2,1)}, u32[]{:S(2)}, u32[]{:S(2)}) collective-permute-start(bf16[256,2048]{1,0:T(8,128)(2,1)} %constant_dynamic-update-slice_fusion.refs_0_), channel_id=1, source_target_pairs={{0,14},{2,0},{4,2},{6,4},{8,6},{10,8},{12,10},{14,12},{1,15},{3,1}... | collective-permute-start | bytes 3145736 | tf_op jit(solution)/shard_map/ppermute | solution.py:268
  47.5 1.8 collective-permute-start.13
  49.3 5.1 %collective-permute-start.3 = (bf16[256,2048]{1,0:T(8,128)(2,1)}, bf16[256,2048]{1,0:T(8,128)(2,1)}, u32[]{:S(2)}, u32[]{:S(2)}) collective-permute-start(bf16[256,2048]{1,0:T(8,128)(2,1)} %constant_dynamic-update-slice_fusion.refs_0_), channel_id=1, source_target_pairs={{0,1},{1,0},{2,3},{3,2},{4,5},{5,4},{6,7},{7,6},{8,9},{9,8},{10,11... | collective-permute-start | bytes 3145736 | tf_op jit(solution)/shard_map/ppermute | solution.py:237
  54.4 2.2 %collective-permute-start.10 = (bf16[256,768]{1,0:T(8,128)(2,1)S(1)}, bf16[256,768]{1,0:T(8,128)(2,1)S(1)}, u32[]{:S(2)}, u32[]{:S(2)}) collective-permute-start(bf16[256,768]{1,0:T(8,128)(2,1)S(1)} %slice.16), channel_id=1, source_target_pairs={{0,48},{16,32},{32,16},{48,0},{1,49},{17,33},{33,17},{49,1},{2,50}... | collective-permute-start | bytes 1179656 | tf_op jit(solution)/shard_map/ppermute | solution.py:237
  56.6 0.1 collective-permute-start.11
  56.7 6.3 %collective-permute-done.11.refs_10_.refs_12_ = bf16[256,640]{1,0:T(8,128)(2,1)S(1)} collective-permute-done((bf16[256,640]{1,0:T(8,128)(2,1)S(1)}, bf16[256,640]{1,0:T(8,128)(2,1)S(1)}, u32[]{:S(2)}, u32[]{:S(2)}) %collective-permute-start.11) | collective-permute-done | bytes 327712 | tf_op jit(solution)/shard_map/ppermute | solution.py:237
  63.0 7.5 %collective-permute-done.12.refs_0_ = bf16[256,2048]{1,0:T(8,128)(2,1)} collective-permute-done((bf16[256,2048]{1,0:T(8,128)(2,1)}, bf16[256,2048]{1,0:T(8,128)(2,1)}, u32[]{:S(2)}, u32[]{:S(2)}) %collective-permute-start.12) | collective-permute-done | bytes 1048608 | tf_op jit(solution)/shard_map/ppermute | solution.py:268
  70.5 3.0 %collective-permute-done.13.refs_2_ = bf16[256,2048]{1,0:T(8,128)(2,1)} collective-permute-done((bf16[256,2048]{1,0:T(8,128)(2,1)}, bf16[256,2048]{1,0:T(8,128)(2,1)}, u32[]{:S(2)}, u32[]{:S(2)}) %collective-permute-start.13) | collective-permute-done | bytes 1048608 | tf_op jit(solution)/shard_map/ppermute | solution.py:267
  73.6 4.5 %collective-permute-start.14 = (bf16[256,2048]{1,0:T(8,128)(2,1)}, bf16[256,2048]{1,0:T(8,128)(2,1)}, u32[]{:S(2)}, u32[]{:S(2)}) collective-permute-start(bf16[256,2048]{1,0:T(8,128)(2,1)} %collective-permute-done.12.refs_0_), channel_id=1, source_target_pairs={{0,1},{1,0},{2,3},{3,2},{4,5},{5,4},{6,7},{7,6},{8,9},{9,8},{10,11... | collective-permute-start | bytes 3145736 | tf_op jit(solution)/shard_map/ppermute | solution.py:237
  78.1 0.1 collective-permute-start.15
  78.2 0.6 pad_add_fusion.1.place
  78.8 7.1 %shard_map.151 = bf16[4,128,1408]{2,1,0:T(8,128)(2,1)} custom-call(s32[4]{0:T(128)} %pad_add_fusion.1.place, bf16[256,2048]{1,0:T(8,128)(2,1)} %constant_dynamic-update-slice_fusion.refs_0_, bf16[256,2048]{1,0:T(8,128)(2,1)} %collective-permute-done.3.refs_1_, bf16[256,1408]{1,0:T(8,128)(2,1)} %copy-done.2, bf16[256,1408]{1,0:T(8,128)(2,1)} %copy-done.5, ...), custom_call_target="tpu_custom_call" | custom-call | flops 1048576 | bytes 65536 | tf_op jit(solution)/shard_map/pallas_call | solution.py:205
  85.9 3.9 %all-to-all-start = ((bf16[4,128,1408]{2,1,0:T(8,128)(2,1)}), bf16[4,128,1408]{2,1,0:T(8,128)(2,1)S(1)}, u32[]{:S(2)}, u32[]{:S(2)}) async-start(bf16[4,128,1408]{2,1,0:T(8,128)(2,1)} %shard_map.151), calls=%async_computation | async-start | bytes 2883584 | tf_op jit(solution)/shard_map/all_to_all | solution.py:241
  89.8 11.3 %shard_map.152 = bf16[4,256,1408]{2,1,0:T(8,128)(2,1)} custom-call(s32[4]{0:T(128)} %pad_add_fusion.1.place, bf16[256,2048]{1,0:T(8,128)(2,1)} %collective-permute-done.12.refs_0_, bf16[256,2048]{1,0:T(8,128)(2,1)} %collective-permute-done.14.refs_1_, bf16[256,2048]{1,0:T(8,128)(2,1)} %collective-permute-done.13.refs_2_, ...), custom_call_target="tpu_custom_call" | custom-call | flops 1048576 | bytes 65536 | tf_op jit(solution)/shard_map/pallas_call | solution.py:205
  101.1 1.3 collective-permute-start.16
  102.4 1.7 collective-permute-start.17
  104.1 4.3 %all-to-all-done.refs_1_ = bf16[4,128,1408]{2,1,0:T(8,128)(2,1)S(1)} async-done(((bf16[4,128,1408]{2,1,0:T(8,128)(2,1)}), bf16[4,128,1408]{2,1,0:T(8,128)(2,1)S(1)}, u32[]{:S(2)}, u32[]{:S(2)}) %all-to-all-start) | async-done | bytes 1441824 | tf_op jit(solution)/shard_map/all_to_all | solution.py:241
  108.5 4.6 %all-to-all-start.1 = ((bf16[4,256,1408]{2,1,0:T(8,128)(2,1)}), bf16[4,256,1408]{2,1,0:T(8,128)(2,1)}, u32[]{:S(2)}, u32[]{:S(2)}) async-start(bf16[4,256,1408]{2,1,0:T(8,128)(2,1)} %shard_map.152), calls=%async_computation.1 | async-start | bytes 5767168 | tf_op jit(solution)/shard_map/all_to_all | solution.py:241
  113.1 14.3 %collective-permute-done.16 = bf16[256,2048]{1,0:T(8,128)(2,1)S(1)} collective-permute-done((bf16[256,2048]{1,0:T(8,128)(2,1)}, bf16[256,2048]{1,0:T(8,128)(2,1)S(1)}, u32[]{:S(2)}, u32[]{:S(2)}) %collective-permute-start.16) | collective-permute-done | bytes 1048608 | tf_op jit(solution)/shard_map/ppermute | solution.py:283
  127.3 1.0 copy-done.11
  128.3 1.3 broadcast_select_fusion.refs_0_
  129.6 1.5 collective-permute-start.18
  131.2 2.4 %collective-permute-done.18.refs_1_ = bf16[256,2048]{1,0:T(8,128)(2,1)} collective-permute-done((bf16[256,2048]{1,0:T(8,128)(2,1)S(1)}, bf16[256,2048]{1,0:T(8,128)(2,1)}, u32[]{:S(2)}, u32[]{:S(2)}) %collective-permute-start.18) | collective-permute-done | bytes 1048608 | tf_op jit(solution)/shard_map/ppermute | solution.py:237
  133.6 7.1 %shard_map.153 = bf16[4,128,1408]{2,1,0:T(8,128)(2,1)} custom-call(s32[4]{0:T(128)} %pad_add_fusion.1.place, bf16[256,2048]{1,0:T(8,128)(2,1)} %copy-done.8, bf16[256,2048]{1,0:T(8,128)(2,1)} %collective-permute-done.18.refs_1_, bf16[256,1408]{1,0:T(8,128)(2,1)} %copy-done.2, bf16[256,1408]{1,0:T(8,128)(2,1)} %copy-done.5, bf16[256,1408]{1,0:T(8,128)(2,1)} %copy-done.6, ...), custom_call_target="tpu_custom_call" | custom-call | flops 1048576 | bytes 65536 | tf_op jit(solution)/shard_map/pallas_call | solution.py:205
  140.7 5.6 %all-to-all-done.1 = bf16[4,256,1408]{2,1,0:T(8,128)(2,1)} async-done(((bf16[4,256,1408]{2,1,0:T(8,128)(2,1)}), bf16[4,256,1408]{2,1,0:T(8,128)(2,1)}, u32[]{:S(2)}, u32[]{:S(2)}) %all-to-all-start.1) | async-done | bytes 2883616 | tf_op jit(solution)/shard_map/all_to_all | solution.py:241
  146.3 4.3 %all-to-all-start.2 = ((bf16[4,128,1408]{2,1,0:T(8,128)(2,1)}), bf16[4,128,1408]{2,1,0:T(8,128)(2,1)}, u32[]{:S(2)}, u32[]{:S(2)}) async-start(bf16[4,128,1408]{2,1,0:T(8,128)(2,1)} %shard_map.153), calls=%async_computation.2 | async-start | bytes 2883584 | tf_op jit(solution)/shard_map/all_to_all | solution.py:241
  150.8 2.6 %reduce_sum.12.refs_0_ = bf16[256,1408]{1,0:T(8,128)(2,1)S(1)} reduce(bf16[4,256,1408]{2,1,0:T(8,128)(2,1)} %all-to-all-done.1, bf16[]{:T(256)} %constant.61.clone.1), dimensions={0}, to_apply=%region_0.1 | reduce | flops 1081344 | bytes 3604482 | tf_op jit(solution)/shard_map/reduce_sum | solution.py:245
  153.4 3.3 %collective-permute-start.22 = (bf16[128,1408]{1,0:T(8,128)(2,1)S(1)}, bf16[128,1408]{1,0:T(8,128)(2,1)S(1)}, u32[]{:S(2)}, u32[]{:S(2)}) collective-permute-start(bf16[128,1408]{1,0:T(8,128)(2,1)S(1)} %slice_select_fusion), channel_id=1, source_target_pairs={{0,8},{6,14},{8,0},{14,6},{1,9},{7,15},{9,1},{15,7},{16,24},{22,30... | collective-permute-start | bytes 1081352 | tf_op jit(solution)/shard_map/ppermute | solution.py:297
  156.9 4.8 %shard_map.154 = (bf16[64,1024]{1,0:T(8,128)(2,1)S(1)}, bf16[64,1024]{1,0:T(8,128)(2,1)S(1)}, bf16[64,1024]{1,0:T(8,128)(2,1)S(1)}, bf16[64,1024]{1,0:T(8,128)(2,1)S(1)}, f32[4,16,64,128]{3,2,1,0:T(8,128)}) custom-call(s32[4]{0:T(128)S(1)} %copy-done.1, bf16[256,1408]{1,0:T(8,128)(2,1)S(1)} %reduce_sum.12.refs_0_, ...), custom_call_target="tpu_custom_call" | custom-call | flops 1048576 | bytes 65536 | tf_op jit(solution)/shard_map/pallas_call | solution.py:119
  161.7 1.3 collective-permute-start.19
  163.0 4.0 %collective-permute-start.20 = (bf16[64,1024]{1,0:T(8,128)(2,1)S(1)}, bf16[64,1024]{1,0:T(8,128)(2,1)S(1)}, u32[]{:S(2)}, u32[]{:S(2)}) collective-permute-start(bf16[64,1024]{1,0:T(8,128)(2,1)S(1)} %get-tuple-element.58), channel_id=1, source_target_pairs={{0,3},{1,2},{2,5},{3,4},{4,7},{5,6},{8,11},{9,10},{10,13},{11,12},... | collective-permute-start | bytes 393224 | tf_op jit(solution)/shard_map/ppermute | solution.py:306
  167.0 0.3 collective-permute-start.21
  167.3 3.0 %collective-permute-done.20.refs_3_ = bf16[64,1024]{1,0:T(8,128)(2,1)S(1)} collective-permute-done((bf16[64,1024]{1,0:T(8,128)(2,1)S(1)}, bf16[64,1024]{1,0:T(8,128)(2,1)S(1)}, u32[]{:S(2)}, u32[]{:S(2)}) %collective-permute-start.20) | collective-permute-done | bytes 131104 | tf_op jit(solution)/shard_map/ppermute | solution.py:306
  170.3 5.7 %shard_map.155 = (bf16[64,1024]{1,0:T(8,128)(2,1)S(1)}, bf16[64,1024]{1,0:T(8,128)(2,1)S(1)}, bf16[64,1024]{1,0:T(8,128)(2,1)S(1)}, bf16[64,1024]{1,0:T(8,128)(2...) custom-call(s32[4]{0:T(128)S(1)} %copy-done.1, ...), custom_call_target="tpu_custom_call", output_to_operand_aliasing={{6}: (8, {})} | custom-call | flops 1048576 | bytes 65536 | tf_op jit(solution)/shard_map/pallas_call | solution.py:119
  176.1 1.3 collective-permute-start.23
  177.4 1.3 collective-permute-start.24
  178.7 1.2 collective-permute-start.25
  179.9 2.5 %collective-permute-start.26 = (bf16[64,1024]{1,0:T(8,128)(2,1)S(1)}, bf16[64,1024]{1,0:T(8,128)(2,1)S(1)}, u32[]{:S(2)}, u32[]{:S(2)}) collective-permute-start(bf16[64,1024]{1,0:T(8,128)(2,1)S(1)} %get-tuple-element.70), channel_id=1, source_target_pairs={{0,5},{1,4},{2,7},{3,6},{4,1},{5,0},{6,3},{7,2},{8,13},{9,12},{10,... | collective-permute-start | bytes 393224 | tf_op jit(solution)/shard_map/ppermute | solution.py:306
  182.4 5.1 %collective-permute-start.27 = (bf16[64,1024]{1,0:T(8,128)(2,1)S(1)}, bf16[64,1024]{1,0:T(8,128)(2,1)S(1)}, u32[]{:S(2)}, u32[]{:S(2)}) collective-permute-start(bf16[64,1024]{1,0:T(8,128)(2,1)S(1)} %get-tuple-element.71), channel_id=1, source_target_pairs={{0,6},{1,7},{2,0},{3,1},{4,2},{5,3},{6,4},{7,5},{8,14},{9,15},{10,... | collective-permute-start | bytes 393224 | tf_op jit(solution)/shard_map/ppermute | solution.py:306
  187.5 0.2 collective-permute-start.28
  187.8 2.7 %collective-permute-done.24.refs_1_ = bf16[64,1024]{1,0:T(8,128)(2,1)S(1)} collective-permute-done((bf16[64,1024]{1,0:T(8,128)(2,1)S(1)}, bf16[64,1024]{1,0:T(8,128)(2,1)S(1)}, u32[]{:S(2)}, u32[]{:S(2)}) %collective-permute-start.24) | collective-permute-done | bytes 131104 | tf_op jit(solution)/shard_map/ppermute | solution.py:306
  190.4 9.0 %collective-permute-done.26.refs_7_ = bf16[64,1024]{1,0:T(8,128)(2,1)S(1)} collective-permute-done((bf16[64,1024]{1,0:T(8,128)(2,1)S(1)}, bf16[64,1024]{1,0:T(8,128)(2,1)S(1)}, u32[]{:S(2)}, u32[]{:S(2)}) %collective-permute-start.26) | collective-permute-done | bytes 131104 | tf_op jit(solution)/shard_map/ppermute | solution.py:306
  199.4 1.6 shard_map.156
  (75 shorter events, 0.7 us)
Async XLA Ops:
  0.6 2.2 %copy-start.20 = (s32[4]{0:T(128)S(1)}, s32[4]{0:T(128)}, u32[]{:S(2)}) copy-start(s32[4]{0:T(128)} %constant.63.clone) | copy-start | bytes 52
  0.6 2.4 %copy-start = (bf16[64,8192]{1,0:T(8,128)(2,1)S(1)}, bf16[64,8192]{1,0:T(8,128)(2,1)}, u32[]{:S(2)}) copy-start(bf16[64,8192]{1,0:T(8,128)(2,1)} %tokens) | copy-start | bytes 3145732
  2.7 29.3 %copy-start.2 = (bf16[256,1408]{1,0:T(8,128)(2,1)}, bf16[256,1408]{1,0:T(8,128)(2,1)S(1)}, u32[]{:S(2)}) copy-start(bf16[256,1408]{1,0:T(8,128)(2,1)S(1)} %fusion.1.refs_2_.refs_4_) | copy-start | bytes 2162692
  3.7 15.5 %collective-permute-start = (bf16[64,2048]{1,0:T(8,128)(2,1)S(1)}, bf16[64,2048]{1,0:T(8,128)(2,1)S(1)}, u32[]{:S(2)}, u32[]{:S(2)}) collective-permute-start(bf16[64,2048]{1,0:T(8,128)(2,1)S(1)} %get-tuple-element.40), channel_id=1, source_target_pairs={{0,64},{64,0},{128,192},{192,128},{1,65},{65,1},{129,193},{193,129... | collective-permute-start | bytes 786440 | tf_op jit(solution)/shard_map/ppermute | solution.py:237
  5.9 28.3 %collective-permute-start.4 = (bf16[256,1408]{1,0:T(8,128)(2,1)S(1)}, bf16[256,1408]{1,0:T(8,128)(2,1)S(1)}, u32[]{:S(2)}, u32[]{:S(2)}) collective-permute-start(bf16[256,1408]{1,0:T(8,128)(2,1)S(1)} %fusion.1.refs_2_.refs_4_), channel_id=1, source_target_pairs={{0,16},{16,0},{32,48},{48,32},{1,17},{17,1},{33,49},{49,33},{2,18}... | collective-permute-start | bytes 2162696 | tf_op jit(solution)/shard_map/ppermute | solution.py:237
  7.1 27.1 %collective-permute-start.5 = (bf16[256,1408]{1,0:T(8,128)(2,1)S(1)}, bf16[256,1408]{1,0:T(8,128)(2,1)S(1)}, u32[]{:S(2)}, u32[]{:S(2)}) collective-permute-start(bf16[256,1408]{1,0:T(8,128)(2,1)S(1)} %fusion.1.refs_2_.refs_4_), channel_id=1, source_target_pairs={{0,48},{16,32},{32,16},{48,0},{1,49},{17,33},{33,17},{49,1},{2,50}... | collective-permute-start | bytes 2162696 | tf_op jit(solution)/shard_map/ppermute | solution.py:237
  8.9 25.3 %collective-permute-start.7 = (bf16[256,1408]{1,0:T(8,128)(2,1)S(1)}, bf16[256,1408]{1,0:T(8,128)(2,1)}, u32[]{:S(2)}, u32[]{:S(2)}) collective-permute-start(bf16[256,1408]{1,0:T(8,128)(2,1)S(1)} %fusion.1.refs_2_.refs_4_), channel_id=1, source_target_pairs={{0,8},{8,0},{1,9},{9,1},{2,10},{10,2},{3,11},{11,3},{4,12},{12,4},... | collective-permute-start | bytes 2162696 | tf_op jit(solution)/shard_map/ppermute | solution.py:237
  15.9 7.6 %collective-permute-start.1 = (bf16[64,2048]{1,0:T(8,128)(2,1)S(1)}, bf16[64,2048]{1,0:T(8,128)(2,1)S(1)}, u32[]{:S(2)}, u32[]{:S(2)}) collective-permute-start(bf16[64,2048]{1,0:T(8,128)(2,1)S(1)} %get-tuple-element.41), channel_id=1, source_target_pairs={{0,128},{64,192},{128,0},{192,64},{1,129},{65,193},{129,1},{193,65... | collective-permute-start | bytes 786440 | tf_op jit(solution)/shard_map/ppermute | solution.py:237
  19.2 12.1 %collective-permute-start.2 = (bf16[64,2048]{1,0:T(8,128)(2,1)S(1)}, bf16[64,2048]{1,0:T(8,128)(2,1)S(1)}, u32[]{:S(2)}, u32[]{:S(2)}) collective-permute-start(bf16[64,2048]{1,0:T(8,128)(2,1)S(1)} %get-tuple-element.42), channel_id=1, source_target_pairs={{0,192},{64,128},{128,64},{192,0},{1,193},{65,129},{129,65},{193,1... | collective-permute-start | bytes 786440 | tf_op jit(solution)/shard_map/ppermute | solution.py:237
  23.5 16.4 %collective-permute-start.6 = (bf16[256,1408]{1,0:T(8,128)(2,1)S(1)}, bf16[256,1408]{1,0:T(8,128)(2,1)S(1)}, u32[]{:S(2)}, u32[]{:S(2)}) collective-permute-start(bf16[256,1408]{1,0:T(8,128)(2,1)S(1)} %fusion.1.refs_2_.refs_4_), channel_id=1, source_target_pairs={{0,32},{16,48},{32,0},{48,16},{1,33},{17,49},{33,1},{49,17},{2,34}... | collective-permute-start | bytes 2162696 | tf_op jit(solution)/shard_map/ppermute | solution.py:237
  34.2 44.5 %copy-start.5 = (bf16[256,1408]{1,0:T(8,128)(2,1)}, bf16[256,1408]{1,0:T(8,128)(2,1)S(1)}, u32[]{:S(2)}) copy-start(bf16[256,1408]{1,0:T(8,128)(2,1)S(1)} %collective-permute-done.4.refs_3_.refs_5_) | copy-start | bytes 2162692
  34.2 44.5 %copy-start.6 = (bf16[256,1408]{1,0:T(8,128)(2,1)}, bf16[256,1408]{1,0:T(8,128)(2,1)S(1)}, u32[]{:S(2)}) copy-start(bf16[256,1408]{1,0:T(8,128)(2,1)S(1)} %collective-permute-done.5.refs_4_.refs_6_) | copy-start | bytes 2162692
  39.9 0.9 copy-start.7
  40.8 13.6 %collective-permute-start.8 = (bf16[256,1408]{1,0:T(8,128)(2,1)}, bf16[256,1408]{1,0:T(8,128)(2,1)S(1)}, u32[]{:S(2)}, u32[]{:S(2)}) collective-permute-start(bf16[256,1408]{1,0:T(8,128)(2,1)} %shard_map.150.refs_6_.refs_8_), channel_id=1, source_target_pairs={{0,16},{16,0},{32,48},{48,32},{1,17},{17,1},{33,49},{49,33},{2,18}... | collective-permute-start | bytes 2162696 | tf_op jit(solution)/shard_map/ppermute | solution.py:237
  41.1 15.5 %collective-permute-start.9 = (bf16[256,1408]{1,0:T(8,128)(2,1)}, bf16[256,1408]{1,0:T(8,128)(2,1)S(1)}, u32[]{:S(2)}, u32[]{:S(2)}) collective-permute-start(bf16[256,1408]{1,0:T(8,128)(2,1)} %shard_map.150.refs_6_.refs_8_), channel_id=1, source_target_pairs={{0,48},{16,32},{32,16},{48,0},{1,49},{17,33},{33,17},{49,1},{2,50}... | collective-permute-start | bytes 2162696 | tf_op jit(solution)/shard_map/ppermute | solution.py:237
  42.3 28.3 %collective-permute-start.12 = (bf16[256,2048]{1,0:T(8,128)(2,1)}, bf16[256,2048]{1,0:T(8,128)(2,1)}, u32[]{:S(2)}, u32[]{:S(2)}) collective-permute-start(bf16[256,2048]{1,0:T(8,128)(2,1)} %constant_dynamic-update-slice_fusion.refs_0_), channel_id=1, source_target_pairs={{0,14},{2,0},{4,2},{6,4},{8,6},{10,8},{12,10},{14,12},{1,15},{3,1}... | collective-permute-start | bytes 3145736 | tf_op jit(solution)/shard_map/ppermute | solution.py:268
  47.5 26.1 %collective-permute-start.13 = (bf16[256,2048]{1,0:T(8,128)(2,1)}, bf16[256,2048]{1,0:T(8,128)(2,1)}, u32[]{:S(2)}, u32[]{:S(2)}) collective-permute-start(bf16[256,2048]{1,0:T(8,128)(2,1)} %constant_dynamic-update-slice_fusion.refs_0_), channel_id=1, source_target_pairs={{0,2},{2,4},{4,6},{6,8},{8,10},{10,12},{12,14},{14,0},{1,3},{3,5},... | collective-permute-start | bytes 3145736 | tf_op jit(solution)/shard_map/ppermute | solution.py:267
  49.3 29.5 %collective-permute-start.3 = (bf16[256,2048]{1,0:T(8,128)(2,1)}, bf16[256,2048]{1,0:T(8,128)(2,1)}, u32[]{:S(2)}, u32[]{:S(2)}) collective-permute-start(bf16[256,2048]{1,0:T(8,128)(2,1)} %constant_dynamic-update-slice_fusion.refs_0_), channel_id=1, source_target_pairs={{0,1},{1,0},{2,3},{3,2},{4,5},{5,4},{6,7},{7,6},{8,9},{9,8},{10,11... | collective-permute-start | bytes 3145736 | tf_op jit(solution)/shard_map/ppermute | solution.py:237
  54.4 24.4 %copy-start.3 = (bf16[256,1408]{1,0:T(8,128)(2,1)}, bf16[256,1408]{1,0:T(8,128)(2,1)S(1)}, u32[]{:S(2)}) copy-start(bf16[256,1408]{1,0:T(8,128)(2,1)S(1)} %collective-permute-done.8.refs_7_.refs_9_) | copy-start | bytes 2162692
  54.4 19.2 %collective-permute-start.10 = (bf16[256,768]{1,0:T(8,128)(2,1)S(1)}, bf16[256,768]{1,0:T(8,128)(2,1)S(1)}, u32[]{:S(2)}, u32[]{:S(2)}) collective-permute-start(bf16[256,768]{1,0:T(8,128)(2,1)S(1)} %slice.16), channel_id=1, source_target_pairs={{0,48},{16,32},{32,16},{48,0},{1,49},{17,33},{33,17},{49,1},{2,50}... | collective-permute-start | bytes 1179656 | tf_op jit(solution)/shard_map/ppermute | solution.py:237
  56.6 22.2 %copy-start.4 = (bf16[256,1408]{1,0:T(8,128)(2,1)}, bf16[256,1408]{1,0:T(8,128)(2,1)S(1)}, u32[]{:S(2)}) copy-start(bf16[256,1408]{1,0:T(8,128)(2,1)S(1)} %collective-permute-done.9.refs_8_.refs_10_) | copy-start | bytes 2162692
  56.6 6.4 %collective-permute-start.11 = (bf16[256,640]{1,0:T(8,128)(2,1)S(1)}, bf16[256,640]{1,0:T(8,128)(2,1)S(1)}, u32[]{:S(2)}, u32[]{:S(2)}) collective-permute-start(bf16[256,640]{1,0:T(8,128)(2,1)S(1)} %slice.17), channel_id=1, source_target_pairs={{0,16},{16,0},{32,48},{48,32},{1,17},{17,1},{33,49},{49,33},{2,18}... | collective-permute-start | bytes 983048 | tf_op jit(solution)/shard_map/ppermute | solution.py:237
  63.0 10.5 %copy-start.10 = (bf16[256,640]{1,0:T(8,128)(2,1)}, bf16[256,640]{1,0:T(8,128)(2,1)S(1)}, u32[]{:S(2)}) copy-start(bf16[256,640]{1,0:T(8,128)(2,1)S(1)} %collective-permute-done.11.refs_10_.refs_12_) | copy-start | bytes 983044
  73.6 5.2 %copy-start.9 = (bf16[256,768]{1,0:T(8,128)(2,1)}, bf16[256,768]{1,0:T(8,128)(2,1)S(1)}, u32[]{:S(2)}) copy-start(bf16[256,768]{1,0:T(8,128)(2,1)S(1)} %collective-permute-done.10.refs_9_.refs_11_) | copy-start | bytes 1179652
  73.6 16.2 %collective-permute-start.14 = (bf16[256,2048]{1,0:T(8,128)(2,1)}, bf16[256,2048]{1,0:T(8,128)(2,1)}, u32[]{:S(2)}, u32[]{:S(2)}) collective-permute-start(bf16[256,2048]{1,0:T(8,128)(2,1)} %collective-permute-done.12.refs_0_), channel_id=1, source_target_pairs={{0,1},{1,0},{2,3},{3,2},{4,5},{5,4},{6,7},{7,6},{8,9},{9,8},{10,11... | collective-permute-start | bytes 3145736 | tf_op jit(solution)/shard_map/ppermute | solution.py:237
  78.1 11.7 %collective-permute-start.15 = (bf16[256,2048]{1,0:T(8,128)(2,1)}, bf16[256,2048]{1,0:T(8,128)(2,1)}, u32[]{:S(2)}, u32[]{:S(2)}) collective-permute-start(bf16[256,2048]{1,0:T(8,128)(2,1)} %collective-permute-done.13.refs_2_), channel_id=1, source_target_pairs={{0,1},{1,0},{2,3},{3,2},{4,5},{5,4},{6,7},{7,6},{8,9},{9,8},{10,11... | collective-permute-start | bytes 3145736 | tf_op jit(solution)/shard_map/ppermute | solution.py:237
  85.9 22.6 %all-to-all-start = ((bf16[4,128,1408]{2,1,0:T(8,128)(2,1)}), bf16[4,128,1408]{2,1,0:T(8,128)(2,1)S(1)}, u32[]{:S(2)}, u32[]{:S(2)}) async-start(bf16[4,128,1408]{2,1,0:T(8,128)(2,1)} %shard_map.151), calls=%async_computation | async-start | bytes 2883584 | tf_op jit(solution)/shard_map/all_to_all | solution.py:241
  101.1 26.2 %collective-permute-start.16 = (bf16[256,2048]{1,0:T(8,128)(2,1)}, bf16[256,2048]{1,0:T(8,128)(2,1)S(1)}, u32[]{:S(2)}, u32[]{:S(2)}) collective-permute-start(bf16[256,2048]{1,0:T(8,128)(2,1)} %collective-permute-done.12.refs_0_), channel_id=1, source_target_pairs={{2,0},{4,2},{10,8},{12,10},{3,1},{5,3},{11,9},{13,11},{18,16},{20,... | collective-permute-start | bytes 3145736 | tf_op jit(solution)/shard_map/ppermute | solution.py:283
  102.4 25.9 %collective-permute-start.17 = (bf16[256,2048]{1,0:T(8,128)(2,1)}, bf16[256,2048]{1,0:T(8,128)(2,1)}, u32[]{:S(2)}, u32[]{:S(2)}) collective-permute-start(bf16[256,2048]{1,0:T(8,128)(2,1)} %collective-permute-done.13.refs_2_), channel_id=1, source_target_pairs={{2,4},{4,6},{10,12},{12,14},{3,5},{5,7},{11,13},{13,15},{18,20},{2... | collective-permute-start | bytes 3145736 | tf_op jit(solution)/shard_map/ppermute | solution.py:282
  108.5 37.9 %all-to-all-start.1 = ((bf16[4,256,1408]{2,1,0:T(8,128)(2,1)}), bf16[4,256,1408]{2,1,0:T(8,128)(2,1)}, u32[]{:S(2)}, u32[]{:S(2)}) async-start(bf16[4,256,1408]{2,1,0:T(8,128)(2,1)} %shard_map.152), calls=%async_computation.1 | async-start | bytes 5767168 | tf_op jit(solution)/shard_map/all_to_all | solution.py:241
  127.3 1.0 copy-start.11
  129.6 4.0 %copy-start.8 = (bf16[256,2048]{1,0:T(8,128)(2,1)}, bf16[256,2048]{1,0:T(8,128)(2,1)S(1)}, u32[]{:S(2)}) copy-start(bf16[256,2048]{1,0:T(8,128)(2,1)S(1)} %broadcast_select_fusion.refs_0_) | copy-start | bytes 3145732
  129.6 4.0 %collective-permute-start.18 = (bf16[256,2048]{1,0:T(8,128)(2,1)S(1)}, bf16[256,2048]{1,0:T(8,128)(2,1)}, u32[]{:S(2)}, u32[]{:S(2)}) collective-permute-start(bf16[256,2048]{1,0:T(8,128)(2,1)S(1)} %broadcast_select_fusion.refs_0_), channel_id=1, source_target_pairs={{0,1},{1,0},{2,3},{3,2},{4,5},{5,4},{6,7},{7,6},{8,9},{9,8},{10,11... | collective-permute-start | bytes 3145736 | tf_op jit(solution)/shard_map/ppermute | solution.py:237
  140.7 9.9 %copy-start.12 = (f32[4,1024]{1,0:T(4,128)S(1)}, f32[4,1024]{1,0:T(4,128)}, u32[]{:S(2)}) copy-start(f32[4,1024]{1,0:T(4,128)} %param.19) | copy-start | bytes 49156
  146.3 24.0 %all-to-all-start.2 = ((bf16[4,128,1408]{2,1,0:T(8,128)(2,1)}), bf16[4,128,1408]{2,1,0:T(8,128)(2,1)}, u32[]{:S(2)}, u32[]{:S(2)}) async-start(bf16[4,128,1408]{2,1,0:T(8,128)(2,1)} %shard_map.153), calls=%async_computation.2 | async-start | bytes 2883584 | tf_op jit(solution)/shard_map/all_to_all | solution.py:241
  150.7 6.0 %copy-start.18 = (f32[16]{0:T(128)S(1)}, f32[16]{0:T(128)}, u32[]{:S(2)}) copy-start(f32[16]{0:T(128)} %param.23) | copy-start | bytes 196
  150.7 6.0 %copy-start.19 = (f32[16]{0:T(128)S(1)}, f32[16]{0:T(128)}, u32[]{:S(2)}) copy-start(f32[16]{0:T(128)} %param.22) | copy-start | bytes 196
  150.7 6.0 %copy-start.15 = (f32[16]{0:T(128)S(1)}, f32[16]{0:T(128)}, u32[]{:S(2)}) copy-start(f32[16]{0:T(128)} %param.24) | copy-start | bytes 196
  150.7 6.2 %copy-start.13 = (f32[4,128]{1,0:T(4,128)S(1)}, f32[4,128]{1,0:T(4,128)}, u32[]{:S(2)}) copy-start(f32[4,128]{1,0:T(4,128)} %param.20) | copy-start | bytes 6148
  150.7 6.2 %copy-start.14 = (f32[4,128]{1,0:T(4,128)S(1)}, f32[4,128]{1,0:T(4,128)}, u32[]{:S(2)}) copy-start(f32[4,128]{1,0:T(4,128)} %param.21) | copy-start | bytes 6148
  150.7 6.2 %copy-start.1 = (s32[4]{0:T(128)S(1)}, s32[4]{0:T(128)}, u32[]{:S(2)}) copy-start(s32[4]{0:T(128)} %pad_add_fusion.1.place) | copy-start | bytes 52
  153.4 16.9 %collective-permute-start.22 = (bf16[128,1408]{1,0:T(8,128)(2,1)S(1)}, bf16[128,1408]{1,0:T(8,128)(2,1)S(1)}, u32[]{:S(2)}, u32[]{:S(2)}) collective-permute-start(bf16[128,1408]{1,0:T(8,128)(2,1)S(1)} %slice_select_fusion), channel_id=1, source_target_pairs={{0,8},{6,14},{8,0},{14,6},{1,9},{7,15},{9,1},{15,7},{16,24},{22,30... | collective-permute-start | bytes 1081352 | tf_op jit(solution)/shard_map/ppermute | solution.py:297
  161.7 5.6 %collective-permute-start.19 = (bf16[64,1024]{1,0:T(8,128)(2,1)S(1)}, bf16[64,1024]{1,0:T(8,128)(2,1)S(1)}, u32[]{:S(2)}, u32[]{:S(2)}) collective-permute-start(bf16[64,1024]{1,0:T(8,128)(2,1)S(1)} %get-tuple-element.57), channel_id=1, source_target_pairs={{0,2},{1,3},{2,4},{3,5},{4,6},{5,7},{8,10},{9,11},{10,12},{11,13},... | collective-permute-start | bytes 393224 | tf_op jit(solution)/shard_map/ppermute | solution.py:306
  163.0 7.3 %collective-permute-start.20 = (bf16[64,1024]{1,0:T(8,128)(2,1)S(1)}, bf16[64,1024]{1,0:T(8,128)(2,1)S(1)}, u32[]{:S(2)}, u32[]{:S(2)}) collective-permute-start(bf16[64,1024]{1,0:T(8,128)(2,1)S(1)} %get-tuple-element.58), channel_id=1, source_target_pairs={{0,3},{1,2},{2,5},{3,4},{4,7},{5,6},{8,11},{9,10},{10,13},{11,12},... | collective-permute-start | bytes 393224 | tf_op jit(solution)/shard_map/ppermute | solution.py:306
  167.0 3.3 %collective-permute-start.21 = (bf16[64,1024]{1,0:T(8,128)(2,1)S(1)}, bf16[64,1024]{1,0:T(8,128)(2,1)S(1)}, u32[]{:S(2)}, u32[]{:S(2)}) collective-permute-start(bf16[64,1024]{1,0:T(8,128)(2,1)S(1)} %get-tuple-element.60), channel_id=1, source_target_pairs={{0,1},{1,0},{2,3},{3,2},{4,5},{5,4},{6,7},{7,6},{8,9},{9,8},{10,11... | collective-permute-start | bytes 393224 | tf_op jit(solution)/shard_map/ppermute | solution.py:306
  170.3 17.4 %copy-start.16 = (s32[8]{0:T(128)S(1)}, s32[8]{0:T(128)}, u32[]{:S(2)}) copy-start(s32[8]{0:T(128)} %constant.64.clone) | copy-start | bytes 100
  170.3 17.4 %copy-start.17 = (s32[8]{0:T(128)S(1)}, s32[8]{0:T(128)}, u32[]{:S(2)}) copy-start(s32[8]{0:T(128)} %constant.65.clone) | copy-start | bytes 100
  176.1 11.5 %collective-permute-start.23 = (bf16[64,1024]{1,0:T(8,128)(2,1)S(1)}, bf16[64,1024]{1,0:T(8,128)(2,1)S(1)}, u32[]{:S(2)}, u32[]{:S(2)}) collective-permute-start(bf16[64,1024]{1,0:T(8,128)(2,1)S(1)} %get-tuple-element.63), channel_id=1, source_target_pairs={{6,0},{7,1},{14,8},{15,9},{22,16},{23,17},{30,24},{31,25},{38,32},... | collective-permute-start | bytes 393224 | tf_op jit(solution)/shard_map/ppermute | solution.py:306
  177.4 13.1 %collective-permute-start.24 = (bf16[64,1024]{1,0:T(8,128)(2,1)S(1)}, bf16[64,1024]{1,0:T(8,128)(2,1)S(1)}, u32[]{:S(2)}, u32[]{:S(2)}) collective-permute-start(bf16[64,1024]{1,0:T(8,128)(2,1)S(1)} %get-tuple-element.64), channel_id=1, source_target_pairs={{6,1},{7,0},{14,9},{15,8},{22,17},{23,16},{30,25},{31,24},{38,33},... | collective-permute-start | bytes 393224 | tf_op jit(solution)/shard_map/ppermute | solution.py:306
  178.7 11.8 %collective-permute-start.25 = (bf16[64,1024]{1,0:T(8,128)(2,1)S(1)}, bf16[64,1024]{1,0:T(8,128)(2,1)S(1)}, u32[]{:S(2)}, u32[]{:S(2)}) collective-permute-start(bf16[64,1024]{1,0:T(8,128)(2,1)S(1)} %get-tuple-element.69), channel_id=1, source_target_pairs={{0,4},{1,5},{2,6},{3,7},{4,0},{5,1},{6,2},{7,3},{8,12},{9,13},{10,... | collective-permute-start | bytes 393224 | tf_op jit(solution)/shard_map/ppermute | solution.py:306
  179.9 19.5 %collective-permute-start.26 = (bf16[64,1024]{1,0:T(8,128)(2,1)S(1)}, bf16[64,1024]{1,0:T(8,128)(2,1)S(1)}, u32[]{:S(2)}, u32[]{:S(2)}) collective-permute-start(bf16[64,1024]{1,0:T(8,128)(2,1)S(1)} %get-tuple-element.70), channel_id=1, source_target_pairs={{0,5},{1,4},{2,7},{3,6},{4,1},{5,0},{6,3},{7,2},{8,13},{9,12},{10,... | collective-permute-start | bytes 393224 | tf_op jit(solution)/shard_map/ppermute | solution.py:306
  182.4 17.0 %collective-permute-start.27 = (bf16[64,1024]{1,0:T(8,128)(2,1)S(1)}, bf16[64,1024]{1,0:T(8,128)(2,1)S(1)}, u32[]{:S(2)}, u32[]{:S(2)}) collective-permute-start(bf16[64,1024]{1,0:T(8,128)(2,1)S(1)} %get-tuple-element.71), channel_id=1, source_target_pairs={{0,6},{1,7},{2,0},{3,1},{4,2},{5,3},{6,4},{7,5},{8,14},{9,15},{10,... | collective-permute-start | bytes 393224 | tf_op jit(solution)/shard_map/ppermute | solution.py:306
  187.5 11.9 %collective-permute-start.28 = (bf16[64,1024]{1,0:T(8,128)(2,1)S(1)}, bf16[64,1024]{1,0:T(8,128)(2,1)S(1)}, u32[]{:S(2)}, u32[]{:S(2)}) collective-permute-start(bf16[64,1024]{1,0:T(8,128)(2,1)S(1)} %get-tuple-element.72), channel_id=1, source_target_pairs={{0,7},{1,6},{2,1},{3,0},{4,3},{5,2},{6,5},{7,4},{8,15},{9,14},{10,... | collective-permute-start | bytes 393224 | tf_op jit(solution)/shard_map/ppermute | solution.py:306

commit v4 on v3

--- a/solution.py
+++ b/solution.py
@@ -67,7 +67,7 @@
     core, zl = place[0], place[1]
     sums, came, *refs = refs
     if late:
-        swapped, *refs = refs
+        came, (swapped, *refs) = [came, *refs[:3]], refs[3:]
         refs = refs[:4] + refs[5:]
     params, (*pieces, states, scratch, sems) = refs[:4], refs[4:]
 
@@ -78,7 +78,8 @@
         return value[112:128]
 
     ahead, behind = (sums[k : k + 128].astype(jnp.float32) for k in (0, 128))
-    total = jnp.sum(whole(came), axis=0).astype(jnp.bfloat16).astype(jnp.float32)
+    total = sum(came[d][...].astype(jnp.float32) for d in range(4))
+    total = total.astype(jnp.bfloat16).astype(jnp.float32)
     always = zl >= 0
     if late:
         first = whole(swapped)
@@ -176,9 +177,9 @@
 TILE = 768
 
 
-def project_kernel(pairs, place, *refs):
+def project_kernel(pairs, together, place, *refs):
     chunks, refs = refs[: 2 * pairs], refs[2 * pairs :]
-    near, far, out = refs[:4], refs[4:9], refs[9]
+    near, far, outs = refs[:4], refs[4:9], refs[9:]
     core, zh, y = place[0], place[2], place[3]
     mine = jnp.concatenate([ref[...] for ref in near], axis=0)
     across = jnp.where(pl.program_id(0) == 0, far[3][...], far[4][...])
@@ -193,22 +194,33 @@
             rows = pl.ds(pl.multiple_of(p * 128 + at * 64, 64), 64)
             for d in range(4):
                 low = half + 64 * d
-                out[y ^ d, rows, :] = partial[low : low + 64].astype(jnp.bfloat16)
-
-
-def project(place, chunks, panels):
+                if together:
+                    outs[0][y ^ d, rows, :] = partial[low : low + 64].astype(jnp.bfloat16)
+                else:
+                    outs[d][rows, :] = partial[low : low + 64].astype(outs[d].dtype)
+
+
+def project(place, chunks, panels, together):
     pairs = len(chunks) // 2
     width = panels[0].shape[1]
     whole = pl.BlockSpec((256, 2048), lambda j: (0, 0))
     column = pl.BlockSpec((256, TILE), lambda j: (0, j))
     single = pl.BlockSpec((256, TILE), lambda j: (0, 0))
-    return pl.pallas_call(
-        functools.partial(project_kernel, pairs),
+    shape = (128 * pairs, width)
+    if together:
+        out_shape = jax.ShapeDtypeStruct((4, *shape), jnp.bfloat16)
+        out_specs = pl.BlockSpec((4, 128 * pairs, TILE), lambda j: (0, 0, j))
+    else:
+        out_shape = [jax.ShapeDtypeStruct(shape, jnp.float32)]
+        out_shape += [jax.ShapeDtypeStruct(shape, jnp.bfloat16)] * 3
+        out_specs = [pl.BlockSpec((128 * pairs, TILE), lambda j: (0, j))] * 4
+    return pl.pallas_call(
+        functools.partial(project_kernel, pairs, together),
         grid=(2,),
-        out_shape=jax.ShapeDtypeStruct((4, 128 * pairs, width), jnp.bfloat16),
+        out_shape=out_shape,
         in_specs=[pl.BlockSpec(memory_space=pltpu.SMEM)]
         + [whole] * len(chunks) + [column] * 7 + [single] * 2,
-        out_specs=pl.BlockSpec((4, 128 * pairs, TILE), lambda j: (0, 0, j)),
+        out_specs=out_specs,
         compiler_params=pltpu.CompilerParams(vmem_limit_bytes=60 << 20),
         cost_estimate=pl.CostEstimate(flops=1 << 20, bytes_accessed=1 << 16, transcendentals=0),
     )(place, *chunks, *panels)
@@ -238,6 +250,10 @@
 
 
 def exchange(parts):
+    return [parts[0]] + [swap(parts[d], "y", d) for d in (1, 2, 3)]
+
+
+def exchange_all(parts):
     return lax.all_to_all(parts, "y", split_axis=0, concat_axis=0, tiled=True)
 
 
@@ -273,17 +289,17 @@
     place = jnp.stack([core, zl, zh, y]).astype(jnp.int32)
     left1, right1 = after((left1, right1), panels)
     sides = [left1, swap(left1, "c", 1), right1, swap(right1, "c", 1)]
-    parts = project(place, [own, own_other], panels)
-    came_own = exchange(parts)
-    parts = project(place, after(sides, parts), panels)
-    came_sides = exchange(parts)
+    parts = project(place, [own, own_other], panels, True)
+    came_own = exchange_all(parts)
+    parts = project(place, after(sides, parts), panels, True)
+    came_sides = exchange_all(parts)
 
     left1, right1 = after((left1, right1), parts)
     right2 = lax.ppermute(right1, line, [(1, 2), (2, 3), (5, 6), (6, 7)])
     left2 = lax.ppermute(left1, line, [(1, 0), (2, 1), (5, 4), (6, 5)])
     second = jnp.where(zl < 2, left2, right2)
     pair = after([second, swap(second, "c", 1)], parts)
-    parts = project(place, pair, panels)
+    parts = project(place, pair, panels, False)
     came_own, came_sides = after((came_own, came_sides), parts)
     came_second = exchange(parts)
 
@@ -305,12 +321,13 @@
         ]
         return lax.ppermute(piece, ("zl", "c"), pairs)
 
-    pieces = [to(early[2], 1, 0, range(3)), to(early[3], 1, 1, range(3))]
-    pieces += [early[0], to(early[1], 0, 1)]
-    came_second, pieces = after((came_second, pieces))
-    *last, states = scan(place, [sums, came_second, swapped], params, states)
-    pieces += [to(last[2], 2, 0), to(last[3], 2, 1), to(last[4], 3, 0), to(last[5], 3, 1)]
-    pieces = [to(last[0], 1, 0, [3]), to(last[1], 1, 1, [3])] + pieces
+    *last, states = scan(place, [sums, *came_second, swapped], params, states)
+    beyond = [to(last[2], 2, 0), to(last[3], 2, 1)]
+    wrapped = [to(last[0], 1, 0, [3]), to(last[1], 1, 1, [3])]
+    behind = [to(last[4], 3, 0), to(last[5], 3, 1)]
+    early = after(early, beyond[0])
+    ahead = [to(early[2], 1, 0, range(3)), to(early[3], 1, 1, range(3))]
+    pieces = wrapped + ahead + [early[0], to(early[1], 0, 1)] + beyond + behind
     origin = zl + jnp.asarray([3, 3, 0, 0, 2, 2, 1, 1])
     columns = (origin % 4) * 2 + (core + jnp.asarray([0, 1] * 4)) % 2
     columns = jnp.concatenate([columns, zl[None]]).astype(jnp.int32)

time: 205 us -> 198 us (0.966); the launches traced: 201 us -> 196 us
  waiting for transfers between devices: 75.7 us -> 63 us
  starting transfers between devices: 73.9 us -> 82.4 us
    ppermute x9, waiting for transfers between devices: 14.7 us -> 1 us  [to(): return lax.ppermute(piece, ('zl', 'c'), pairs)]
    ppermute x9, starting transfers between devices: 17.1 us -> 25.7 us  [to(): return lax.ppermute(piece, ('zl', 'c'), pairs)]
    all_to_all x3 -> x2, starting transfers between devices: 12.8 us -> 8.46 us  [exchange_all(): return lax.all_to_all(parts, 'y', split_axis=0, concat_axis=0, tiled=True)]
    ppermute x15 -> x18, starting transfers between devices: 30.7 us -> 34.7 us  [swap(): return lax.ppermute(value, axis, [(i, i ^ distance) for i in range(size)])]
    ppermute x15 -> x18, waiting for transfers between devices: 26.3 us -> 29.8 us  [swap(): return lax.ppermute(value, axis, [(i, i ^ distance) for i in range(size)])]
    all_to_all x3 -> x2, waiting for transfers between devices: 9.92 us -> 7.13 us  [exchange_all(): return lax.all_to_all(parts, 'y', split_axis=0, concat_axis=0, tiled=True)]
    unnamed x48 -> x50, local copies, waits for them, and re-layouts: 5.03 us -> 5 us
  transfers between devices with their start and end apart: 32 -> 34, of which waited for: 14 -> 14; matrix products, arithmetic and copies ran while one was open for 4% -> 4% of each run, Pallas kernels for 15% -> 16%
where the time goes in v4:
time: 198 us; the launch traced here: 196 us
  starting transfers between devices  82.4 us (42%)
  waiting for transfers between devices  63 us (32%)
  Pallas kernels  38.3 us (19%)
  local copies, waits for them, and re-layouts  6.03 us (3%)
  other arithmetic  5.58 us (3%)
    ppermute x18, starting transfers between devices, swap(): return lax.ppermute(value, axis, [(i, i ^ distance) for i in range(size)])  34.7 us
    ppermute x18, waiting for transfers between devices, swap(): return lax.ppermute(value, axis, [(i, i ^ distance) for i in range(size)])  29.8 us
    ppermute x9, starting transfers between devices, to(): return lax.ppermute(piece, ('zl', 'c'), pairs)  25.7 us
    pallas_call x3, Pallas kernels, project(): pl.pallas_call(functools.partial(project_kernel, pairs, together), grid=(...  25.6 us
    ppermute x1, waiting for transfers between devices, per_device(): left2 = lax.ppermute(left1, line, [(1, 0), (2, 1), (5, 4), (6, 5)])  14.2 us
    pallas_call x2, Pallas kernels, scan(): pl.pallas_call(functools.partial(scan_kernel, late), out_shape=[jax.Shape...  10.4 us
    all_to_all x2, starting transfers between devices, exchange_all(): return lax.all_to_all(parts, 'y', split_axis=0, concat_axis=0, tiled=True)  8.46 us
    ppermute x1, waiting for transfers between devices, per_device(): left1 = lax.ppermute(own_sent, line, [(i, (i - 1) % 8) for i in range(8)])  7.52 us
  transfers between devices with their start and end apart: 34, of which 14 were waited for; matrix products, arithmetic and copies ran while one was open for 4% of the time, Pallas kernels for 16%

profile of v4, /device:TPU:1, one launch (start us, length us, event | category | flops | bytes accessed | tf_op | source)
XLA Modules:
  0.0 196.3 jit_solution(16985121265622942373)
XLA Ops:
  0.7 0.9 copy.18
  1.6 1.2 fusion.1.refs_2_.refs_4_
  3.0 0.7 shard_map.149
  3.7 2.2 %collective-permute-start = (bf16[64,2048]{1,0:T(8,128)(2,1)S(1)}, bf16[64,2048]{1,0:T(8,128)(2,1)S(1)}, u32[]{:S(2)}, u32[]{:S(2)}) collective-permute-start(bf16[64,2048]{1,0:T(8,128)(2,1)S(1)} %get-tuple-element.43), channel_id=1, source_target_pairs={{0,64},{64,0},{128,192},{192,128},{1,65},{65,1},{129,193},{193,129... | collective-permute-start | bytes 786440 | tf_op jit(solution)/shard_map/ppermute | solution.py:249
  5.9 1.2 collective-permute-start.4
  7.1 1.8 collective-permute-start.5
  8.9 6.9 %collective-permute-start.7 = (bf16[256,1408]{1,0:T(8,128)(2,1)S(1)}, bf16[256,1408]{1,0:T(8,128)(2,1)}, u32[]{:S(2)}, u32[]{:S(2)}) collective-permute-start(bf16[256,1408]{1,0:T(8,128)(2,1)S(1)} %fusion.1.refs_2_.refs_4_), channel_id=1, source_target_pairs={{0,8},{8,0},{1,9},{9,1},{2,10},{10,2},{3,11},{11,3},{4,12},{12,4},... | collective-permute-start | bytes 2162696 | tf_op jit(solution)/shard_map/ppermute | solution.py:249
  15.9 2.6 %collective-permute-start.1 = (bf16[64,2048]{1,0:T(8,128)(2,1)S(1)}, bf16[64,2048]{1,0:T(8,128)(2,1)S(1)}, u32[]{:S(2)}, u32[]{:S(2)}) collective-permute-start(bf16[64,2048]{1,0:T(8,128)(2,1)S(1)} %get-tuple-element.44), channel_id=1, source_target_pairs={{0,128},{64,192},{128,0},{192,64},{1,129},{65,193},{129,1},{193,65... | collective-permute-start | bytes 786440 | tf_op jit(solution)/shard_map/ppermute | solution.py:249
  18.5 0.7 constant_dynamic-update-slice_fusion.3
  19.2 0.7 constant_dynamic-update-slice_fusion.2
  19.9 3.5 %collective-permute-done.1 = bf16[64,2048]{1,0:T(8,128)(2,1)S(1)} collective-permute-done((bf16[64,2048]{1,0:T(8,128)(2,1)S(1)}, bf16[64,2048]{1,0:T(8,128)(2,1)S(1)}, u32[]{:S(2)}, u32[]{:S(2)}) %collective-permute-start.1) | collective-permute-done | bytes 262176 | tf_op jit(solution)/shard_map/ppermute | solution.py:249
  23.5 0.9 collective-permute-start.6
  24.4 0.7 constant_dynamic-update-slice_fusion.1
  25.1 6.2 %collective-permute-done.2 = bf16[64,2048]{1,0:T(8,128)(2,1)S(1)} collective-permute-done((bf16[64,2048]{1,0:T(8,128)(2,1)S(1)}, bf16[64,2048]{1,0:T(8,128)(2,1)S(1)}, u32[]{:S(2)}, u32[]{:S(2)}) %collective-permute-start.2) | collective-permute-done | bytes 262176 | tf_op jit(solution)/shard_map/ppermute | solution.py:249
  31.3 0.7 constant_dynamic-update-slice_fusion.refs_0_
  32.0 2.2 %collective-permute-done.7.given = bf16[256,1408]{1,0:T(8,128)(2,1)} collective-permute-done((bf16[256,1408]{1,0:T(8,128)(2,1)S(1)}, bf16[256,1408]{1,0:T(8,128)(2,1)}, u32[]{:S(2)}, u32[]{:S(2)}) %collective-permute-start.7) | collective-permute-done | bytes 720928 | tf_op jit(solution)/shard_map/ppermute | solution.py:249
  34.2 5.6 %collective-permute-done.6.refs_5_.refs_7_ = bf16[256,1408]{1,0:T(8,128)(2,1)S(1)} collective-permute-done((bf16[256,1408]{1,0:T(8,128)(2,1)S(1)}, bf16[256,1408]{1,0:T(8,128)(2,1)S(1)}, u32[]{:S(2)}, u32[]{:S(2)}) %collective-permute-start.6) | collective-permute-done | bytes 720928 | tf_op jit(solution)/shard_map/ppermute | solution.py:249
  39.9 0.9 copy-done.8
  40.8 0.3 collective-permute-start.8
  41.1 1.2 collective-permute-start.9
  42.2 5.2 %collective-permute-start.12 = (bf16[256,2048]{1,0:T(8,128)(2,1)}, bf16[256,2048]{1,0:T(8,128)(2,1)}, u32[]{:S(2)}, u32[]{:S(2)}) collective-permute-start(bf16[256,2048]{1,0:T(8,128)(2,1)} %constant_dynamic-update-slice_fusion.refs_0_), channel_id=1, source_target_pairs={{0,14},{2,0},{4,2},{6,4},{8,6},{10,8},{12,10},{14,12},{1,15},{3,1}... | collective-permute-start | bytes 3145736 | tf_op jit(solution)/shard_map/ppermute | solution.py:284
  47.5 1.8 collective-permute-start.13
  49.2 5.1 %collective-permute-start.3 = (bf16[256,2048]{1,0:T(8,128)(2,1)}, bf16[256,2048]{1,0:T(8,128)(2,1)}, u32[]{:S(2)}, u32[]{:S(2)}) collective-permute-start(bf16[256,2048]{1,0:T(8,128)(2,1)} %constant_dynamic-update-slice_fusion.refs_0_), channel_id=1, source_target_pairs={{0,1},{1,0},{2,3},{3,2},{4,5},{5,4},{6,7},{7,6},{8,9},{9,8},{10,11... | collective-permute-start | bytes 3145736 | tf_op jit(solution)/shard_map/ppermute | solution.py:249
  54.4 2.2 %collective-permute-start.10 = (bf16[256,768]{1,0:T(8,128)(2,1)S(1)}, bf16[256,768]{1,0:T(8,128)(2,1)S(1)}, u32[]{:S(2)}, u32[]{:S(2)}) collective-permute-start(bf16[256,768]{1,0:T(8,128)(2,1)S(1)} %slice.16), channel_id=1, source_target_pairs={{0,48},{16,32},{32,16},{48,0},{1,49},{17,33},{33,17},{49,1},{2,50}... | collective-permute-start | bytes 1179656 | tf_op jit(solution)/shard_map/ppermute | solution.py:249
  56.7 6.3 %collective-permute-done.11.refs_10_.refs_12_ = bf16[256,640]{1,0:T(8,128)(2,1)S(1)} collective-permute-done((bf16[256,640]{1,0:T(8,128)(2,1)S(1)}, bf16[256,640]{1,0:T(8,128)(2,1)S(1)}, u32[]{:S(2)}, u32[]{:S(2)}) %collective-permute-start.11) | collective-permute-done | bytes 327712 | tf_op jit(solution)/shard_map/ppermute | solution.py:249
  63.0 7.5 %collective-permute-done.12.refs_0_ = bf16[256,2048]{1,0:T(8,128)(2,1)} collective-permute-done((bf16[256,2048]{1,0:T(8,128)(2,1)}, bf16[256,2048]{1,0:T(8,128)(2,1)}, u32[]{:S(2)}, u32[]{:S(2)}) %collective-permute-start.12) | collective-permute-done | bytes 1048608 | tf_op jit(solution)/shard_map/ppermute | solution.py:284
  70.5 3.0 %collective-permute-done.13.refs_2_ = bf16[256,2048]{1,0:T(8,128)(2,1)} collective-permute-done((bf16[256,2048]{1,0:T(8,128)(2,1)}, bf16[256,2048]{1,0:T(8,128)(2,1)}, u32[]{:S(2)}, u32[]{:S(2)}) %collective-permute-start.13) | collective-permute-done | bytes 1048608 | tf_op jit(solution)/shard_map/ppermute | solution.py:283
  73.5 4.5 %collective-permute-start.14 = (bf16[256,2048]{1,0:T(8,128)(2,1)}, bf16[256,2048]{1,0:T(8,128)(2,1)}, u32[]{:S(2)}, u32[]{:S(2)}) collective-permute-start(bf16[256,2048]{1,0:T(8,128)(2,1)} %collective-permute-done.12.refs_0_), channel_id=1, source_target_pairs={{0,1},{1,0},{2,3},{3,2},{4,5},{5,4},{6,7},{7,6},{8,9},{9,8},{10,11... | collective-permute-start | bytes 3145736 | tf_op jit(solution)/shard_map/ppermute | solution.py:249
  78.0 0.1 collective-permute-start.15
  78.1 0.6 pad_add_fusion.1.place
  78.8 7.1 %shard_map.151 = bf16[4,128,1408]{2,1,0:T(8,128)(2,1)} custom-call(s32[4]{0:T(128)} %pad_add_fusion.1.place, bf16[256,2048]{1,0:T(8,128)(2,1)} %constant_dynamic-update-slice_fusion.refs_0_, bf16[256,2048]{1,0:T(8,128)(2,1)} %collective-permute-done.3.refs_1_, bf16[256,1408]{1,0:T(8,128)(2,1)} %copy-done.3, bf16[256,1408]{1,0:T(8,128)(2,1)} %copy-done.6, ...), custom_call_target="tpu_custom_call" | custom-call | flops 1048576 | bytes 65536 | tf_op jit(solution)/shard_map/pallas_call | solution.py:217
  85.9 3.9 %all-to-all-start = ((bf16[4,128,1408]{2,1,0:T(8,128)(2,1)}), bf16[4,128,1408]{2,1,0:T(8,128)(2,1)S(1)}, u32[]{:S(2)}, u32[]{:S(2)}) async-start(bf16[4,128,1408]{2,1,0:T(8,128)(2,1)} %shard_map.151), calls=%async_computation | async-start | bytes 2883584 | tf_op jit(solution)/shard_map/all_to_all | solution.py:257
  89.8 11.3 %shard_map.152 = bf16[4,256,1408]{2,1,0:T(8,128)(2,1)} custom-call(s32[4]{0:T(128)} %pad_add_fusion.1.place, bf16[256,2048]{1,0:T(8,128)(2,1)} %collective-permute-done.12.refs_0_, bf16[256,2048]{1,0:T(8,128)(2,1)} %collective-permute-done.14.refs_1_, bf16[256,2048]{1,0:T(8,128)(2,1)} %collective-permute-done.13.refs_2_, ...), custom_call_target="tpu_custom_call" | custom-call | flops 1048576 | bytes 65536 | tf_op jit(solution)/shard_map/pallas_call | solution.py:217
  101.1 1.3 collective-permute-start.16
  102.4 1.7 collective-permute-start.17
  104.1 4.4 %all-to-all-done.refs_1_ = bf16[4,128,1408]{2,1,0:T(8,128)(2,1)S(1)} async-done(((bf16[4,128,1408]{2,1,0:T(8,128)(2,1)}), bf16[4,128,1408]{2,1,0:T(8,128)(2,1)S(1)}, u32[]{:S(2)}, u32[]{:S(2)}) %all-to-all-start) | async-done | bytes 1441824 | tf_op jit(solution)/shard_map/all_to_all | solution.py:257
  108.5 4.6 %all-to-all-start.1 = ((bf16[4,256,1408]{2,1,0:T(8,128)(2,1)}), bf16[4,256,1408]{2,1,0:T(8,128)(2,1)}, u32[]{:S(2)}, u32[]{:S(2)}) async-start(bf16[4,256,1408]{2,1,0:T(8,128)(2,1)} %shard_map.152), calls=%async_computation.1 | async-start | bytes 5767168 | tf_op jit(solution)/shard_map/all_to_all | solution.py:257
  113.0 14.2 %collective-permute-done.16 = bf16[256,2048]{1,0:T(8,128)(2,1)S(1)} collective-permute-done((bf16[256,2048]{1,0:T(8,128)(2,1)}, bf16[256,2048]{1,0:T(8,128)(2,1)S(1)}, u32[]{:S(2)}, u32[]{:S(2)}) %collective-permute-start.16) | collective-permute-done | bytes 1048608 | tf_op jit(solution)/shard_map/ppermute | solution.py:299
  127.2 0.1 broadcast_select_fusion.refs_0_
  127.4 1.6 collective-permute-start.18
  129.0 2.3 %collective-permute-done.18.refs_1_ = bf16[256,2048]{1,0:T(8,128)(2,1)S(1)} collective-permute-done((bf16[256,2048]{1,0:T(8,128)(2,1)S(1)}, bf16[256,2048]{1,0:T(8,128)(2,1)S(1)}, u32[]{:S(2)}, u32[]{:S(2)}) %collective-permute-start.18) | collective-permute-done | bytes 1048608 | tf_op jit(solution)/shard_map/ppermute | solution.py:249
  131.2 1.0 copy-done.12
  132.2 7.3 %shard_map.153 = (f32[128,1408]{1,0:T(8,128)}, bf16[128,1408]{1,0:T(8,128)(2,1)}, bf16[128,1408]{1,0:T(8,128)(2,1)}, bf16[128,1408]{1,0:T(8,128)(2,1)}) custom-call(s32[4]{0:T(128)} %pad_add_fusion.1.place, bf16[256,2048]{1,0:T(8,128)(2,1)} %copy-done.9, bf16[256,2048]{1,0:T(8,128)(2,1)} %copy-done.12, bf16[256,1408]{1,0:T(8,128)(2,1)} %copy-done.3, ...), custom_call_target="tpu_custom_call" | custom-call | flops 1048576 | bytes 65536 | tf_op jit(solution)/shard_map/pallas_call | solution.py:217
  139.5 1.5 collective-permute-start.19
  141.0 2.4 %collective-permute-start.20 = (bf16[128,1408]{1,0:T(8,128)(2,1)}, bf16[128,1408]{1,0:T(8,128)(2,1)}, u32[]{:S(2)}, u32[]{:S(2)}) collective-permute-start(bf16[128,1408]{1,0:T(8,128)(2,1)} %get-tuple-element.60), channel_id=1, source_target_pairs={{0,128},{64,192},{128,0},{192,64},{1,129},{65,193},{129,1},{193,65... | collective-permute-start | bytes 1081352 | tf_op jit(solution)/shard_map/ppermute | solution.py:249
  143.5 2.8 %all-to-all-done.1 = bf16[4,256,1408]{2,1,0:T(8,128)(2,1)} async-done(((bf16[4,256,1408]{2,1,0:T(8,128)(2,1)}), bf16[4,256,1408]{2,1,0:T(8,128)(2,1)}, u32[]{:S(2)}, u32[]{:S(2)}) %all-to-all-start.1) | async-done | bytes 2883616 | tf_op jit(solution)/shard_map/all_to_all | solution.py:257
  146.3 2.6 %reduce_sum.12.refs_0_ = bf16[256,1408]{1,0:T(8,128)(2,1)S(1)} reduce(bf16[4,256,1408]{2,1,0:T(8,128)(2,1)} %all-to-all-done.1, bf16[]{:T(256)} %constant.61.clone.1), dimensions={0}, to_apply=%region_0.1 | reduce | flops 1081344 | bytes 3604482 | tf_op jit(solution)/shard_map/reduce_sum | solution.py:261
  149.0 0.8 slice_select_fusion
  149.8 3.4 %collective-permute-start.22 = (bf16[128,1408]{1,0:T(8,128)(2,1)}, bf16[128,1408]{1,0:T(8,128)(2,1)}, u32[]{:S(2)}, u32[]{:S(2)}) collective-permute-start(bf16[128,1408]{1,0:T(8,128)(2,1)} %slice_select_fusion), channel_id=1, source_target_pairs={{0,8},{6,14},{8,0},{14,6},{1,9},{7,15},{9,1},{15,7},{16,24},{22,30... | collective-permute-start | bytes 1081352 | tf_op jit(solution)/shard_map/ppermute | solution.py:313
  153.4 4.8 %shard_map.154 = (bf16[64,1024]{1,0:T(8,128)(2,1)S(1)}, bf16[64,1024]{1,0:T(8,128)(2,1)S(1)}, bf16[64,1024]{1,0:T(8,128)(2,1)S(1)}, bf16[64,1024]{1,0:T(8,128)(2,1)S(1)}, f32[4,16,64,128]{3,2,1,0:T(8,128)}) custom-call(s32[4]{0:T(128)S(1)} %copy-done.2, bf16[256,1408]{1,0:T(8,128)(2,1)S(1)} %reduce_sum.12.refs_0_, ...), custom_call_target="tpu_custom_call" | custom-call | flops 1048576 | bytes 65536 | tf_op jit(solution)/shard_map/pallas_call | solution.py:120
  158.2 3.6 %collective-permute-done.20.refs_3_ = bf16[128,1408]{1,0:T(8,128)(2,1)} collective-permute-done((bf16[128,1408]{1,0:T(8,128)(2,1)}, bf16[128,1408]{1,0:T(8,128)(2,1)}, u32[]{:S(2)}, u32[]{:S(2)}) %collective-permute-start.20) | collective-permute-done | bytes 360480 | tf_op jit(solution)/shard_map/ppermute | solution.py:249
  161.8 0.4 collective-permute-done.22.refs_5_
  162.2 5.6 %shard_map.155 = (bf16[64,1024]{1,0:T(8,128)(2,1)S(1)}, bf16[64,1024]{1,0:T(8,128)(2,1)S(1)}, bf16[64,1024]{1,0:T(8,128)(2,1)S(1)}, bf16[64,1024]{1,0:T(8,128)(2...) custom-call(s32[4]{0:T(128)S(1)} %copy-done.2, ...), custom_call_target="tpu_custom_call", output_to_operand_aliasing={{6}: (11, {})} | custom-call | flops 1048576 | bytes 65536 | tf_op jit(solution)/shard_map/pallas_call | solution.py:120
  167.8 3.4 %collective-permute-start.25 = (bf16[64,1024]{1,0:T(8,128)(2,1)S(1)}, bf16[64,1024]{1,0:T(8,128)(2,1)S(1)}, u32[]{:S(2)}, u32[]{:S(2)}) collective-permute-start(bf16[64,1024]{1,0:T(8,128)(2,1)S(1)} %get-tuple-element.71), channel_id=1, source_target_pairs={{0,4},{1,5},{2,6},{3,7},{4,0},{5,1},{6,2},{7,3},{8,12},{9,13},{10,... | collective-permute-start | bytes 393224 | tf_op jit(solution)/shard_map/ppermute | solution.py:322
  171.2 1.3 collective-permute-start.23
  172.5 1.3 collective-permute-start.24
  173.8 3.8 %collective-permute-start.29 = (bf16[64,1024]{1,0:T(8,128)(2,1)S(1)}, bf16[64,1024]{1,0:T(8,128)(2,1)S(1)}, u32[]{:S(2)}, u32[]{:S(2)}) collective-permute-start(bf16[64,1024]{1,0:T(8,128)(2,1)S(1)} %get-tuple-element.76), channel_id=1, source_target_pairs={{0,5},{1,4},{2,7},{3,6},{4,1},{5,0},{6,3},{7,2},{8,13},{9,12},{10,... | collective-permute-start | bytes 393224 | tf_op jit(solution)/shard_map/ppermute | solution.py:322
  177.6 2.6 %collective-permute-start.30 = (bf16[64,1024]{1,0:T(8,128)(2,1)S(1)}, bf16[64,1024]{1,0:T(8,128)(2,1)S(1)}, u32[]{:S(2)}, u32[]{:S(2)}) collective-permute-start(bf16[64,1024]{1,0:T(8,128)(2,1)S(1)} %get-tuple-element.77), channel_id=1, source_target_pairs={{0,6},{1,7},{2,0},{3,1},{4,2},{5,3},{6,4},{7,5},{8,14},{9,15},{10,... | collective-permute-start | bytes 393224 | tf_op jit(solution)/shard_map/ppermute | solution.py:322
  180.2 4.2 %collective-permute-start.31 = (bf16[64,1024]{1,0:T(8,128)(2,1)S(1)}, bf16[64,1024]{1,0:T(8,128)(2,1)S(1)}, u32[]{:S(2)}, u32[]{:S(2)}) collective-permute-start(bf16[64,1024]{1,0:T(8,128)(2,1)S(1)} %get-tuple-element.78), channel_id=1, source_target_pairs={{0,7},{1,6},{2,1},{3,0},{4,3},{5,2},{6,5},{7,4},{8,15},{9,14},{10,... | collective-permute-start | bytes 393224 | tf_op jit(solution)/shard_map/ppermute | solution.py:322
  184.4 6.7 %collective-permute-start.26 = (bf16[64,1024]{1,0:T(8,128)(2,1)S(1)}, bf16[64,1024]{1,0:T(8,128)(2,1)S(1)}, u32[]{:S(2)}, u32[]{:S(2)}) collective-permute-start(bf16[64,1024]{1,0:T(8,128)(2,1)S(1)} %get-tuple-element.72), channel_id=1, source_target_pairs={{0,2},{1,3},{2,4},{3,5},{4,6},{5,7},{8,10},{9,11},{10,12},{11,13},... | collective-permute-start | bytes 393224 | tf_op jit(solution)/shard_map/ppermute | solution.py:322
  191.2 1.3 collective-permute-start.27
  192.5 1.1 collective-permute-start.28
  193.7 1.0 collective-permute-done.27.refs_3_
  194.7 1.6 shard_map.156
  (81 shorter events, 0.9 us)
Async XLA Ops:
  0.6 2.2 %copy-start.21 = (s32[4]{0:T(128)S(1)}, s32[4]{0:T(128)}, u32[]{:S(2)}) copy-start(s32[4]{0:T(128)} %constant.63.clone) | copy-start | bytes 52
  0.6 2.4 %copy-start = (bf16[64,8192]{1,0:T(8,128)(2,1)S(1)}, bf16[64,8192]{1,0:T(8,128)(2,1)}, u32[]{:S(2)}) copy-start(bf16[64,8192]{1,0:T(8,128)(2,1)} %tokens) | copy-start | bytes 3145732
  2.7 29.3 %copy-start.3 = (bf16[256,1408]{1,0:T(8,128)(2,1)}, bf16[256,1408]{1,0:T(8,128)(2,1)S(1)}, u32[]{:S(2)}) copy-start(bf16[256,1408]{1,0:T(8,128)(2,1)S(1)} %fusion.1.refs_2_.refs_4_) | copy-start | bytes 2162692
  3.7 15.5 %collective-permute-start = (bf16[64,2048]{1,0:T(8,128)(2,1)S(1)}, bf16[64,2048]{1,0:T(8,128)(2,1)S(1)}, u32[]{:S(2)}, u32[]{:S(2)}) collective-permute-start(bf16[64,2048]{1,0:T(8,128)(2,1)S(1)} %get-tuple-element.43), channel_id=1, source_target_pairs={{0,64},{64,0},{128,192},{192,128},{1,65},{65,1},{129,193},{193,129... | collective-permute-start | bytes 786440 | tf_op jit(solution)/shard_map/ppermute | solution.py:249
  5.9 28.3 %collective-permute-start.4 = (bf16[256,1408]{1,0:T(8,128)(2,1)S(1)}, bf16[256,1408]{1,0:T(8,128)(2,1)S(1)}, u32[]{:S(2)}, u32[]{:S(2)}) collective-permute-start(bf16[256,1408]{1,0:T(8,128)(2,1)S(1)} %fusion.1.refs_2_.refs_4_), channel_id=1, source_target_pairs={{0,16},{16,0},{32,48},{48,32},{1,17},{17,1},{33,49},{49,33},{2,18}... | collective-permute-start | bytes 2162696 | tf_op jit(solution)/shard_map/ppermute | solution.py:249
  7.1 27.1 %collective-permute-start.5 = (bf16[256,1408]{1,0:T(8,128)(2,1)S(1)}, bf16[256,1408]{1,0:T(8,128)(2,1)S(1)}, u32[]{:S(2)}, u32[]{:S(2)}) collective-permute-start(bf16[256,1408]{1,0:T(8,128)(2,1)S(1)} %fusion.1.refs_2_.refs_4_), channel_id=1, source_target_pairs={{0,48},{16,32},{32,16},{48,0},{1,49},{17,33},{33,17},{49,1},{2,50}... | collective-permute-start | bytes 2162696 | tf_op jit(solution)/shard_map/ppermute | solution.py:249
  8.9 25.3 %collective-permute-start.7 = (bf16[256,1408]{1,0:T(8,128)(2,1)S(1)}, bf16[256,1408]{1,0:T(8,128)(2,1)}, u32[]{:S(2)}, u32[]{:S(2)}) collective-permute-start(bf16[256,1408]{1,0:T(8,128)(2,1)S(1)} %fusion.1.refs_2_.refs_4_), channel_id=1, source_target_pairs={{0,8},{8,0},{1,9},{9,1},{2,10},{10,2},{3,11},{11,3},{4,12},{12,4},... | collective-permute-start | bytes 2162696 | tf_op jit(solution)/shard_map/ppermute | solution.py:249
  15.9 7.6 %collective-permute-start.1 = (bf16[64,2048]{1,0:T(8,128)(2,1)S(1)}, bf16[64,2048]{1,0:T(8,128)(2,1)S(1)}, u32[]{:S(2)}, u32[]{:S(2)}) collective-permute-start(bf16[64,2048]{1,0:T(8,128)(2,1)S(1)} %get-tuple-element.44), channel_id=1, source_target_pairs={{0,128},{64,192},{128,0},{192,64},{1,129},{65,193},{129,1},{193,65... | collective-permute-start | bytes 786440 | tf_op jit(solution)/shard_map/ppermute | solution.py:249
  19.2 12.1 %collective-permute-start.2 = (bf16[64,2048]{1,0:T(8,128)(2,1)S(1)}, bf16[64,2048]{1,0:T(8,128)(2,1)S(1)}, u32[]{:S(2)}, u32[]{:S(2)}) collective-permute-start(bf16[64,2048]{1,0:T(8,128)(2,1)S(1)} %get-tuple-element.45), channel_id=1, source_target_pairs={{0,192},{64,128},{128,64},{192,0},{1,193},{65,129},{129,65},{193,1... | collective-permute-start | bytes 786440 | tf_op jit(solution)/shard_map/ppermute | solution.py:249
  23.5 16.4 %collective-permute-start.6 = (bf16[256,1408]{1,0:T(8,128)(2,1)S(1)}, bf16[256,1408]{1,0:T(8,128)(2,1)S(1)}, u32[]{:S(2)}, u32[]{:S(2)}) collective-permute-start(bf16[256,1408]{1,0:T(8,128)(2,1)S(1)} %fusion.1.refs_2_.refs_4_), channel_id=1, source_target_pairs={{0,32},{16,48},{32,0},{48,16},{1,33},{17,49},{33,1},{49,17},{2,34}... | collective-permute-start | bytes 2162696 | tf_op jit(solution)/shard_map/ppermute | solution.py:249
  34.2 44.6 %copy-start.6 = (bf16[256,1408]{1,0:T(8,128)(2,1)}, bf16[256,1408]{1,0:T(8,128)(2,1)S(1)}, u32[]{:S(2)}) copy-start(bf16[256,1408]{1,0:T(8,128)(2,1)S(1)} %collective-permute-done.4.refs_3_.refs_5_) | copy-start | bytes 2162692
  34.2 44.5 %copy-start.7 = (bf16[256,1408]{1,0:T(8,128)(2,1)}, bf16[256,1408]{1,0:T(8,128)(2,1)S(1)}, u32[]{:S(2)}) copy-start(bf16[256,1408]{1,0:T(8,128)(2,1)S(1)} %collective-permute-done.5.refs_4_.refs_6_) | copy-start | bytes 2162692
  39.9 0.9 copy-start.8
  40.8 13.6 %collective-permute-start.8 = (bf16[256,1408]{1,0:T(8,128)(2,1)}, bf16[256,1408]{1,0:T(8,128)(2,1)S(1)}, u32[]{:S(2)}, u32[]{:S(2)}) collective-permute-start(bf16[256,1408]{1,0:T(8,128)(2,1)} %shard_map.150.refs_6_.refs_8_), channel_id=1, source_target_pairs={{0,16},{16,0},{32,48},{48,32},{1,17},{17,1},{33,49},{49,33},{2,18}... | collective-permute-start | bytes 2162696 | tf_op jit(solution)/shard_map/ppermute | solution.py:249
  41.1 15.5 %collective-permute-start.9 = (bf16[256,1408]{1,0:T(8,128)(2,1)}, bf16[256,1408]{1,0:T(8,128)(2,1)S(1)}, u32[]{:S(2)}, u32[]{:S(2)}) collective-permute-start(bf16[256,1408]{1,0:T(8,128)(2,1)} %shard_map.150.refs_6_.refs_8_), channel_id=1, source_target_pairs={{0,48},{16,32},{32,16},{48,0},{1,49},{17,33},{33,17},{49,1},{2,50}... | collective-permute-start | bytes 2162696 | tf_op jit(solution)/shard_map/ppermute | solution.py:249
  42.2 28.3 %collective-permute-start.12 = (bf16[256,2048]{1,0:T(8,128)(2,1)}, bf16[256,2048]{1,0:T(8,128)(2,1)}, u32[]{:S(2)}, u32[]{:S(2)}) collective-permute-start(bf16[256,2048]{1,0:T(8,128)(2,1)} %constant_dynamic-update-slice_fusion.refs_0_), channel_id=1, source_target_pairs={{0,14},{2,0},{4,2},{6,4},{8,6},{10,8},{12,10},{14,12},{1,15},{3,1}... | collective-permute-start | bytes 3145736 | tf_op jit(solution)/shard_map/ppermute | solution.py:284
  47.5 26.1 %collective-permute-start.13 = (bf16[256,2048]{1,0:T(8,128)(2,1)}, bf16[256,2048]{1,0:T(8,128)(2,1)}, u32[]{:S(2)}, u32[]{:S(2)}) collective-permute-start(bf16[256,2048]{1,0:T(8,128)(2,1)} %constant_dynamic-update-slice_fusion.refs_0_), channel_id=1, source_target_pairs={{0,2},{2,4},{4,6},{6,8},{8,10},{10,12},{12,14},{14,0},{1,3},{3,5},... | collective-permute-start | bytes 3145736 | tf_op jit(solution)/shard_map/ppermute | solution.py:283
  49.2 29.5 %collective-permute-start.3 = (bf16[256,2048]{1,0:T(8,128)(2,1)}, bf16[256,2048]{1,0:T(8,128)(2,1)}, u32[]{:S(2)}, u32[]{:S(2)}) collective-permute-start(bf16[256,2048]{1,0:T(8,128)(2,1)} %constant_dynamic-update-slice_fusion.refs_0_), channel_id=1, source_target_pairs={{0,1},{1,0},{2,3},{3,2},{4,5},{5,4},{6,7},{7,6},{8,9},{9,8},{10,11... | collective-permute-start | bytes 3145736 | tf_op jit(solution)/shard_map/ppermute | solution.py:249
  54.3 24.4 %copy-start.4 = (bf16[256,1408]{1,0:T(8,128)(2,1)}, bf16[256,1408]{1,0:T(8,128)(2,1)S(1)}, u32[]{:S(2)}) copy-start(bf16[256,1408]{1,0:T(8,128)(2,1)S(1)} %collective-permute-done.8.refs_7_.refs_9_) | copy-start | bytes 2162692
  54.4 19.2 %collective-permute-start.10 = (bf16[256,768]{1,0:T(8,128)(2,1)S(1)}, bf16[256,768]{1,0:T(8,128)(2,1)S(1)}, u32[]{:S(2)}, u32[]{:S(2)}) collective-permute-start(bf16[256,768]{1,0:T(8,128)(2,1)S(1)} %slice.16), channel_id=1, source_target_pairs={{0,48},{16,32},{32,16},{48,0},{1,49},{17,33},{33,17},{49,1},{2,50}... | collective-permute-start | bytes 1179656 | tf_op jit(solution)/shard_map/ppermute | solution.py:249
  56.5 22.3 %copy-start.5 = (bf16[256,1408]{1,0:T(8,128)(2,1)}, bf16[256,1408]{1,0:T(8,128)(2,1)S(1)}, u32[]{:S(2)}) copy-start(bf16[256,1408]{1,0:T(8,128)(2,1)S(1)} %collective-permute-done.9.refs_8_.refs_10_) | copy-start | bytes 2162692
  56.6 6.4 %collective-permute-start.11 = (bf16[256,640]{1,0:T(8,128)(2,1)S(1)}, bf16[256,640]{1,0:T(8,128)(2,1)S(1)}, u32[]{:S(2)}, u32[]{:S(2)}) collective-permute-start(bf16[256,640]{1,0:T(8,128)(2,1)S(1)} %slice.17), channel_id=1, source_target_pairs={{0,16},{16,0},{32,48},{48,32},{1,17},{17,1},{33,49},{49,33},{2,18}... | collective-permute-start | bytes 983048 | tf_op jit(solution)/shard_map/ppermute | solution.py:249
  63.0 10.5 %copy-start.11 = (bf16[256,640]{1,0:T(8,128)(2,1)}, bf16[256,640]{1,0:T(8,128)(2,1)S(1)}, u32[]{:S(2)}) copy-start(bf16[256,640]{1,0:T(8,128)(2,1)S(1)} %collective-permute-done.11.refs_10_.refs_12_) | copy-start | bytes 983044
  73.5 5.3 %copy-start.10 = (bf16[256,768]{1,0:T(8,128)(2,1)}, bf16[256,768]{1,0:T(8,128)(2,1)S(1)}, u32[]{:S(2)}) copy-start(bf16[256,768]{1,0:T(8,128)(2,1)S(1)} %collective-permute-done.10.refs_9_.refs_11_) | copy-start | bytes 1179652
  73.5 16.3 %collective-permute-start.14 = (bf16[256,2048]{1,0:T(8,128)(2,1)}, bf16[256,2048]{1,0:T(8,128)(2,1)}, u32[]{:S(2)}, u32[]{:S(2)}) collective-permute-start(bf16[256,2048]{1,0:T(8,128)(2,1)} %collective-permute-done.12.refs_0_), channel_id=1, source_target_pairs={{0,1},{1,0},{2,3},{3,2},{4,5},{5,4},{6,7},{7,6},{8,9},{9,8},{10,11... | collective-permute-start | bytes 3145736 | tf_op jit(solution)/shard_map/ppermute | solution.py:249
  78.0 11.8 %collective-permute-start.15 = (bf16[256,2048]{1,0:T(8,128)(2,1)}, bf16[256,2048]{1,0:T(8,128)(2,1)}, u32[]{:S(2)}, u32[]{:S(2)}) collective-permute-start(bf16[256,2048]{1,0:T(8,128)(2,1)} %collective-permute-done.13.refs_2_), channel_id=1, source_target_pairs={{0,1},{1,0},{2,3},{3,2},{4,5},{5,4},{6,7},{7,6},{8,9},{9,8},{10,11... | collective-permute-start | bytes 3145736 | tf_op jit(solution)/shard_map/ppermute | solution.py:249
  85.9 22.5 %all-to-all-start = ((bf16[4,128,1408]{2,1,0:T(8,128)(2,1)}), bf16[4,128,1408]{2,1,0:T(8,128)(2,1)S(1)}, u32[]{:S(2)}, u32[]{:S(2)}) async-start(bf16[4,128,1408]{2,1,0:T(8,128)(2,1)} %shard_map.151), calls=%async_computation | async-start | bytes 2883584 | tf_op jit(solution)/shard_map/all_to_all | solution.py:257
  101.1 26.2 %collective-permute-start.16 = (bf16[256,2048]{1,0:T(8,128)(2,1)}, bf16[256,2048]{1,0:T(8,128)(2,1)S(1)}, u32[]{:S(2)}, u32[]{:S(2)}) collective-permute-start(bf16[256,2048]{1,0:T(8,128)(2,1)} %collective-permute-done.12.refs_0_), channel_id=1, source_target_pairs={{2,0},{4,2},{10,8},{12,10},{3,1},{5,3},{11,9},{13,11},{18,16},{20,... | collective-permute-start | bytes 3145736 | tf_op jit(solution)/shard_map/ppermute | solution.py:299
  102.4 24.9 %collective-permute-start.17 = (bf16[256,2048]{1,0:T(8,128)(2,1)}, bf16[256,2048]{1,0:T(8,128)(2,1)}, u32[]{:S(2)}, u32[]{:S(2)}) collective-permute-start(bf16[256,2048]{1,0:T(8,128)(2,1)} %collective-permute-done.13.refs_2_), channel_id=1, source_target_pairs={{2,4},{4,6},{10,12},{12,14},{3,5},{5,7},{11,13},{13,15},{18,20},{2... | collective-permute-start | bytes 3145736 | tf_op jit(solution)/shard_map/ppermute | solution.py:298
  108.5 37.8 %all-to-all-start.1 = ((bf16[4,256,1408]{2,1,0:T(8,128)(2,1)}), bf16[4,256,1408]{2,1,0:T(8,128)(2,1)}, u32[]{:S(2)}, u32[]{:S(2)}) async-start(bf16[4,256,1408]{2,1,0:T(8,128)(2,1)} %shard_map.152), calls=%async_computation.1 | async-start | bytes 5767168 | tf_op jit(solution)/shard_map/all_to_all | solution.py:257
  127.3 3.9 %copy-start.9 = (bf16[256,2048]{1,0:T(8,128)(2,1)}, bf16[256,2048]{1,0:T(8,128)(2,1)S(1)}, u32[]{:S(2)}) copy-start(bf16[256,2048]{1,0:T(8,128)(2,1)S(1)} %broadcast_select_fusion.refs_0_) | copy-start | bytes 3145732
  127.4 3.9 %collective-permute-start.18 = (bf16[256,2048]{1,0:T(8,128)(2,1)S(1)}, bf16[256,2048]{1,0:T(8,128)(2,1)S(1)}, u32[]{:S(2)}, u32[]{:S(2)}) collective-permute-start(bf16[256,2048]{1,0:T(8,128)(2,1)S(1)} %broadcast_select_fusion.refs_0_), channel_id=1, source_target_pairs={{0,1},{1,0},{2,3},{3,2},{4,5},{5,4},{6,7},{7,6},{8,9},{9,8},{10,11... | collective-permute-start | bytes 3145736 | tf_op jit(solution)/shard_map/ppermute | solution.py:249
  131.2 1.0 copy-start.12
  139.5 18.7 %collective-permute-start.19 = (bf16[128,1408]{1,0:T(8,128)(2,1)}, bf16[128,1408]{1,0:T(8,128)(2,1)S(1)}, u32[]{:S(2)}, u32[]{:S(2)}) collective-permute-start(bf16[128,1408]{1,0:T(8,128)(2,1)} %get-tuple-element.59), channel_id=1, source_target_pairs={{0,64},{64,0},{128,192},{192,128},{1,65},{65,1},{129,193},{193,129... | collective-permute-start | bytes 1081352 | tf_op jit(solution)/shard_map/ppermute | solution.py:249
  141.0 20.8 %collective-permute-start.20 = (bf16[128,1408]{1,0:T(8,128)(2,1)}, bf16[128,1408]{1,0:T(8,128)(2,1)}, u32[]{:S(2)}, u32[]{:S(2)}) collective-permute-start(bf16[128,1408]{1,0:T(8,128)(2,1)} %get-tuple-element.60), channel_id=1, source_target_pairs={{0,128},{64,192},{128,0},{192,64},{1,129},{65,193},{129,1},{193,65... | collective-permute-start | bytes 1081352 | tf_op jit(solution)/shard_map/ppermute | solution.py:249
  143.4 18.4 %collective-permute-start.21 = (bf16[128,1408]{1,0:T(8,128)(2,1)}, bf16[128,1408]{1,0:T(8,128)(2,1)}, u32[]{:S(2)}, u32[]{:S(2)}) collective-permute-start(bf16[128,1408]{1,0:T(8,128)(2,1)} %get-tuple-element.61), channel_id=1, source_target_pairs={{0,192},{64,128},{128,64},{192,0},{1,193},{65,129},{129,65},{193,1... | collective-permute-start | bytes 1081352 | tf_op jit(solution)/shard_map/ppermute | solution.py:249
  146.3 6.9 %copy-start.19 = (f32[16]{0:T(128)S(1)}, f32[16]{0:T(128)}, u32[]{:S(2)}) copy-start(f32[16]{0:T(128)} %param.23) | copy-start | bytes 196
  146.3 6.9 %copy-start.20 = (f32[16]{0:T(128)S(1)}, f32[16]{0:T(128)}, u32[]{:S(2)}) copy-start(f32[16]{0:T(128)} %param.22) | copy-start | bytes 196
  146.3 6.9 %copy-start.16 = (f32[16]{0:T(128)S(1)}, f32[16]{0:T(128)}, u32[]{:S(2)}) copy-start(f32[16]{0:T(128)} %param.24) | copy-start | bytes 196
  146.3 7.1 %copy-start.13 = (f32[4,1024]{1,0:T(4,128)S(1)}, f32[4,1024]{1,0:T(4,128)}, u32[]{:S(2)}) copy-start(f32[4,1024]{1,0:T(4,128)} %param.19) | copy-start | bytes 49156
  146.3 7.1 %copy-start.14 = (f32[4,128]{1,0:T(4,128)S(1)}, f32[4,128]{1,0:T(4,128)}, u32[]{:S(2)}) copy-start(f32[4,128]{1,0:T(4,128)} %param.20) | copy-start | bytes 6148
  146.3 7.1 %copy-start.15 = (f32[4,128]{1,0:T(4,128)S(1)}, f32[4,128]{1,0:T(4,128)}, u32[]{:S(2)}) copy-start(f32[4,128]{1,0:T(4,128)} %param.21) | copy-start | bytes 6148
  146.3 7.1 %copy-start.2 = (s32[4]{0:T(128)S(1)}, s32[4]{0:T(128)}, u32[]{:S(2)}) copy-start(s32[4]{0:T(128)} %pad_add_fusion.1.place) | copy-start | bytes 52
  149.0 13.2 %copy-start.1 = (f32[128,1408]{1,0:T(8,128)S(1)}, f32[128,1408]{1,0:T(8,128)}, u32[]{:S(2)}) copy-start(f32[128,1408]{1,0:T(8,128)} %get-tuple-element.58.refs_1_) | copy-start | bytes 2162692
  149.8 12.4 %collective-permute-start.22 = (bf16[128,1408]{1,0:T(8,128)(2,1)}, bf16[128,1408]{1,0:T(8,128)(2,1)}, u32[]{:S(2)}, u32[]{:S(2)}) collective-permute-start(bf16[128,1408]{1,0:T(8,128)(2,1)} %slice_select_fusion), channel_id=1, source_target_pairs={{0,8},{6,14},{8,0},{14,6},{1,9},{7,15},{9,1},{15,7},{16,24},{22,30... | collective-permute-start | bytes 1081352 | tf_op jit(solution)/shard_map/ppermute | solution.py:313
  162.2 31.4 %copy-start.17 = (s32[8]{0:T(128)S(1)}, s32[8]{0:T(128)}, u32[]{:S(2)}) copy-start(s32[8]{0:T(128)} %constant.64.clone) | copy-start | bytes 100
  162.2 31.4 %copy-start.18 = (s32[8]{0:T(128)S(1)}, s32[8]{0:T(128)}, u32[]{:S(2)}) copy-start(s32[8]{0:T(128)} %constant.65.clone) | copy-start | bytes 100
  167.8 12.4 %collective-permute-start.25 = (bf16[64,1024]{1,0:T(8,128)(2,1)S(1)}, bf16[64,1024]{1,0:T(8,128)(2,1)S(1)}, u32[]{:S(2)}, u32[]{:S(2)}) collective-permute-start(bf16[64,1024]{1,0:T(8,128)(2,1)S(1)} %get-tuple-element.71), channel_id=1, source_target_pairs={{0,4},{1,5},{2,6},{3,7},{4,0},{5,1},{6,2},{7,3},{8,12},{9,13},{10,... | collective-permute-start | bytes 393224 | tf_op jit(solution)/shard_map/ppermute | solution.py:322
  171.2 13.3 %collective-permute-start.23 = (bf16[64,1024]{1,0:T(8,128)(2,1)S(1)}, bf16[64,1024]{1,0:T(8,128)(2,1)S(1)}, u32[]{:S(2)}, u32[]{:S(2)}) collective-permute-start(bf16[64,1024]{1,0:T(8,128)(2,1)S(1)} %get-tuple-element.65), channel_id=1, source_target_pairs={{6,0},{7,1},{14,8},{15,9},{22,16},{23,17},{30,24},{31,25},{38,32},... | collective-permute-start | bytes 393224 | tf_op jit(solution)/shard_map/ppermute | solution.py:322
  172.5 18.7 %collective-permute-start.24 = (bf16[64,1024]{1,0:T(8,128)(2,1)S(1)}, bf16[64,1024]{1,0:T(8,128)(2,1)S(1)}, u32[]{:S(2)}, u32[]{:S(2)}) collective-permute-start(bf16[64,1024]{1,0:T(8,128)(2,1)S(1)} %get-tuple-element.66), channel_id=1, source_target_pairs={{6,1},{7,0},{14,9},{15,8},{22,17},{23,16},{30,25},{31,24},{38,33},... | collective-permute-start | bytes 393224 | tf_op jit(solution)/shard_map/ppermute | solution.py:322
  173.8 18.7 %collective-permute-start.29 = (bf16[64,1024]{1,0:T(8,128)(2,1)S(1)}, bf16[64,1024]{1,0:T(8,128)(2,1)S(1)}, u32[]{:S(2)}, u32[]{:S(2)}) collective-permute-start(bf16[64,1024]{1,0:T(8,128)(2,1)S(1)} %get-tuple-element.76), channel_id=1, source_target_pairs={{0,5},{1,4},{2,7},{3,6},{4,1},{5,0},{6,3},{7,2},{8,13},{9,12},{10,... | collective-permute-start | bytes 393224 | tf_op jit(solution)/shard_map/ppermute | solution.py:322
  177.6 16.1 %collective-permute-start.30 = (bf16[64,1024]{1,0:T(8,128)(2,1)S(1)}, bf16[64,1024]{1,0:T(8,128)(2,1)S(1)}, u32[]{:S(2)}, u32[]{:S(2)}) collective-permute-start(bf16[64,1024]{1,0:T(8,128)(2,1)S(1)} %get-tuple-element.77), channel_id=1, source_target_pairs={{0,6},{1,7},{2,0},{3,1},{4,2},{5,3},{6,4},{7,5},{8,14},{9,15},{10,... | collective-permute-start | bytes 393224 | tf_op jit(solution)/shard_map/ppermute | solution.py:322
  180.2 13.5 %collective-permute-start.31 = (bf16[64,1024]{1,0:T(8,128)(2,1)S(1)}, bf16[64,1024]{1,0:T(8,128)(2,1)S(1)}, u32[]{:S(2)}, u32[]{:S(2)}) collective-permute-start(bf16[64,1024]{1,0:T(8,128)(2,1)S(1)} %get-tuple-element.78), channel_id=1, source_target_pairs={{0,7},{1,6},{2,1},{3,0},{4,3},{5,2},{6,5},{7,4},{8,15},{9,14},{10,... | collective-permute-start | bytes 393224 | tf_op jit(solution)/shard_map/ppermute | solution.py:322
  184.4 9.2 %collective-permute-start.26 = (bf16[64,1024]{1,0:T(8,128)(2,1)S(1)}, bf16[64,1024]{1,0:T(8,128)(2,1)S(1)}, u32[]{:S(2)}, u32[]{:S(2)}) collective-permute-start(bf16[64,1024]{1,0:T(8,128)(2,1)S(1)} %get-tuple-element.72), channel_id=1, source_target_pairs={{0,2},{1,3},{2,4},{3,5},{4,6},{5,7},{8,10},{9,11},{10,12},{11,13},... | collective-permute-start | bytes 393224 | tf_op jit(solution)/shard_map/ppermute | solution.py:322
  191.2 3.5 %collective-permute-start.27 = (bf16[64,1024]{1,0:T(8,128)(2,1)S(1)}, bf16[64,1024]{1,0:T(8,128)(2,1)S(1)}, u32[]{:S(2)}, u32[]{:S(2)}) collective-permute-start(bf16[64,1024]{1,0:T(8,128)(2,1)S(1)} %get-tuple-element.73), channel_id=1, source_target_pairs={{0,3},{1,2},{2,5},{3,4},{4,7},{5,6},{8,11},{9,10},{10,13},{11,12},... | collective-permute-start | bytes 393224 | tf_op jit(solution)/shard_map/ppermute | solution.py:322
  192.5 2.2 %collective-permute-start.28 = (bf16[64,1024]{1,0:T(8,128)(2,1)S(1)}, bf16[64,1024]{1,0:T(8,128)(2,1)S(1)}, u32[]{:S(2)}, u32[]{:S(2)}) collective-permute-start(bf16[64,1024]{1,0:T(8,128)(2,1)S(1)} %get-tuple-element.75), channel_id=1, source_target_pairs={{0,1},{1,0},{2,3},{3,2},{4,5},{5,4},{6,7},{7,6},{8,9},{9,8},{10,11... | collective-permute-start | bytes 393224 | tf_op jit(solution)/shard_map/ppermute | solution.py:322

commit v5 on v4

--- a/solution.py
+++ b/solution.py
@@ -287,10 +287,10 @@
     panels = near + [twin, next_x, mirror_x, *across]
 
     place = jnp.stack([core, zl, zh, y]).astype(jnp.int32)
-    left1, right1 = after((left1, right1), panels)
-    sides = [left1, swap(left1, "c", 1), right1, swap(right1, "c", 1)]
     parts = project(place, [own, own_other], panels, True)
     came_own = exchange_all(parts)
+    left1, right1 = after((left1, right1), parts)
+    sides = [left1, swap(left1, "c", 1), right1, swap(right1, "c", 1)]
     parts = project(place, after(sides, parts), panels, True)
     came_sides = exchange_all(parts)
 

time: 198 us -> 200 us (1.010)
  local copies, waits for them, and re-layouts: 6.03 us -> 10.1 us
    ppermute x1, waiting for transfers between devices: 14.2 us -> 19.5 us  [per_device(): left2 = lax.ppermute(left1, line, [(1, 0), (2, 1), (5, 4), (6, 5)])]
    all_to_all x2, waiting for transfers between devices: 7.13 us -> 2.34 us  [exchange_all(): return lax.all_to_all(parts, 'y', split_axis=0, concat_axis=0, tiled=True)]
    ppermute x1, waiting for transfers between devices: 7.52 us -> 3.71 us  [per_device(): left1 = lax.ppermute(own_sent, line, [(i, (i - 1) % 8) for i in range(8)])]
    ppermute x1, starting transfers between devices: 3.38 us -> 6.87 us  [per_device(): lax.ppermute(jnp.where(zl == 3, sums[:128], sums[128:]), line, [(i, (i +...]
    unnamed x50, local copies, waits for them, and re-layouts: 5 us -> 7.49 us
    ppermute x9, waiting for transfers between devices: 1 us -> 3.29 us  [to(): return lax.ppermute(piece, ('zl', 'c'), pairs)]
  transfers between devices with their start and end apart: 34 -> 34, of which waited for: 14 -> 18; matrix products, arithmetic and copies ran while one was open for 4% -> 4% of each run, Pallas kernels for 16% -> 15%
where the time goes in v5:
time: 200 us; the launch traced here: 199 us
  starting transfers between devices  81.5 us (41%)
  waiting for transfers between devices  61.8 us (31%)
  Pallas kernels  38.3 us (19%)
  local copies, waits for them, and re-layouts  10.1 us (5%)
  other arithmetic  6.3 us (3%)
    ppermute x18, starting transfers between devices, swap(): return lax.ppermute(value, axis, [(i, i ^ distance) for i in range(size)])  32.9 us
    ppermute x18, waiting for transfers between devices, swap(): return lax.ppermute(value, axis, [(i, i ^ distance) for i in range(size)])  29.7 us
    ppermute x9, starting transfers between devices, to(): return lax.ppermute(piece, ('zl', 'c'), pairs)  25.7 us
    pallas_call x3, Pallas kernels, project(): pl.pallas_call(functools.partial(project_kernel, pairs, together), grid=(...  25.6 us
    ppermute x1, waiting for transfers between devices, per_device(): left2 = lax.ppermute(left1, line, [(1, 0), (2, 1), (5, 4), (6, 5)])  19.5 us
    pallas_call x2, Pallas kernels, scan(): pl.pallas_call(functools.partial(scan_kernel, late), out_shape=[jax.Shape...  10.4 us
    all_to_all x2, starting transfers between devices, exchange_all(): return lax.all_to_all(parts, 'y', split_axis=0, concat_axis=0, tiled=True)  8.47 us
    unnamed x50, local copies, waits for them, and re-layouts  7.49 us
  transfers between devices with their start and end apart: 34, of which 18 were waited for; matrix products, arithmetic and copies ran while one was open for 4% of the time, Pallas kernels for 15%

profile of v5, /device:TPU:1, one launch (start us, length us, event | category | flops | bytes accessed | tf_op | source)
XLA Modules:
  0.0 199.0 jit_solution(11885627486518523825)
XLA Ops:
  0.7 0.7 xor_multiply_fusion
  1.6 0.8 copy.18
  2.4 1.2 fusion.1.refs_2_.refs_4_
  3.6 0.7 shard_map.149
  4.3 2.2 %collective-permute-start = (bf16[64,2048]{1,0:T(8,128)(2,1)S(1)}, bf16[64,2048]{1,0:T(8,128)(2,1)S(1)}, u32[]{:S(2)}, u32[]{:S(2)}) collective-permute-start(bf16[64,2048]{1,0:T(8,128)(2,1)S(1)} %get-tuple-element.43), channel_id=1, source_target_pairs={{0,64},{64,0},{128,192},{192,128},{1,65},{65,1},{129,193},{193,129... | collective-permute-start | bytes 786440 | tf_op jit(solution)/shard_map/ppermute | solution.py:249
  6.5 1.2 collective-permute-start.4
  7.8 1.8 collective-permute-start.5
  9.6 6.9 %collective-permute-start.7 = (bf16[256,1408]{1,0:T(8,128)(2,1)S(1)}, bf16[256,1408]{1,0:T(8,128)(2,1)}, u32[]{:S(2)}, u32[]{:S(2)}) collective-permute-start(bf16[256,1408]{1,0:T(8,128)(2,1)S(1)} %fusion.1.refs_2_.refs_4_), channel_id=1, source_target_pairs={{0,8},{8,0},{1,9},{9,1},{2,10},{10,2},{3,11},{11,3},{4,12},{12,4},... | collective-permute-start | bytes 2162696 | tf_op jit(solution)/shard_map/ppermute | solution.py:249
  16.5 2.6 %collective-permute-start.1 = (bf16[64,2048]{1,0:T(8,128)(2,1)S(1)}, bf16[64,2048]{1,0:T(8,128)(2,1)S(1)}, u32[]{:S(2)}, u32[]{:S(2)}) collective-permute-start(bf16[64,2048]{1,0:T(8,128)(2,1)S(1)} %get-tuple-element.44), channel_id=1, source_target_pairs={{0,128},{64,192},{128,0},{192,64},{1,129},{65,193},{129,1},{193,65... | collective-permute-start | bytes 786440 | tf_op jit(solution)/shard_map/ppermute | solution.py:249
  19.1 0.7 constant_dynamic-update-slice_fusion.3
  19.8 0.7 constant_dynamic-update-slice_fusion.2
  20.6 3.5 %collective-permute-done.1 = bf16[64,2048]{1,0:T(8,128)(2,1)S(1)} collective-permute-done((bf16[64,2048]{1,0:T(8,128)(2,1)S(1)}, bf16[64,2048]{1,0:T(8,128)(2,1)S(1)}, u32[]{:S(2)}, u32[]{:S(2)}) %collective-permute-start.1) | collective-permute-done | bytes 262176 | tf_op jit(solution)/shard_map/ppermute | solution.py:249
  24.1 0.9 collective-permute-start.6
  25.0 0.7 constant_dynamic-update-slice_fusion.1
  25.7 6.2 %collective-permute-done.2 = bf16[64,2048]{1,0:T(8,128)(2,1)S(1)} collective-permute-done((bf16[64,2048]{1,0:T(8,128)(2,1)S(1)}, bf16[64,2048]{1,0:T(8,128)(2,1)S(1)}, u32[]{:S(2)}, u32[]{:S(2)}) %collective-permute-start.2) | collective-permute-done | bytes 262176 | tf_op jit(solution)/shard_map/ppermute | solution.py:249
  31.9 0.7 constant_dynamic-update-slice_fusion.refs_0_
  32.7 2.2 %collective-permute-done.7.given = bf16[256,1408]{1,0:T(8,128)(2,1)} collective-permute-done((bf16[256,1408]{1,0:T(8,128)(2,1)S(1)}, bf16[256,1408]{1,0:T(8,128)(2,1)}, u32[]{:S(2)}, u32[]{:S(2)}) %collective-permute-start.7) | collective-permute-done | bytes 720928 | tf_op jit(solution)/shard_map/ppermute | solution.py:249
  34.9 5.6 %collective-permute-done.6.refs_5_.refs_7_ = bf16[256,1408]{1,0:T(8,128)(2,1)S(1)} collective-permute-done((bf16[256,1408]{1,0:T(8,128)(2,1)S(1)}, bf16[256,1408]{1,0:T(8,128)(2,1)S(1)}, u32[]{:S(2)}, u32[]{:S(2)}) %collective-permute-start.6) | collective-permute-done | bytes 720928 | tf_op jit(solution)/shard_map/ppermute | solution.py:249
  40.5 0.9 copy-done.8
  41.7 1.2 collective-permute-start.9
  42.9 7.3 %collective-permute-start.3 = (bf16[256,2048]{1,0:T(8,128)(2,1)}, bf16[256,2048]{1,0:T(8,128)(2,1)}, u32[]{:S(2)}, u32[]{:S(2)}) collective-permute-start(bf16[256,2048]{1,0:T(8,128)(2,1)} %constant_dynamic-update-slice_fusion.refs_0_), channel_id=1, source_target_pairs={{0,1},{1,0},{2,3},{3,2},{4,5},{5,4},{6,7},{7,6},{8,9},{9,8},{10,11... | collective-permute-start | bytes 3145736 | tf_op jit(solution)/shard_map/ppermute | solution.py:249
  50.1 4.5 %collective-permute-start.12 = (bf16[256,2048]{1,0:T(8,128)(2,1)}, bf16[256,2048]{1,0:T(8,128)(2,1)}, u32[]{:S(2)}, u32[]{:S(2)}) collective-permute-start(bf16[256,2048]{1,0:T(8,128)(2,1)} %constant_dynamic-update-slice_fusion.refs_0_), channel_id=1, source_target_pairs={{0,14},{2,0},{4,2},{6,4},{8,6},{10,8},{12,10},{14,12},{1,15},{3,1}... | collective-permute-start | bytes 3145736 | tf_op jit(solution)/shard_map/ppermute | solution.py:284
  54.7 0.8 slice.16
  55.5 2.1 %collective-permute-start.10 = (bf16[256,768]{1,0:T(8,128)(2,1)}, bf16[256,768]{1,0:T(8,128)(2,1)S(1)}, u32[]{:S(2)}, u32[]{:S(2)}) collective-permute-start(bf16[256,768]{1,0:T(8,128)(2,1)} %slice.16), channel_id=1, source_target_pairs={{0,48},{16,32},{32,16},{48,0},{1,49},{17,33},{33,17},{49,1},{2,50}... | collective-permute-start | bytes 1179656 | tf_op jit(solution)/shard_map/ppermute | solution.py:249
  57.6 0.8 slice.17
  59.0 5.9 %collective-permute-done.11.refs_10_.refs_12_ = bf16[256,640]{1,0:T(8,128)(2,1)} collective-permute-done((bf16[256,640]{1,0:T(8,128)(2,1)}, bf16[256,640]{1,0:T(8,128)(2,1)}, u32[]{:S(2)}, u32[]{:S(2)}) %collective-permute-start.11) | collective-permute-done | bytes 327712 | tf_op jit(solution)/shard_map/ppermute | solution.py:249
  64.9 1.1 collective-permute-done.10.refs_9_.refs_11_
  66.1 0.7 copy-done.10
  66.8 7.1 %shard_map.151 = bf16[4,128,1408]{2,1,0:T(8,128)(2,1)} custom-call(s32[4]{0:T(128)} %pad_add_fusion.1.place, bf16[256,2048]{1,0:T(8,128)(2,1)} %constant_dynamic-update-slice_fusion.refs_0_, bf16[256,2048]{1,0:T(8,128)(2,1)} %collective-permute-done.3.refs_1_, bf16[256,1408]{1,0:T(8,128)(2,1)} %copy-done.3, bf16[256,1408]{1,0:T(8,128)(2,1)} %copy-done.6, ...), custom_call_target="tpu_custom_call" | custom-call | flops 1048576 | bytes 65536 | tf_op jit(solution)/shard_map/pallas_call | solution.py:217
  73.9 3.7 %collective-permute-done.12.refs_0_ = bf16[256,2048]{1,0:T(8,128)(2,1)} collective-permute-done((bf16[256,2048]{1,0:T(8,128)(2,1)}, bf16[256,2048]{1,0:T(8,128)(2,1)}, u32[]{:S(2)}, u32[]{:S(2)}) %collective-permute-start.12) | collective-permute-done | bytes 1048608 | tf_op jit(solution)/shard_map/ppermute | solution.py:284
  77.6 3.1 %collective-permute-done.13.refs_2_ = bf16[256,2048]{1,0:T(8,128)(2,1)} collective-permute-done((bf16[256,2048]{1,0:T(8,128)(2,1)}, bf16[256,2048]{1,0:T(8,128)(2,1)}, u32[]{:S(2)}, u32[]{:S(2)}) %collective-permute-start.13) | collective-permute-done | bytes 1048608 | tf_op jit(solution)/shard_map/ppermute | solution.py:283
  80.7 1.1 collective-permute-start.14
  81.8 3.9 %all-to-all-start = ((bf16[4,128,1408]{2,1,0:T(8,128)(2,1)}), bf16[4,128,1408]{2,1,0:T(8,128)(2,1)S(1)}, u32[]{:S(2)}, u32[]{:S(2)}) async-start(bf16[4,128,1408]{2,1,0:T(8,128)(2,1)} %shard_map.151), calls=%async_computation | async-start | bytes 2883584 | tf_op jit(solution)/shard_map/all_to_all | solution.py:257
  85.8 0.9 copy-done.12
  86.7 1.0 copy-done.13
  87.6 11.3 %shard_map.152 = bf16[4,256,1408]{2,1,0:T(8,128)(2,1)} custom-call(s32[4]{0:T(128)} %pad_add_fusion.1.place, bf16[256,2048]{1,0:T(8,128)(2,1)} %collective-permute-done.12.refs_0_, bf16[256,2048]{1,0:T(8,128)(2,1)} %copy-done.12, bf16[256,2048]{1,0:T(8,128)(2,1)} %collective-permute-done.13.refs_2_, bf16[256,2048]{1,0:T(8,128)(2,1)} %copy-done.13, ...), custom_call_target="tpu_custom_call" | custom-call | flops 1048576 | bytes 65536 | tf_op jit(solution)/shard_map/pallas_call | solution.py:217
  98.9 1.3 collective-permute-start.16
  100.2 1.7 collective-permute-start.17
  101.9 2.3 %all-to-all-done.refs_1_ = bf16[4,128,1408]{2,1,0:T(8,128)(2,1)S(1)} async-done(((bf16[4,128,1408]{2,1,0:T(8,128)(2,1)}), bf16[4,128,1408]{2,1,0:T(8,128)(2,1)S(1)}, u32[]{:S(2)}, u32[]{:S(2)}) %all-to-all-start) | async-done | bytes 1441824 | tf_op jit(solution)/shard_map/all_to_all | solution.py:257
  104.3 4.6 %all-to-all-start.1 = ((bf16[4,256,1408]{2,1,0:T(8,128)(2,1)}), bf16[4,256,1408]{2,1,0:T(8,128)(2,1)}, u32[]{:S(2)}, u32[]{:S(2)}) async-start(bf16[4,256,1408]{2,1,0:T(8,128)(2,1)} %shard_map.152), calls=%async_computation.1 | async-start | bytes 5767168 | tf_op jit(solution)/shard_map/all_to_all | solution.py:257
  108.9 19.5 %collective-permute-done.16 = bf16[256,2048]{1,0:T(8,128)(2,1)S(1)} collective-permute-done((bf16[256,2048]{1,0:T(8,128)(2,1)}, bf16[256,2048]{1,0:T(8,128)(2,1)S(1)}, u32[]{:S(2)}, u32[]{:S(2)}) %collective-permute-start.16) | collective-permute-done | bytes 1048608 | tf_op jit(solution)/shard_map/ppermute | solution.py:299
  128.5 1.2 collective-permute-start.18
  129.7 2.3 %collective-permute-done.18.refs_1_ = bf16[256,2048]{1,0:T(8,128)(2,1)S(1)} collective-permute-done((bf16[256,2048]{1,0:T(8,128)(2,1)S(1)}, bf16[256,2048]{1,0:T(8,128)(2,1)S(1)}, u32[]{:S(2)}, u32[]{:S(2)}) %collective-permute-start.18) | collective-permute-done | bytes 1048608 | tf_op jit(solution)/shard_map/ppermute | solution.py:249
  132.0 1.0 copy-done.11
  132.9 7.3 %shard_map.153 = (f32[128,1408]{1,0:T(8,128)}, bf16[128,1408]{1,0:T(8,128)(2,1)}, bf16[128,1408]{1,0:T(8,128)(2,1)}, bf16[128,1408]{1,0:T(8,128)(2,1)}) custom-call(s32[4]{0:T(128)} %pad_add_fusion.1.place, bf16[256,2048]{1,0:T(8,128)(2,1)} %copy-done.9, bf16[256,2048]{1,0:T(8,128)(2,1)} %copy-done.11, bf16[256,1408]{1,0:T(8,128)(2,1)} %copy-done.3, ...), custom_call_target="tpu_custom_call" | custom-call | flops 1048576 | bytes 65536 | tf_op jit(solution)/shard_map/pallas_call | solution.py:217
  140.2 1.5 collective-permute-start.19
  141.7 2.4 %collective-permute-start.20 = (bf16[128,1408]{1,0:T(8,128)(2,1)}, bf16[128,1408]{1,0:T(8,128)(2,1)}, u32[]{:S(2)}, u32[]{:S(2)}) collective-permute-start(bf16[128,1408]{1,0:T(8,128)(2,1)} %get-tuple-element.60), channel_id=1, source_target_pairs={{0,128},{64,192},{128,0},{192,64},{1,129},{65,193},{129,1},{193,65... | collective-permute-start | bytes 1081352 | tf_op jit(solution)/shard_map/ppermute | solution.py:249
  144.3 2.6 %reduce_sum.12.refs_0_ = bf16[256,1408]{1,0:T(8,128)(2,1)S(1)} reduce(bf16[4,256,1408]{2,1,0:T(8,128)(2,1)} %all-to-all-done.1, bf16[]{:T(256)} %constant.61.clone.1), dimensions={0}, to_apply=%region_0.1 | reduce | flops 1081344 | bytes 3604482 | tf_op jit(solution)/shard_map/reduce_sum | solution.py:261
  146.9 0.8 slice_select_fusion
  147.7 6.9 %collective-permute-start.22 = (bf16[128,1408]{1,0:T(8,128)(2,1)}, bf16[128,1408]{1,0:T(8,128)(2,1)}, u32[]{:S(2)}, u32[]{:S(2)}) collective-permute-start(bf16[128,1408]{1,0:T(8,128)(2,1)} %slice_select_fusion), channel_id=1, source_target_pairs={{0,8},{6,14},{8,0},{14,6},{1,9},{7,15},{9,1},{15,7},{16,24},{22,30... | collective-permute-start | bytes 1081352 | tf_op jit(solution)/shard_map/ppermute | solution.py:313
  154.8 4.8 %shard_map.154 = (bf16[64,1024]{1,0:T(8,128)(2,1)S(1)}, bf16[64,1024]{1,0:T(8,128)(2,1)S(1)}, bf16[64,1024]{1,0:T(8,128)(2,1)S(1)}, bf16[64,1024]{1,0:T(8,128)(2,1)S(1)}, f32[4,16,64,128]{3,2,1,0:T(8,128)}) custom-call(s32[4]{0:T(128)S(1)} %copy-done.2, bf16[256,1408]{1,0:T(8,128)(2,1)S(1)} %reduce_sum.12.refs_0_, ...), custom_call_target="tpu_custom_call" | custom-call | flops 1048576 | bytes 65536 | tf_op jit(solution)/shard_map/pallas_call | solution.py:120
  159.7 0.7 collective-permute-done.20.refs_3_
  160.4 2.0 %collective-permute-done.21.refs_4_ = bf16[128,1408]{1,0:T(8,128)(2,1)} collective-permute-done((bf16[128,1408]{1,0:T(8,128)(2,1)}, bf16[128,1408]{1,0:T(8,128)(2,1)}, u32[]{:S(2)}, u32[]{:S(2)}) %collective-permute-start.21) | collective-permute-done | bytes 360480 | tf_op jit(solution)/shard_map/ppermute | solution.py:249
  162.6 5.6 %shard_map.155 = (bf16[64,1024]{1,0:T(8,128)(2,1)S(1)}, bf16[64,1024]{1,0:T(8,128)(2,1)S(1)}, bf16[64,1024]{1,0:T(8,128)(2,1)S(1)}, bf16[64,1024]{1,0:T(8,128)(2...) custom-call(s32[4]{0:T(128)S(1)} %copy-done.2, ...), custom_call_target="tpu_custom_call", output_to_operand_aliasing={{6}: (11, {})} | custom-call | flops 1048576 | bytes 65536 | tf_op jit(solution)/shard_map/pallas_call | solution.py:120
  168.2 6.6 %collective-permute-start.25 = (bf16[64,1024]{1,0:T(8,128)(2,1)S(1)}, bf16[64,1024]{1,0:T(8,128)(2,1)S(1)}, u32[]{:S(2)}, u32[]{:S(2)}) collective-permute-start(bf16[64,1024]{1,0:T(8,128)(2,1)S(1)} %get-tuple-element.71), channel_id=1, source_target_pairs={{0,4},{1,5},{2,6},{3,7},{4,0},{5,1},{6,2},{7,3},{8,12},{9,13},{10,... | collective-permute-start | bytes 393224 | tf_op jit(solution)/shard_map/ppermute | solution.py:322
  174.8 1.3 collective-permute-start.23
  176.1 1.3 collective-permute-start.24
  178.0 5.5 %collective-permute-start.30 = (bf16[64,1024]{1,0:T(8,128)(2,1)S(1)}, bf16[64,1024]{1,0:T(8,128)(2,1)S(1)}, u32[]{:S(2)}, u32[]{:S(2)}) collective-permute-start(bf16[64,1024]{1,0:T(8,128)(2,1)S(1)} %get-tuple-element.77), channel_id=1, source_target_pairs={{0,6},{1,7},{2,0},{3,1},{4,2},{5,3},{6,4},{7,5},{8,14},{9,15},{10,... | collective-permute-start | bytes 393224 | tf_op jit(solution)/shard_map/ppermute | solution.py:322
  183.5 7.8 %collective-permute-start.31 = (bf16[64,1024]{1,0:T(8,128)(2,1)S(1)}, bf16[64,1024]{1,0:T(8,128)(2,1)S(1)}, u32[]{:S(2)}, u32[]{:S(2)}) collective-permute-start(bf16[64,1024]{1,0:T(8,128)(2,1)S(1)} %get-tuple-element.78), channel_id=1, source_target_pairs={{0,7},{1,6},{2,1},{3,0},{4,3},{5,2},{6,5},{7,4},{8,15},{9,14},{10,... | collective-permute-start | bytes 393224 | tf_op jit(solution)/shard_map/ppermute | solution.py:322
  191.2 1.3 collective-permute-start.26
  192.6 1.3 collective-permute-start.27
  194.1 1.7 collective-permute-done.31.refs_9_
  196.0 1.4 collective-permute-done.27.refs_3_
  197.4 1.6 shard_map.156
  (81 shorter events, 3.0 us)
Async XLA Ops:
  0.6 3.0 %copy-start = (bf16[64,8192]{1,0:T(8,128)(2,1)S(1)}, bf16[64,8192]{1,0:T(8,128)(2,1)}, u32[]{:S(2)}) copy-start(bf16[64,8192]{1,0:T(8,128)(2,1)} %tokens) | copy-start | bytes 3145732
  3.6 29.0 %copy-start.3 = (bf16[256,1408]{1,0:T(8,128)(2,1)}, bf16[256,1408]{1,0:T(8,128)(2,1)S(1)}, u32[]{:S(2)}) copy-start(bf16[256,1408]{1,0:T(8,128)(2,1)S(1)} %fusion.1.refs_2_.refs_4_) | copy-start | bytes 2162692
  4.3 15.5 %collective-permute-start = (bf16[64,2048]{1,0:T(8,128)(2,1)S(1)}, bf16[64,2048]{1,0:T(8,128)(2,1)S(1)}, u32[]{:S(2)}, u32[]{:S(2)}) collective-permute-start(bf16[64,2048]{1,0:T(8,128)(2,1)S(1)} %get-tuple-element.43), channel_id=1, source_target_pairs={{0,64},{64,0},{128,192},{192,128},{1,65},{65,1},{129,193},{193,129... | collective-permute-start | bytes 786440 | tf_op jit(solution)/shard_map/ppermute | solution.py:249
  6.5 28.3 %collective-permute-start.4 = (bf16[256,1408]{1,0:T(8,128)(2,1)S(1)}, bf16[256,1408]{1,0:T(8,128)(2,1)S(1)}, u32[]{:S(2)}, u32[]{:S(2)}) collective-permute-start(bf16[256,1408]{1,0:T(8,128)(2,1)S(1)} %fusion.1.refs_2_.refs_4_), channel_id=1, source_target_pairs={{0,16},{16,0},{32,48},{48,32},{1,17},{17,1},{33,49},{49,33},{2,18}... | collective-permute-start | bytes 2162696 | tf_op jit(solution)/shard_map/ppermute | solution.py:249
  7.8 27.1 %collective-permute-start.5 = (bf16[256,1408]{1,0:T(8,128)(2,1)S(1)}, bf16[256,1408]{1,0:T(8,128)(2,1)S(1)}, u32[]{:S(2)}, u32[]{:S(2)}) collective-permute-start(bf16[256,1408]{1,0:T(8,128)(2,1)S(1)} %fusion.1.refs_2_.refs_4_), channel_id=1, source_target_pairs={{0,48},{16,32},{32,16},{48,0},{1,49},{17,33},{33,17},{49,1},{2,50}... | collective-permute-start | bytes 2162696 | tf_op jit(solution)/shard_map/ppermute | solution.py:249
  9.6 25.3 %collective-permute-start.7 = (bf16[256,1408]{1,0:T(8,128)(2,1)S(1)}, bf16[256,1408]{1,0:T(8,128)(2,1)}, u32[]{:S(2)}, u32[]{:S(2)}) collective-permute-start(bf16[256,1408]{1,0:T(8,128)(2,1)S(1)} %fusion.1.refs_2_.refs_4_), channel_id=1, source_target_pairs={{0,8},{8,0},{1,9},{9,1},{2,10},{10,2},{3,11},{11,3},{4,12},{12,4},... | collective-permute-start | bytes 2162696 | tf_op jit(solution)/shard_map/ppermute | solution.py:249
  16.5 7.6 %collective-permute-start.1 = (bf16[64,2048]{1,0:T(8,128)(2,1)S(1)}, bf16[64,2048]{1,0:T(8,128)(2,1)S(1)}, u32[]{:S(2)}, u32[]{:S(2)}) collective-permute-start(bf16[64,2048]{1,0:T(8,128)(2,1)S(1)} %get-tuple-element.44), channel_id=1, source_target_pairs={{0,128},{64,192},{128,0},{192,64},{1,129},{65,193},{129,1},{193,65... | collective-permute-start | bytes 786440 | tf_op jit(solution)/shard_map/ppermute | solution.py:249
  19.8 12.1 %collective-permute-start.2 = (bf16[64,2048]{1,0:T(8,128)(2,1)S(1)}, bf16[64,2048]{1,0:T(8,128)(2,1)S(1)}, u32[]{:S(2)}, u32[]{:S(2)}) collective-permute-start(bf16[64,2048]{1,0:T(8,128)(2,1)S(1)} %get-tuple-element.45), channel_id=1, source_target_pairs={{0,192},{64,128},{128,64},{192,0},{1,193},{65,129},{129,65},{193,1... | collective-permute-start | bytes 786440 | tf_op jit(solution)/shard_map/ppermute | solution.py:249
  24.1 16.4 %collective-permute-start.6 = (bf16[256,1408]{1,0:T(8,128)(2,1)S(1)}, bf16[256,1408]{1,0:T(8,128)(2,1)S(1)}, u32[]{:S(2)}, u32[]{:S(2)}) collective-permute-start(bf16[256,1408]{1,0:T(8,128)(2,1)S(1)} %fusion.1.refs_2_.refs_4_), channel_id=1, source_target_pairs={{0,32},{16,48},{32,0},{48,16},{1,33},{17,49},{33,1},{49,17},{2,34}... | collective-permute-start | bytes 2162696 | tf_op jit(solution)/shard_map/ppermute | solution.py:249
  34.8 31.2 %copy-start.6 = (bf16[256,1408]{1,0:T(8,128)(2,1)}, bf16[256,1408]{1,0:T(8,128)(2,1)S(1)}, u32[]{:S(2)}) copy-start(bf16[256,1408]{1,0:T(8,128)(2,1)S(1)} %collective-permute-done.4.refs_3_.refs_5_) | copy-start | bytes 2162692
  34.9 31.2 %copy-start.7 = (bf16[256,1408]{1,0:T(8,128)(2,1)}, bf16[256,1408]{1,0:T(8,128)(2,1)S(1)}, u32[]{:S(2)}) copy-start(bf16[256,1408]{1,0:T(8,128)(2,1)S(1)} %collective-permute-done.5.refs_4_.refs_6_) | copy-start | bytes 2162692
  40.5 0.9 copy-start.8
  41.4 13.3 %collective-permute-start.8 = (bf16[256,1408]{1,0:T(8,128)(2,1)}, bf16[256,1408]{1,0:T(8,128)(2,1)S(1)}, u32[]{:S(2)}, u32[]{:S(2)}) collective-permute-start(bf16[256,1408]{1,0:T(8,128)(2,1)} %shard_map.150.refs_6_.refs_8_), channel_id=1, source_target_pairs={{0,16},{16,0},{32,48},{48,32},{1,17},{17,1},{33,49},{49,33},{2,18}... | collective-permute-start | bytes 2162696 | tf_op jit(solution)/shard_map/ppermute | solution.py:249
  41.7 15.9 %collective-permute-start.9 = (bf16[256,1408]{1,0:T(8,128)(2,1)}, bf16[256,1408]{1,0:T(8,128)(2,1)S(1)}, u32[]{:S(2)}, u32[]{:S(2)}) collective-permute-start(bf16[256,1408]{1,0:T(8,128)(2,1)} %shard_map.150.refs_6_.refs_8_), channel_id=1, source_target_pairs={{0,48},{16,32},{32,16},{48,0},{1,49},{17,33},{33,17},{49,1},{2,50}... | collective-permute-start | bytes 2162696 | tf_op jit(solution)/shard_map/ppermute | solution.py:249
  42.9 16.2 %collective-permute-start.3 = (bf16[256,2048]{1,0:T(8,128)(2,1)}, bf16[256,2048]{1,0:T(8,128)(2,1)}, u32[]{:S(2)}, u32[]{:S(2)}) collective-permute-start(bf16[256,2048]{1,0:T(8,128)(2,1)} %constant_dynamic-update-slice_fusion.refs_0_), channel_id=1, source_target_pairs={{0,1},{1,0},{2,3},{3,2},{4,5},{5,4},{6,7},{7,6},{8,9},{9,8},{10,11... | collective-permute-start | bytes 3145736 | tf_op jit(solution)/shard_map/ppermute | solution.py:249
  50.1 27.4 %collective-permute-start.12 = (bf16[256,2048]{1,0:T(8,128)(2,1)}, bf16[256,2048]{1,0:T(8,128)(2,1)}, u32[]{:S(2)}, u32[]{:S(2)}) collective-permute-start(bf16[256,2048]{1,0:T(8,128)(2,1)} %constant_dynamic-update-slice_fusion.refs_0_), channel_id=1, source_target_pairs={{0,14},{2,0},{4,2},{6,4},{8,6},{10,8},{12,10},{14,12},{1,15},{3,1}... | collective-permute-start | bytes 3145736 | tf_op jit(solution)/shard_map/ppermute | solution.py:284
  54.7 26.0 %collective-permute-start.13 = (bf16[256,2048]{1,0:T(8,128)(2,1)}, bf16[256,2048]{1,0:T(8,128)(2,1)}, u32[]{:S(2)}, u32[]{:S(2)}) collective-permute-start(bf16[256,2048]{1,0:T(8,128)(2,1)} %constant_dynamic-update-slice_fusion.refs_0_), channel_id=1, source_target_pairs={{0,2},{2,4},{4,6},{6,8},{8,10},{10,12},{12,14},{14,0},{1,3},{3,5},... | collective-permute-start | bytes 3145736 | tf_op jit(solution)/shard_map/ppermute | solution.py:283
  54.7 11.4 %copy-start.4 = (bf16[256,1408]{1,0:T(8,128)(2,1)}, bf16[256,1408]{1,0:T(8,128)(2,1)S(1)}, u32[]{:S(2)}) copy-start(bf16[256,1408]{1,0:T(8,128)(2,1)S(1)} %collective-permute-done.8.refs_7_.refs_9_) | copy-start | bytes 2162692
  55.5 10.5 %collective-permute-start.10 = (bf16[256,768]{1,0:T(8,128)(2,1)}, bf16[256,768]{1,0:T(8,128)(2,1)S(1)}, u32[]{:S(2)}, u32[]{:S(2)}) collective-permute-start(bf16[256,768]{1,0:T(8,128)(2,1)} %slice.16), channel_id=1, source_target_pairs={{0,48},{16,32},{32,16},{48,0},{1,49},{17,33},{33,17},{49,1},{2,50}... | collective-permute-start | bytes 1179656 | tf_op jit(solution)/shard_map/ppermute | solution.py:249
  57.6 8.5 %copy-start.5 = (bf16[256,1408]{1,0:T(8,128)(2,1)}, bf16[256,1408]{1,0:T(8,128)(2,1)S(1)}, u32[]{:S(2)}) copy-start(bf16[256,1408]{1,0:T(8,128)(2,1)S(1)} %collective-permute-done.9.refs_8_.refs_10_) | copy-start | bytes 2162692
  58.4 6.5 %collective-permute-start.11 = (bf16[256,640]{1,0:T(8,128)(2,1)}, bf16[256,640]{1,0:T(8,128)(2,1)}, u32[]{:S(2)}, u32[]{:S(2)}) collective-permute-start(bf16[256,640]{1,0:T(8,128)(2,1)} %slice.17), channel_id=1, source_target_pairs={{0,16},{16,0},{32,48},{48,32},{1,17},{17,1},{33,49},{49,33},{2,18}... | collective-permute-start | bytes 983048 | tf_op jit(solution)/shard_map/ppermute | solution.py:249
  66.1 0.7 copy-start.10
  80.7 5.0 %collective-permute-start.14 = (bf16[256,2048]{1,0:T(8,128)(2,1)}, bf16[256,2048]{1,0:T(8,128)(2,1)S(1)}, u32[]{:S(2)}, u32[]{:S(2)}) collective-permute-start(bf16[256,2048]{1,0:T(8,128)(2,1)} %collective-permute-done.12.refs_0_), channel_id=1, source_target_pairs={{0,1},{1,0},{2,3},{3,2},{4,5},{5,4},{6,7},{7,6},{8,9},{9,8},{10,11... | collective-permute-start | bytes 3145736 | tf_op jit(solution)/shard_map/ppermute | solution.py:249
  81.8 4.0 %collective-permute-start.15 = (bf16[256,2048]{1,0:T(8,128)(2,1)}, bf16[256,2048]{1,0:T(8,128)(2,1)S(1)}, u32[]{:S(2)}, u32[]{:S(2)}) collective-permute-start(bf16[256,2048]{1,0:T(8,128)(2,1)} %collective-permute-done.13.refs_2_), channel_id=1, source_target_pairs={{0,1},{1,0},{2,3},{3,2},{4,5},{5,4},{6,7},{7,6},{8,9},{9,8},{10,11... | collective-permute-start | bytes 3145736 | tf_op jit(solution)/shard_map/ppermute | solution.py:249
  81.8 22.5 %all-to-all-start = ((bf16[4,128,1408]{2,1,0:T(8,128)(2,1)}), bf16[4,128,1408]{2,1,0:T(8,128)(2,1)S(1)}, u32[]{:S(2)}, u32[]{:S(2)}) async-start(bf16[4,128,1408]{2,1,0:T(8,128)(2,1)} %shard_map.151), calls=%async_computation | async-start | bytes 2883584 | tf_op jit(solution)/shard_map/all_to_all | solution.py:257
  85.7 1.0 copy-start.12
  86.7 1.0 copy-start.13
  98.9 29.4 %collective-permute-start.16 = (bf16[256,2048]{1,0:T(8,128)(2,1)}, bf16[256,2048]{1,0:T(8,128)(2,1)S(1)}, u32[]{:S(2)}, u32[]{:S(2)}) collective-permute-start(bf16[256,2048]{1,0:T(8,128)(2,1)} %collective-permute-done.12.refs_0_), channel_id=1, source_target_pairs={{2,0},{4,2},{10,8},{12,10},{3,1},{5,3},{11,9},{13,11},{18,16},{20,... | collective-permute-start | bytes 3145736 | tf_op jit(solution)/shard_map/ppermute | solution.py:299
  100.2 28.1 %collective-permute-start.17 = (bf16[256,2048]{1,0:T(8,128)(2,1)}, bf16[256,2048]{1,0:T(8,128)(2,1)}, u32[]{:S(2)}, u32[]{:S(2)}) collective-permute-start(bf16[256,2048]{1,0:T(8,128)(2,1)} %collective-permute-done.13.refs_2_), channel_id=1, source_target_pairs={{2,4},{4,6},{10,12},{12,14},{3,5},{5,7},{11,13},{13,15},{18,20},{2... | collective-permute-start | bytes 3145736 | tf_op jit(solution)/shard_map/ppermute | solution.py:298
  104.3 40.0 %all-to-all-start.1 = ((bf16[4,256,1408]{2,1,0:T(8,128)(2,1)}), bf16[4,256,1408]{2,1,0:T(8,128)(2,1)}, u32[]{:S(2)}, u32[]{:S(2)}) async-start(bf16[4,256,1408]{2,1,0:T(8,128)(2,1)} %shard_map.152), calls=%async_computation.1 | async-start | bytes 5767168 | tf_op jit(solution)/shard_map/all_to_all | solution.py:257
  128.4 3.5 %copy-start.9 = (bf16[256,2048]{1,0:T(8,128)(2,1)}, bf16[256,2048]{1,0:T(8,128)(2,1)S(1)}, u32[]{:S(2)}) copy-start(bf16[256,2048]{1,0:T(8,128)(2,1)S(1)} %broadcast_select_fusion.refs_0_) | copy-start | bytes 3145732
  128.5 3.5 %collective-permute-start.18 = (bf16[256,2048]{1,0:T(8,128)(2,1)S(1)}, bf16[256,2048]{1,0:T(8,128)(2,1)S(1)}, u32[]{:S(2)}, u32[]{:S(2)}) collective-permute-start(bf16[256,2048]{1,0:T(8,128)(2,1)S(1)} %broadcast_select_fusion.refs_0_), channel_id=1, source_target_pairs={{0,1},{1,0},{2,3},{3,2},{4,5},{5,4},{6,7},{7,6},{8,9},{9,8},{10,11... | collective-permute-start | bytes 3145736 | tf_op jit(solution)/shard_map/ppermute | solution.py:249
  132.0 1.0 copy-start.11
  140.2 19.5 %collective-permute-start.19 = (bf16[128,1408]{1,0:T(8,128)(2,1)}, bf16[128,1408]{1,0:T(8,128)(2,1)S(1)}, u32[]{:S(2)}, u32[]{:S(2)}) collective-permute-start(bf16[128,1408]{1,0:T(8,128)(2,1)} %get-tuple-element.59), channel_id=1, source_target_pairs={{0,64},{64,0},{128,192},{192,128},{1,65},{65,1},{129,193},{193,129... | collective-permute-start | bytes 1081352 | tf_op jit(solution)/shard_map/ppermute | solution.py:249
  141.7 18.6 %collective-permute-start.20 = (bf16[128,1408]{1,0:T(8,128)(2,1)}, bf16[128,1408]{1,0:T(8,128)(2,1)}, u32[]{:S(2)}, u32[]{:S(2)}) collective-permute-start(bf16[128,1408]{1,0:T(8,128)(2,1)} %get-tuple-element.60), channel_id=1, source_target_pairs={{0,128},{64,192},{128,0},{192,64},{1,129},{65,193},{129,1},{193,65... | collective-permute-start | bytes 1081352 | tf_op jit(solution)/shard_map/ppermute | solution.py:249
  144.1 18.2 %collective-permute-start.21 = (bf16[128,1408]{1,0:T(8,128)(2,1)}, bf16[128,1408]{1,0:T(8,128)(2,1)}, u32[]{:S(2)}, u32[]{:S(2)}) collective-permute-start(bf16[128,1408]{1,0:T(8,128)(2,1)} %get-tuple-element.61), channel_id=1, source_target_pairs={{0,192},{64,128},{128,64},{192,0},{1,193},{65,129},{129,65},{193,1... | collective-permute-start | bytes 1081352 | tf_op jit(solution)/shard_map/ppermute | solution.py:249
  144.2 10.4 %copy-start.20 = (f32[16]{0:T(128)S(1)}, f32[16]{0:T(128)}, u32[]{:S(2)}) copy-start(f32[16]{0:T(128)} %param.23) | copy-start | bytes 196
  144.2 10.4 %copy-start.21 = (f32[16]{0:T(128)S(1)}, f32[16]{0:T(128)}, u32[]{:S(2)}) copy-start(f32[16]{0:T(128)} %param.22) | copy-start | bytes 196
  144.2 10.4 %copy-start.17 = (f32[16]{0:T(128)S(1)}, f32[16]{0:T(128)}, u32[]{:S(2)}) copy-start(f32[16]{0:T(128)} %param.24) | copy-start | bytes 196
  144.2 10.5 %copy-start.14 = (f32[4,1024]{1,0:T(4,128)S(1)}, f32[4,1024]{1,0:T(4,128)}, u32[]{:S(2)}) copy-start(f32[4,1024]{1,0:T(4,128)} %param.19) | copy-start | bytes 49156
  144.3 10.5 %copy-start.15 = (f32[4,128]{1,0:T(4,128)S(1)}, f32[4,128]{1,0:T(4,128)}, u32[]{:S(2)}) copy-start(f32[4,128]{1,0:T(4,128)} %param.20) | copy-start | bytes 6148
  144.3 10.5 %copy-start.16 = (f32[4,128]{1,0:T(4,128)S(1)}, f32[4,128]{1,0:T(4,128)}, u32[]{:S(2)}) copy-start(f32[4,128]{1,0:T(4,128)} %param.21) | copy-start | bytes 6148
  144.3 10.5 %copy-start.2 = (s32[4]{0:T(128)S(1)}, s32[4]{0:T(128)}, u32[]{:S(2)}) copy-start(s32[4]{0:T(128)} %pad_add_fusion.1.place) | copy-start | bytes 52
  146.9 15.7 %copy-start.1 = (f32[128,1408]{1,0:T(8,128)S(1)}, f32[128,1408]{1,0:T(8,128)}, u32[]{:S(2)}) copy-start(f32[128,1408]{1,0:T(8,128)} %get-tuple-element.58.refs_1_) | copy-start | bytes 2162692
  147.7 14.9 %collective-permute-start.22 = (bf16[128,1408]{1,0:T(8,128)(2,1)}, bf16[128,1408]{1,0:T(8,128)(2,1)}, u32[]{:S(2)}, u32[]{:S(2)}) collective-permute-start(bf16[128,1408]{1,0:T(8,128)(2,1)} %slice_select_fusion), channel_id=1, source_target_pairs={{0,8},{6,14},{8,0},{14,6},{1,9},{7,15},{9,1},{15,7},{16,24},{22,30... | collective-permute-start | bytes 1081352 | tf_op jit(solution)/shard_map/ppermute | solution.py:313
  162.6 31.4 %copy-start.18 = (s32[8]{0:T(128)S(1)}, s32[8]{0:T(128)}, u32[]{:S(2)}) copy-start(s32[8]{0:T(128)} %constant.64.clone) | copy-start | bytes 100
  162.6 31.4 %copy-start.19 = (s32[8]{0:T(128)S(1)}, s32[8]{0:T(128)}, u32[]{:S(2)}) copy-start(s32[8]{0:T(128)} %constant.65.clone) | copy-start | bytes 100
  168.2 15.3 %collective-permute-start.25 = (bf16[64,1024]{1,0:T(8,128)(2,1)S(1)}, bf16[64,1024]{1,0:T(8,128)(2,1)S(1)}, u32[]{:S(2)}, u32[]{:S(2)}) collective-permute-start(bf16[64,1024]{1,0:T(8,128)(2,1)S(1)} %get-tuple-element.71), channel_id=1, source_target_pairs={{0,4},{1,5},{2,6},{3,7},{4,0},{5,1},{6,2},{7,3},{8,12},{9,13},{10,... | collective-permute-start | bytes 393224 | tf_op jit(solution)/shard_map/ppermute | solution.py:322
  174.8 16.4 %collective-permute-start.23 = (bf16[64,1024]{1,0:T(8,128)(2,1)S(1)}, bf16[64,1024]{1,0:T(8,128)(2,1)S(1)}, u32[]{:S(2)}, u32[]{:S(2)}) collective-permute-start(bf16[64,1024]{1,0:T(8,128)(2,1)S(1)} %get-tuple-element.65), channel_id=1, source_target_pairs={{6,0},{7,1},{14,8},{15,9},{22,16},{23,17},{30,24},{31,25},{38,32},... | collective-permute-start | bytes 393224 | tf_op jit(solution)/shard_map/ppermute | solution.py:322
  176.1 16.4 %collective-permute-start.24 = (bf16[64,1024]{1,0:T(8,128)(2,1)S(1)}, bf16[64,1024]{1,0:T(8,128)(2,1)S(1)}, u32[]{:S(2)}, u32[]{:S(2)}) collective-permute-start(bf16[64,1024]{1,0:T(8,128)(2,1)S(1)} %get-tuple-element.66), channel_id=1, source_target_pairs={{6,1},{7,0},{14,9},{15,8},{22,17},{23,16},{30,25},{31,24},{38,33},... | collective-permute-start | bytes 393224 | tf_op jit(solution)/shard_map/ppermute | solution.py:322
  177.4 16.5 %collective-permute-start.29 = (bf16[64,1024]{1,0:T(8,128)(2,1)S(1)}, bf16[64,1024]{1,0:T(8,128)(2,1)S(1)}, u32[]{:S(2)}, u32[]{:S(2)}) collective-permute-start(bf16[64,1024]{1,0:T(8,128)(2,1)S(1)} %get-tuple-element.76), channel_id=1, source_target_pairs={{0,5},{1,4},{2,7},{3,6},{4,1},{5,0},{6,3},{7,2},{8,13},{9,12},{10,... | collective-permute-start | bytes 393224 | tf_op jit(solution)/shard_map/ppermute | solution.py:322
  178.0 16.1 %collective-permute-start.30 = (bf16[64,1024]{1,0:T(8,128)(2,1)S(1)}, bf16[64,1024]{1,0:T(8,128)(2,1)S(1)}, u32[]{:S(2)}, u32[]{:S(2)}) collective-permute-start(bf16[64,1024]{1,0:T(8,128)(2,1)S(1)} %get-tuple-element.77), channel_id=1, source_target_pairs={{0,6},{1,7},{2,0},{3,1},{4,2},{5,3},{6,4},{7,5},{8,14},{9,15},{10,... | collective-permute-start | bytes 393224 | tf_op jit(solution)/shard_map/ppermute | solution.py:322
  183.5 12.3 %collective-permute-start.31 = (bf16[64,1024]{1,0:T(8,128)(2,1)S(1)}, bf16[64,1024]{1,0:T(8,128)(2,1)S(1)}, u32[]{:S(2)}, u32[]{:S(2)}) collective-permute-start(bf16[64,1024]{1,0:T(8,128)(2,1)S(1)} %get-tuple-element.78), channel_id=1, source_target_pairs={{0,7},{1,6},{2,1},{3,0},{4,3},{5,2},{6,5},{7,4},{8,15},{9,14},{10,... | collective-permute-start | bytes 393224 | tf_op jit(solution)/shard_map/ppermute | solution.py:322
  191.2 4.7 %collective-permute-start.26 = (bf16[64,1024]{1,0:T(8,128)(2,1)S(1)}, bf16[64,1024]{1,0:T(8,128)(2,1)S(1)}, u32[]{:S(2)}, u32[]{:S(2)}) collective-permute-start(bf16[64,1024]{1,0:T(8,128)(2,1)S(1)} %get-tuple-element.72), channel_id=1, source_target_pairs={{0,2},{1,3},{2,4},{3,5},{4,6},{5,7},{8,10},{9,11},{10,12},{11,13},... | collective-permute-start | bytes 393224 | tf_op jit(solution)/shard_map/ppermute | solution.py:322
  192.6 4.8 %collective-permute-start.27 = (bf16[64,1024]{1,0:T(8,128)(2,1)S(1)}, bf16[64,1024]{1,0:T(8,128)(2,1)S(1)}, u32[]{:S(2)}, u32[]{:S(2)}) collective-permute-start(bf16[64,1024]{1,0:T(8,128)(2,1)S(1)} %get-tuple-element.73), channel_id=1, source_target_pairs={{0,3},{1,2},{2,5},{3,4},{4,7},{5,6},{8,11},{9,10},{10,13},{11,12},... | collective-permute-start | bytes 393224 | tf_op jit(solution)/shard_map/ppermute | solution.py:322
  193.9 3.5 %collective-permute-start.28 = (bf16[64,1024]{1,0:T(8,128)(2,1)S(1)}, bf16[64,1024]{1,0:T(8,128)(2,1)S(1)}, u32[]{:S(2)}, u32[]{:S(2)}) collective-permute-start(bf16[64,1024]{1,0:T(8,128)(2,1)S(1)} %get-tuple-element.75), channel_id=1, source_target_pairs={{0,1},{1,0},{2,3},{3,2},{4,5},{5,4},{6,7},{7,6},{8,9},{9,8},{10,11... | collective-permute-start | bytes 393224 | tf_op jit(solution)/shard_map/ppermute | solution.py:322
